TPU v7x, 32 devices: a whole 2x2x4 slice. The times are simulated.
32 devices in a mesh: dp: 8 (over y, x, core), mp: 4 (over z).
Axes of the slice: x: 2, y: 2, z: 4, core: 2. Of those that a mesh axis runs over, the one named last changes fastest.
Arguments:
- hidden_in: bfloat16 [8192, 2048], P('dp'), may hold values from -6 to 6
- cotangent: bfloat16 [8192, 2048], P('dp'), may hold values from -6 to 6
- doc_lengths: int32 [8, 8], replicated, may hold values from 1 to 256, 1024 in all within a row
- w_query: bfloat16 [2048, 2048], P('dp', 'mp'), may hold values from -0.125 to 0.125
- w_key: bfloat16 [2048, 1024], P('dp', 'mp'), may hold values from -0.125 to 0.125
- w_value: bfloat16 [2048, 1024], P('dp', 'mp'), may hold values from -0.125 to 0.125
- w_out: bfloat16 [2048, 2048], P('mp', 'dp'), may hold values from -1 to 1
- w_gate: bfloat16 [2048, 6144], P('dp', 'mp'), may hold values from -0.125 to 0.125
- w_up: bfloat16 [2048, 6144], P('dp', 'mp'), may hold values from -0.125 to 0.125
- w_down: bfloat16 [6144, 2048], P('mp', 'dp'), may hold values from -0.078125 to 0.078125
- norm_attn: bfloat16 [2048], P('dp'), may hold values from 0.099609375 to 1.8984375
- norm_mlp: bfloat16 [2048], P('dp'), may hold values from 0.099609375 to 1.8984375
- norm_query: bfloat16 [128], P('dp'), may hold values from 0.099609375 to 1.8984375
- norm_key: bfloat16 [128], P('dp'), may hold values from 0.099609375 to 1.8984375
Outputs:
- output: bfloat16 [8192, 2048], P('dp')
- grad_input: float32 [8192, 2048], P('dp')
- grad_query_w: float32 [2048, 2048], P('dp', 'mp')
- grad_key_w: float32 [2048, 1024], P('dp', 'mp')
- grad_value_w: float32 [2048, 1024], P('dp', 'mp')
- grad_out_w: float32 [2048, 2048], P('mp', 'dp')
- grad_gate_w: float32 [2048, 6144], P('dp', 'mp')
- grad_up_w: float32 [2048, 6144], P('dp', 'mp')
- grad_down_w: float32 [6144, 2048], P('mp', 'dp')
- grad_norm_attn: float32 [2048], P('dp')
- grad_norm_mlp: float32 [2048], P('dp')
- grad_norm_query: float32 [128], P('dp')
- grad_norm_key: float32 [128], P('dp')
Inputs may be any that keep to these rules, and one draw needn't show every extreme that they name: Each row of doc_lengths sums to 1024 and its largest entry is 256.
All inputs are finite; a program needn't handle non-finite values.
Results may differ from a plain program's by a relative error of at most 0.015.
Values may be sent and summed in bfloat16 or wider, within the bound.
No kernel may reach another device: no remote copies, remote signals or barrier semaphores. Data moves between devices by JAX's collectives and lax.ppermute only.
A program may use at most 256 MiB of HBM per device.

v0:
```python
import jax
import jax.numpy as jnp
from jax import lax
from jax.sharding import PartitionSpec as P

HD = 128
ROW = 1024
TOK_DEV = 1024


EPSILON = 1e-06
ROPE_BASE = 1000000.0


def rms_scale(values, scale_gain):
    return (
        values * lax.rsqrt(jnp.mean(values * values, axis=-1, keepdims=True) + EPSILON) * scale_gain
    )


def rotate(values, position):
    half_dim = values.shape[-1] // 2
    inverse = ROPE_BASE ** (-(2.0 * jnp.arange(half_dim, dtype=jnp.float32)) / values.shape[-1])
    angles = position.astype(jnp.float32)[:, None] * inverse[None, :]
    cosine = jnp.cos(angles)[:, None, :]
    sine_part = jnp.sin(angles)[:, None, :]
    first_half = values[..., :half_dim]
    second_half = values[..., half_dim:]
    return jnp.concatenate(
        [
            first_half * cosine - second_half * sine_part,
            second_half * cosine + first_half * sine_part,
        ],
        axis=-1,
    )


def doc_bounds(doc_lengths):
    starts = jnp.cumsum(doc_lengths, axis=1) - doc_lengths
    row_base = jnp.arange(doc_lengths.shape[0], dtype=jnp.int32)[:, None] * ROW
    doc_begin = (starts + row_base).reshape(-1)
    return (doc_begin, doc_begin + doc_lengths.reshape(-1))


def place_docs(doc_lengths, n_dev, docs_dev):
    row_count = doc_lengths.shape[0]
    per_row = doc_lengths.shape[1]
    row_ids = jnp.arange(row_count, dtype=jnp.int32)
    column = row_ids * per_row // n_dev
    signed = jnp.where((column % 2 == 0)[:, None], -doc_lengths, doc_lengths)
    order_key = signed * per_row + jnp.arange(per_row, dtype=jnp.int32)[None, :]
    ranking = jnp.argsort(jnp.argsort(order_key, axis=1), axis=1)
    linear = (row_ids[:, None] * per_row + ranking).reshape(-1)
    return linear % n_dev * docs_dev + linear // n_dev


def home_plan(doc_begin, doc_finish, doc_place, device, n_dev, docs_dev, slot_rows):
    low_edge = device * TOK_DEV
    high_edge = low_edge + TOK_DEV
    piece_lo = jnp.maximum(doc_begin, low_edge)
    piece_hi = jnp.minimum(doc_finish, high_edge)
    present = piece_lo < piece_hi
    target = doc_place // docs_dev
    chosen = present[None, :] & (target[None, :] == jnp.arange(n_dev, dtype=jnp.int32)[:, None])
    send_lo = jnp.sum(jnp.where(chosen, piece_lo[None, :], 0), axis=1)
    send_len = jnp.sum(jnp.where(chosen, (piece_hi - piece_lo)[None, :], 0), axis=1)
    slot_ramp = jnp.arange(slot_rows, dtype=jnp.int32)
    send_valid = slot_ramp[None, :] < send_len[:, None]
    send_rows = jnp.where(send_valid, send_lo[:, None] - low_edge + slot_ramp[None, :], 0)
    global_pos = low_edge + jnp.arange(TOK_DEV, dtype=jnp.int32)
    member = (global_pos[:, None] >= doc_begin[None, :]) & (
        global_pos[:, None] < doc_finish[None, :]
    )
    token_lo = jnp.sum(jnp.where(member, piece_lo[None, :], 0), axis=1)
    token_dev = jnp.sum(jnp.where(member, target[None, :], 0), axis=1)
    back_rows = token_dev * slot_rows + global_pos - token_lo
    position = global_pos - jnp.sum(jnp.where(member, doc_begin[None, :], 0), axis=1)
    return (send_rows, send_valid, back_rows, position)


def docs_plan(doc_begin, doc_finish, doc_place, device, n_dev, docs_dev, doc_most, slot_rows):
    wanted = device * docs_dev + jnp.arange(docs_dev, dtype=jnp.int32)
    picked = doc_place[None, :] == wanted[:, None]
    doc_start = jnp.sum(jnp.where(picked, doc_begin[None, :], 0), axis=1)
    doc_end = jnp.sum(jnp.where(picked, doc_finish[None, :], 0), axis=1)
    doc_ramp = jnp.arange(doc_most, dtype=jnp.int32)
    doc_token = doc_start[:, None] + doc_ramp[None, :]
    inside = doc_token < doc_end[:, None]
    source = doc_token // TOK_DEV
    offset = doc_token - jnp.maximum(doc_start[:, None], source * TOK_DEV)
    gather_rows = jnp.where(inside, source * slot_rows + offset, 0).reshape(-1)
    home_ids = jnp.arange(n_dev, dtype=jnp.int32)
    part_lo = jnp.maximum(doc_start[None, :], home_ids[:, None] * TOK_DEV)
    part_hi = jnp.minimum(doc_end[None, :], (home_ids[:, None] + 1) * TOK_DEV)
    has_part = part_lo < part_hi
    slot_base = jnp.arange(docs_dev, dtype=jnp.int32)[None, :] * doc_most
    which_lo = jnp.sum(jnp.where(has_part, part_lo - doc_start[None, :] + slot_base, 0), axis=1)
    which_len = jnp.sum(jnp.where(has_part, part_hi - part_lo, 0), axis=1)
    slot_ramp = jnp.arange(slot_rows, dtype=jnp.int32)
    return_valid = slot_ramp[None, :] < which_len[:, None]
    return_rows = jnp.where(return_valid, which_lo[:, None] + slot_ramp[None, :], 0)
    return (gather_rows, inside.reshape(-1), return_rows, return_valid)


def pick_rows(values, row_ids, row_valid):
    picked_rows = jnp.take(values, row_ids.reshape(-1), axis=0)
    masked_rows = jnp.where(
        row_valid.reshape(-1)[:, None], picked_rows, jnp.zeros((), values.dtype)
    )
    return masked_rows.reshape(row_ids.shape + values.shape[1:])


def on_device(
    hidden_in,
    cotangent,
    doc_lengths,
    w_query,
    w_key,
    w_value,
    w_out,
    w_gate,
    w_up,
    w_down,
    norm_attn,
    norm_mlp,
    norm_query,
    norm_key,
):
    n_dev = lax.axis_size("dp")
    device = lax.axis_index("dp")
    docs_row = doc_lengths.shape[1]
    docs_dev = TOK_DEV * docs_row // ROW
    doc_most = 2 * ROW // n_dev
    slot_rows = min(TOK_DEV, doc_most)
    query_cols = w_query.shape[1]
    key_cols = w_key.shape[1]
    query_local = query_cols // HD
    key_local = key_cols // HD
    group_size = query_local // key_local
    score_scale = HD ** (-0.5)
    causal = (
        jnp.arange(doc_most, dtype=jnp.int32)[:, None]
        >= jnp.arange(doc_most, dtype=jnp.int32)[None, :]
    )

    def attn_weights():
        return (
            lax.all_gather(w_query, "dp", axis=0, tiled=True),
            lax.all_gather(w_key, "dp", axis=0, tiled=True),
            lax.all_gather(w_value, "dp", axis=0, tiled=True),
            lax.all_gather(w_out, "dp", axis=1, tiled=True),
            lax.all_gather(norm_attn, "dp", axis=0, tiled=True),
            lax.all_gather(norm_query, "dp", axis=0, tiled=True),
            lax.all_gather(norm_key, "dp", axis=0, tiled=True),
        )

    def mlp_weights():
        return (
            lax.all_gather(w_gate, "dp", axis=0, tiled=True),
            lax.all_gather(w_up, "dp", axis=0, tiled=True),
            lax.all_gather(w_down, "dp", axis=1, tiled=True),
            lax.all_gather(norm_mlp, "dp", axis=0, tiled=True),
        )

    doc_begin, doc_finish = doc_bounds(doc_lengths)
    doc_place = place_docs(doc_lengths, n_dev, docs_dev)
    send_rows, send_valid, back_rows, position = home_plan(
        doc_begin, doc_finish, doc_place, device, n_dev, docs_dev, slot_rows
    )
    gather_rows, inside, return_rows, return_valid = docs_plan(
        doc_begin, doc_finish, doc_place, device, n_dev, docs_dev, doc_most, slot_rows
    )
    full_query, full_key, full_value, full_out, gain_attn, gain_query, gain_key = attn_weights()
    hidden = hidden_in.astype(jnp.float32)
    gain_attn_f = gain_attn.astype(jnp.float32)
    normed = rms_scale(hidden, gain_attn_f).astype(jnp.bfloat16)
    query_lin = jnp.dot(normed, full_query, preferred_element_type=jnp.float32)
    key_lin = jnp.dot(normed, full_key, preferred_element_type=jnp.float32)
    value_home = jnp.dot(normed, full_value, preferred_element_type=jnp.float32).astype(
        jnp.bfloat16
    )

    def heads_prep(query_flat, key_flat, gain_q, gain_k):
        query_heads = rotate(
            rms_scale(query_flat.reshape(TOK_DEV, query_local, HD), gain_q), position
        )
        key_heads = rotate(rms_scale(key_flat.reshape(TOK_DEV, key_local, HD), gain_k), position)
        return (query_heads.reshape(TOK_DEV, query_cols), key_heads.reshape(TOK_DEV, key_cols))

    rotated, prep_back = jax.vjp(
        heads_prep, query_lin, key_lin, gain_query.astype(jnp.float32), gain_key.astype(jnp.float32)
    )
    query_send = pick_rows(rotated[0].astype(jnp.bfloat16), send_rows, send_valid)
    key_send = pick_rows(rotated[1].astype(jnp.bfloat16), send_rows, send_valid)
    value_send = pick_rows(value_home, send_rows, send_valid)
    query_got, key_got, value_got = (
        lax.all_to_all(query_send, "dp", split_axis=0, concat_axis=0, tiled=True),
        lax.all_to_all(key_send, "dp", split_axis=0, concat_axis=0, tiled=True),
        lax.all_to_all(value_send, "dp", split_axis=0, concat_axis=0, tiled=True),
    )
    query_docs = pick_rows(query_got.reshape(-1, query_cols), gather_rows, inside).reshape(
        docs_dev, doc_most, query_local, HD
    )
    key_docs = pick_rows(key_got.reshape(-1, key_cols), gather_rows, inside).reshape(
        docs_dev, doc_most, key_local, HD
    )
    value_docs = pick_rows(value_got.reshape(-1, key_cols), gather_rows, inside).reshape(
        docs_dev, doc_most, key_local, HD
    )

    def doc_scores(query_slot, key_slot):
        grouped = query_slot.reshape(doc_most, key_local, group_size, HD)
        raw_scores = (
            jnp.einsum("qkgd,skd->kgqs", grouped, key_slot, preferred_element_type=jnp.float32)
            * score_scale
        )
        return jnp.where(causal, raw_scores, -1e30)

    def forward_slot(query_slot, key_slot, value_slot):
        scores = doc_scores(query_slot, key_slot)
        row_peak = jnp.max(scores, axis=-1, keepdims=True)
        expsum = jnp.exp(scores - row_peak)
        row_total = jnp.sum(expsum, axis=-1, keepdims=True)
        weights = (expsum / row_total).astype(jnp.bfloat16)
        attended = jnp.einsum(
            "kgqs,skd->qkgd", weights, value_slot, preferred_element_type=jnp.float32
        )
        return (attended.reshape(doc_most, query_cols).astype(jnp.bfloat16), row_peak, row_total)

    attended_docs, peak_docs, total_docs = jax.vmap(forward_slot)(query_docs, key_docs, value_docs)
    attended_send = pick_rows(attended_docs.reshape(-1, query_cols), return_rows, return_valid)
    attended_back = lax.all_to_all(attended_send, "dp", split_axis=0, concat_axis=0, tiled=True)
    attended_home = jnp.take(attended_back.reshape(-1, query_cols), back_rows, axis=0)
    branch = lax.psum(jnp.dot(attended_home, full_out, preferred_element_type=jnp.float32), "mp")
    middle = hidden + branch
    full_gate, full_up, full_down, gain_mlp = mlp_weights()
    gain_mlp_f = gain_mlp.astype(jnp.float32)
    normed_two = rms_scale(middle, gain_mlp_f).astype(jnp.bfloat16)
    gate_lin = jnp.dot(normed_two, full_gate, preferred_element_type=jnp.float32)
    upward = jnp.dot(normed_two, full_up, preferred_element_type=jnp.float32)
    product = (jax.nn.silu(gate_lin) * upward).astype(jnp.bfloat16)
    down_part = jnp.dot(product, full_down, preferred_element_type=jnp.float32)
    output = (middle + lax.psum(down_part.astype(jnp.bfloat16), "mp").astype(jnp.float32)).astype(
        jnp.bfloat16
    )
    full_gate, full_up, full_down, gain_mlp = mlp_weights()
    gain_mlp_f = gain_mlp.astype(jnp.float32)
    grad_down_w = jnp.einsum("tf,td->fd", product, cotangent, preferred_element_type=jnp.float32)
    grad_product = jnp.einsum("td,fd->tf", cotangent, full_down, preferred_element_type=jnp.float32)
    sigmoid_gate = jax.nn.sigmoid(gate_lin)
    grad_gate = (
        grad_product * upward * sigmoid_gate * (1.0 + gate_lin * (1.0 - sigmoid_gate))
    ).astype(jnp.bfloat16)
    grad_upward = (grad_product * gate_lin * sigmoid_gate).astype(jnp.bfloat16)
    grad_gate_w = jnp.einsum("td,tf->df", normed_two, grad_gate, preferred_element_type=jnp.float32)
    grad_up_w = jnp.einsum("td,tf->df", normed_two, grad_upward, preferred_element_type=jnp.float32)
    normed_two_part = jnp.einsum(
        "tf,df->td", grad_gate, full_gate, preferred_element_type=jnp.float32
    )
    normed_two_part = normed_two_part + jnp.einsum(
        "tf,df->td", grad_upward, full_up, preferred_element_type=jnp.float32
    )
    grad_normed_two = lax.psum(normed_two_part, "mp")
    mlp_norm_pair = jax.vjp(rms_scale, middle, gain_mlp_f)
    grad_middle_norm, grad_norm_mlp = mlp_norm_pair[1](grad_normed_two)
    grad_middle = cotangent.astype(jnp.float32) + grad_middle_norm
    mlp_grads = (
        lax.psum_scatter(grad_gate_w, "dp", scatter_dimension=0, tiled=True),
        lax.psum_scatter(grad_up_w, "dp", scatter_dimension=0, tiled=True),
        lax.psum_scatter(grad_down_w, "dp", scatter_dimension=1, tiled=True),
        lax.psum_scatter(grad_norm_mlp, "dp", scatter_dimension=0, tiled=True),
    )
    full_query, full_key, full_value, full_out, gain_attn, gain_query, gain_key = attn_weights()
    gain_attn_f = gain_attn.astype(jnp.float32)
    grad_branch = grad_middle.astype(jnp.bfloat16)
    grad_out_w = jnp.einsum(
        "tc,td->cd", attended_home, grad_branch, preferred_element_type=jnp.float32
    )
    grad_attended = jnp.einsum(
        "td,cd->tc", grad_branch, full_out, preferred_element_type=jnp.float32
    ).astype(jnp.bfloat16)
    grad_send = pick_rows(grad_attended, send_rows, send_valid)
    grad_got = lax.all_to_all(grad_send, "dp", split_axis=0, concat_axis=0, tiled=True)
    grad_docs = pick_rows(grad_got.reshape(-1, query_cols), gather_rows, inside).reshape(
        docs_dev, doc_most, query_local, HD
    )

    def backward_slot(query_slot, key_slot, value_slot, grad_slot, peak_slot, total_slot):
        scores = doc_scores(query_slot, key_slot)
        weights = jnp.exp(scores - peak_slot) / total_slot
        grouped = query_slot.reshape(doc_most, key_local, group_size, HD)
        grad_grouped = grad_slot.reshape(doc_most, key_local, group_size, HD)
        grad_weights = jnp.einsum(
            "qkgd,skd->kgqs", grad_grouped, value_slot, preferred_element_type=jnp.float32
        )
        row_delta = jnp.sum(weights * grad_weights, axis=-1, keepdims=True)
        grad_scores = (weights * (grad_weights - row_delta)).astype(jnp.bfloat16)
        grad_query = (
            jnp.einsum("kgqs,skd->qkgd", grad_scores, key_slot, preferred_element_type=jnp.float32)
            * score_scale
        )
        grad_key = (
            jnp.einsum("kgqs,qkgd->skd", grad_scores, grouped, preferred_element_type=jnp.float32)
            * score_scale
        )
        grad_value = jnp.einsum(
            "kgqs,qkgd->skd",
            weights.astype(jnp.bfloat16),
            grad_grouped,
            preferred_element_type=jnp.float32,
        )
        return (
            grad_query.reshape(doc_most, query_cols).astype(jnp.bfloat16),
            grad_key.reshape(doc_most, key_cols).astype(jnp.bfloat16),
            grad_value.reshape(doc_most, key_cols).astype(jnp.bfloat16),
        )

    grad_query_docs, grad_key_docs, grad_value_docs = jax.vmap(backward_slot)(
        query_docs, key_docs, value_docs, grad_docs, peak_docs, total_docs
    )
    query_return = pick_rows(grad_query_docs.reshape(-1, query_cols), return_rows, return_valid)
    key_return = pick_rows(grad_key_docs.reshape(-1, key_cols), return_rows, return_valid)
    value_return = pick_rows(grad_value_docs.reshape(-1, key_cols), return_rows, return_valid)
    query_back, key_back, value_back = (
        lax.all_to_all(query_return, "dp", split_axis=0, concat_axis=0, tiled=True),
        lax.all_to_all(key_return, "dp", split_axis=0, concat_axis=0, tiled=True),
        lax.all_to_all(value_return, "dp", split_axis=0, concat_axis=0, tiled=True),
    )
    grad_query_home = jnp.take(query_back.reshape(-1, query_cols), back_rows, axis=0).astype(
        jnp.float32
    )
    grad_key_home = jnp.take(key_back.reshape(-1, key_cols), back_rows, axis=0).astype(jnp.float32)
    grad_value_lin = jnp.take(value_back.reshape(-1, key_cols), back_rows, axis=0)
    grad_query_f, grad_key_f, grad_gain_query, grad_gain_key = prep_back(
        (grad_query_home, grad_key_home)
    )
    grad_query_lin = grad_query_f.astype(jnp.bfloat16)
    grad_key_lin = grad_key_f.astype(jnp.bfloat16)
    grad_query_w = jnp.einsum(
        "td,tc->dc", normed, grad_query_lin, preferred_element_type=jnp.float32
    )
    grad_key_w = jnp.einsum("td,tc->dc", normed, grad_key_lin, preferred_element_type=jnp.float32)
    grad_value_w = jnp.einsum(
        "td,tc->dc", normed, grad_value_lin, preferred_element_type=jnp.float32
    )
    normed_part = jnp.einsum(
        "tc,dc->td", grad_query_lin, full_query, preferred_element_type=jnp.float32
    )
    normed_part = normed_part + jnp.einsum(
        "tc,dc->td", grad_key_lin, full_key, preferred_element_type=jnp.float32
    )
    normed_part = normed_part + jnp.einsum(
        "tc,dc->td", grad_value_lin, full_value, preferred_element_type=jnp.float32
    )
    grad_normed, gain_query_sum, gain_key_sum = lax.psum(
        (normed_part, grad_gain_query, grad_gain_key), "mp"
    )
    attn_norm_pair = jax.vjp(rms_scale, hidden, gain_attn_f)
    grad_hidden_norm, grad_norm_attn = attn_norm_pair[1](grad_normed)
    grad_input = grad_middle + grad_hidden_norm
    attn_grads = (
        lax.psum_scatter(grad_query_w, "dp", scatter_dimension=0, tiled=True),
        lax.psum_scatter(grad_key_w, "dp", scatter_dimension=0, tiled=True),
        lax.psum_scatter(grad_value_w, "dp", scatter_dimension=0, tiled=True),
        lax.psum_scatter(grad_out_w, "dp", scatter_dimension=1, tiled=True),
        lax.psum_scatter(grad_norm_attn, "dp", scatter_dimension=0, tiled=True),
        lax.psum_scatter(gain_query_sum, "dp", scatter_dimension=0, tiled=True),
        lax.psum_scatter(gain_key_sum, "dp", scatter_dimension=0, tiled=True),
    )
    return (
        output,
        grad_input,
        attn_grads[0],
        attn_grads[1],
        attn_grads[2],
        attn_grads[3],
        mlp_grads[0],
        mlp_grads[1],
        mlp_grads[2],
        attn_grads[4],
        mlp_grads[3],
        attn_grads[5],
        attn_grads[6],
    )


def solution(mesh):
    return jax.shard_map(
        on_device,
        mesh=mesh,
        in_specs=(
            P("dp", None),
            P("dp", None),
            P(),
            P("dp", "mp"),
            P("dp", "mp"),
            P("dp", "mp"),
            P("mp", "dp"),
            P("dp", "mp"),
            P("dp", "mp"),
            P("mp", "dp"),
            P("dp"),
            P("dp"),
            P("dp"),
            P("dp"),
        ),
        out_specs=(
            P("dp", None),
            P("dp", None),
            P("dp", "mp"),
            P("dp", "mp"),
            P("dp", "mp"),
            P("mp", "dp"),
            P("dp", "mp"),
            P("dp", "mp"),
            P("mp", "dp"),
            P("dp"),
            P("dp"),
            P("dp"),
            P("dp"),
        ),
        check_vma=False,
    )
```

profile of v0, /device:TPU:0, one launch (start us, length us, event | category | flops | bytes accessed | tf_op | source)
XLA Modules:
  0.0 2167.3 jit_solution(12336115504664694873)
XLA Ops:
  31.1 13.2 all-reduce.12
  223.7 15.6 all-to-all-done.3
  260.9 280.1 %all-reduce.18.cloned.1.call-done = f32[1024,2048]{1,0:T(8,128)} async-done(((f32[1024,2048]{1,0:T(8,128)}), f32[1024,2048]{1,0:T(8,128)}) %all-reduce.18.cloned.1.call-update) | async-done | bytes 8388624 | tf_op jit(solution)/shard_map/psum | solution.py:234
  553.1 34.2 %all-gather.18.cloned.1.call-done = bf16[2048,1536]{1,0:T(8,128)(2,1)} async-done(((bf16[256,1536]{1,0:T(8,128)(2,1)}), bf16[2048,1536]{1,0:T(8,128)(2,1)}) %all-gather.18.cloned.1.call-update) | async-done | bytes 6291472 | tf_op jit(solution)/shard_map/all_gather | solution.py:159
  587.3 11.7 fusion.75
  599.0 35.7 %all-gather.20.cloned.1.call-done = bf16[2048,1536]{1,0:T(8,128)(2,1)} async-done(((bf16[256,1536]{1,0:T(8,128)(2,1)}), bf16[2048,1536]{1,0:T(8,128)(2,1)}) %all-gather.20.cloned.1.call-update) | async-done | bytes 6291472 | tf_op jit(solution)/shard_map/all_gather | solution.py:160
  634.8 11.7 fusion.76
  646.4 36.9 %all-gather.22.cloned.1.call-done = bf16[1536,2048]{1,0:T(8,128)(2,1)} async-done(((bf16[1536,256]{1,0:T(8,128)(2,1)}), bf16[1536,2048]{1,0:T(8,128)(2,1)}) %all-gather.22.cloned.1.call-update) | async-done | bytes 6291472 | tf_op jit(solution)/shard_map/all_gather | solution.py:161
  683.3 15.9 multiply_convert_fusion.1
  732.3 278.1 %all-reduce.22.cloned.1.call-done = f32[1024,2048]{1,0:T(8,128)} async-done(((f32[1024,2048]{1,0:T(8,128)}), f32[1024,2048]{1,0:T(8,128)}) %all-reduce.22.cloned.1.call-update) | async-done | bytes 8388624 | tf_op jit(solution)/shard_map/psum | solution.py:263
  1018.1 149.2 %all-reduce.20.cloned.1.call-done = bf16[1024,2048]{1,0:T(8,128)(2,1)} async-done(((bf16[1024,2048]{1,0:T(8,128)(2,1)}), bf16[1024,2048]{1,0:T(8,128)(2,1)}) %all-reduce.20.cloned.1.call-update) | async-done | bytes 4194320 | tf_op jit(solution)/shard_map/psum | solution.py:243
  1167.3 12.3 fusion.5
  1194.4 30.5 %all_to_all.40 = bf16[8,256,512]{2,1,0:T(8,128)(2,1)S(1)} all-to-all(bf16[8,256,512]{2,1,0:T(8,128)(2,1)S(1)} %bitcast.174), channel_id=1, replica_groups=mesh['dp'=8,'mp'=4] {'dp'}, dimensions={0} | all-to-all | bytes 4194304 | tf_op jit(solution)/shard_map/all_to_all | solution.py:283
  1283.2 18.5 all_to_all.41
  1421.8 11.5 fusion.83
  1448.0 221.7 %all-reduce.24.cloned.1.call-done = f32[1024,2048]{1,0:T(8,128)} async-done(((f32[1024,2048]{1,0:T(8,128)}), f32[1024,2048]{1,0:T(8,128)}) %all-reduce.24.cloned.1.call-update) | async-done | bytes 8388624 | tf_op jit(solution)/shard_map/psum | solution.py:355
  1675.8 24.2 %all-reduce.10 = (f32[2048]{0:T(1024)S(1)}, f32[2048]{0:T(1024)S(1)}, f32[128]{0:T(128)S(1)}, f32[128]{0:T(128)S(1)}) all-reduce(f32[2048]{0:T(1024)S(1)} %get-tuple-element.25, f32[2048]{0:T(1024)S(1)} %copy-done.57, f32[128]{0:T(128)S(1)} %get-tuple-element.27, ...), channel_id=9, replica_groups=mesh['dp'=8,'mp'=4] {'dp'}, use_global_device_ids=true, to_apply=%region_35.42.clone | all-reduce | flops 4352 | bytes 34816
  1711.7 11.7 fusion.6
  1723.5 35.7 %reduce-scatter.12.cloned.1.call-done = f32[256,256]{1,0:T(8,128)} async-done(((f32[2048,256]{1,0:T(8,128)}), f32[256,256]{1,0:T(8,128)}) %reduce-scatter.12.cloned.1.call-update) | async-done | bytes 262160 | tf_op jit(solution)/shard_map/reduce_scatter | solution.py:364
  1759.1 55.5 %reduce-scatter.14.cloned.1.call-done = f32[512,256]{1,0:T(8,128)} async-done(((f32[512,2048]{1,0:T(8,128)}), f32[512,256]{1,0:T(8,128)}) %reduce-scatter.14.cloned.1.call-update) | async-done | bytes 524304 | tf_op jit(solution)/shard_map/reduce_scatter | solution.py:365
  1814.7 55.1 %reduce-scatter.8.cloned.1.call-done = f32[256,512]{1,0:T(8,128)} async-done(((f32[2048,512]{1,0:T(8,128)}), f32[256,512]{1,0:T(8,128)}) %reduce-scatter.8.cloned.1.call-update) | async-done | bytes 524304 | tf_op jit(solution)/shard_map/reduce_scatter | solution.py:362
  1869.8 96.8 %reduce-scatter.16.cloned.1.call-done = f32[256,1536]{1,0:T(8,128)} async-done(((f32[2048,1536]{1,0:T(8,128)}), f32[256,1536]{1,0:T(8,128)}) %reduce-scatter.16.cloned.1.call-update) | async-done | bytes 1572880 | tf_op jit(solution)/shard_map/reduce_scatter | solution.py:268
  1966.5 96.7 %reduce-scatter.18.cloned.1.call-done = f32[256,1536]{1,0:T(8,128)} async-done(((f32[2048,1536]{1,0:T(8,128)}), f32[256,1536]{1,0:T(8,128)}) %reduce-scatter.18.cloned.1.call-update) | async-done | bytes 1572880 | tf_op jit(solution)/shard_map/reduce_scatter | solution.py:269
  2063.3 96.8 %reduce-scatter.20.cloned.1.call-done = f32[1536,256]{1,0:T(8,128)} async-done(((f32[1536,2048]{1,0:T(8,128)}), f32[1536,256]{1,0:T(8,128)}) %reduce-scatter.20.cloned.1.call-update) | async-done | bytes 1572880 | tf_op jit(solution)/shard_map/reduce_scatter | solution.py:270
  (376 shorter events, 499.9 us)
Async XLA Ops:
  7.2 43.6 %all-gather.12.cloned.1.call-start = ((), (), s32[]{:S(2)}) async-start(), calls=%async_computation.16 | async-start | bytes 1179648 | tf_op jit(solution)/shard_map/all_gather | solution.py:149
  8.0 53.6 %all-gather.10.cloned.1.call-start = ((), (), s32[]{:S(2)}) async-start(), calls=%async_computation.15 | async-start | bytes 1179648 | tf_op jit(solution)/shard_map/all_gather | solution.py:150
  8.7 82.7 %all-gather.14.cloned.1.call-start = ((), (), s32[]{:S(2)}) async-start(), calls=%async_computation.17 | async-start | bytes 2359296 | tf_op jit(solution)/shard_map/all_gather | solution.py:148
  85.9 19.2 all-to-all-start
  105.1 20.2 all-to-all-start.1
  126.2 34.6 %all-to-all-start.2 = ((bf16[8,256,512]{2,1,0:T(8,128)(2,1)}), bf16[8,256,512]{2,1,0:T(8,128)(2,1)S(1)}, u32[]{:S(2)}, u32[]{:S(2)}) async-start(bf16[8,256,512]{2,1,0:T(8,128)(2,1)} %bitcast.172), calls=%async_computation.2 | async-start | bytes 4194304 | tf_op jit(solution)/shard_map/all_to_all | solution.py:197
  130.3 112.9 %all-gather.16.cloned.1.call-start = ((), (), s32[]{:S(2)}) async-start(), calls=%async_computation.18 | async-start | bytes 2359296 | tf_op jit(solution)/shard_map/all_gather | solution.py:151
  208.4 30.8 %all-to-all-start.3 = ((bf16[8,256,512]{2,1,0:T(8,128)(2,1)}), bf16[8,256,512]{2,1,0:T(8,128)(2,1)S(1)}, u32[]{:S(2)}, u32[]{:S(2)}) async-start(bf16[8,256,512]{2,1,0:T(8,128)(2,1)} %bitcast.173), calls=%async_computation.3 | async-start | bytes 4194304 | tf_op jit(solution)/shard_map/all_to_all | solution.py:232
  212.6 328.4 %all-reduce.18.cloned.1.call-start = ((), (), s32[]{:S(2)}) async-start(), calls=%async_computation.19 | async-start | bytes 16777216 | tf_op jit(solution)/shard_map/psum | solution.py:234
  250.8 336.5 %all-gather.18.cloned.1.call-start = ((), (), s32[]{:S(2)}) async-start(), calls=%async_computation.20 | async-start | bytes 7077888 | tf_op jit(solution)/shard_map/all_gather | solution.py:159
  251.4 383.4 %all-gather.20.cloned.1.call-start = ((), (), s32[]{:S(2)}) async-start(), calls=%async_computation.21 | async-start | bytes 7077888 | tf_op jit(solution)/shard_map/all_gather | solution.py:160
  252.1 431.2 %all-gather.22.cloned.1.call-start = ((), (), s32[]{:S(2)}) async-start(), calls=%async_computation.22 | async-start | bytes 7077888 | tf_op jit(solution)/shard_map/all_gather | solution.py:161
  252.9 757.6 %all-reduce.22.cloned.1.call-start = ((), (), s32[]{:S(2)}) async-start(), calls=%async_computation.24 | async-start | bytes 16777216 | tf_op jit(solution)/shard_map/psum | solution.py:263
  719.5 447.8 %all-reduce.20.cloned.1.call-start = ((), (), s32[]{:S(2)}) async-start(), calls=%async_computation.23 | async-start | bytes 8388608 | tf_op jit(solution)/shard_map/psum | solution.py:243
  1301.7 25.5 %all-to-all-start.7 = ((bf16[8,256,256]{2,1,0:T(8,128)(2,1)}), bf16[8,256,256]{2,1,0:T(8,128)(2,1)S(1)}, u32[]{:S(2)}, u32[]{:S(2)}) async-start(bf16[8,256,256]{2,1,0:T(8,128)(2,1)} %bitcast.37), calls=%async_computation.7 | async-start | bytes 2097152 | tf_op jit(solution)/shard_map/all_to_all | solution.py:327
  1327.2 30.9 %all-to-all-start.5 = ((bf16[8,256,512]{2,1,0:T(8,128)(2,1)}), bf16[8,256,512]{2,1,0:T(8,128)(2,1)S(1)}, u32[]{:S(2)}, u32[]{:S(2)}) async-start(bf16[8,256,512]{2,1,0:T(8,128)(2,1)} %bitcast.171), calls=%async_computation.5 | async-start | bytes 4194304 | tf_op jit(solution)/shard_map/all_to_all | solution.py:325
  1331.4 338.3 %all-reduce.24.cloned.1.call-start = ((), (), s32[]{:S(2)}) async-start(), calls=%async_computation.25 | async-start | bytes 16777216 | tf_op jit(solution)/shard_map/psum | solution.py:355
  1380.7 342.8 %reduce-scatter.10.cloned.1.call-start = ((), (), s32[]{:S(2)}) async-start(), calls=%async_computation.27 | async-start | bytes 2359296 | tf_op jit(solution)/shard_map/reduce_scatter | solution.py:363
  1386.6 372.6 %reduce-scatter.12.cloned.1.call-start = ((), (), s32[]{:S(2)}) async-start(), calls=%async_computation.28 | async-start | bytes 2359296 | tf_op jit(solution)/shard_map/reduce_scatter | solution.py:364
  1391.9 422.8 %reduce-scatter.14.cloned.1.call-start = ((), (), s32[]{:S(2)}) async-start(), calls=%async_computation.29 | async-start | bytes 4718592 | tf_op jit(solution)/shard_map/reduce_scatter | solution.py:365
  1399.8 470.0 %reduce-scatter.8.cloned.1.call-start = ((), (), s32[]{:S(2)}) async-start(), calls=%async_computation.26 | async-start | bytes 4718592 | tf_op jit(solution)/shard_map/reduce_scatter | solution.py:362
  1406.6 559.9 %reduce-scatter.16.cloned.1.call-start = ((), (), s32[]{:S(2)}) async-start(), calls=%async_computation.30 | async-start | bytes 14155776 | tf_op jit(solution)/shard_map/reduce_scatter | solution.py:268
  1420.0 643.3 %reduce-scatter.18.cloned.1.call-start = ((), (), s32[]{:S(2)}) async-start(), calls=%async_computation.31 | async-start | bytes 14155776 | tf_op jit(solution)/shard_map/reduce_scatter | solution.py:269
  1433.4 726.6 %reduce-scatter.20.cloned.1.call-start = ((), (), s32[]{:S(2)}) async-start(), calls=%async_computation.32 | async-start | bytes 14155776 | tf_op jit(solution)/shard_map/reduce_scatter | solution.py:270
  (80 other events, 2762.0 us)
Sparse Core Ops, SparseCore 0:
  9.9 26.1 all-gather.11
  38.1 23.4 all-gather.9
  63.5 27.8 all-gather.13
  132.7 38.2 all-gather.15
  250.9 290.0 all-reduce.17
  542.8 44.5 all-gather.17
  589.2 45.5 all-gather.19
  636.6 46.6 all-gather.21
  719.6 290.8 all-reduce.21
  1013.3 153.9 all-reduce.19
  1380.8 288.8 all-reduce.23
  1673.8 40.2 reduce-scatter.9
  1717.9 41.1 reduce-scatter.11
  1763.3 51.3 reduce-scatter.13
  1818.4 51.3 reduce-scatter.7
  1874.1 92.3 reduce-scatter.15
  1970.9 92.3 reduce-scatter.17
  2067.6 92.3 reduce-scatter.19
where the time goes:
time: 2180 us; the launch traced here: 2170 us
  waiting for transfers between devices  1510 us (69%)
  local copies, waits for them, and re-layouts  195 us (9%)
  matrix products  188 us (9%)
  blocking collectives  115 us (5%)
  other arithmetic  108 us (5%)
  starting transfers between devices  35.7 us (2%)
    psum x1, waiting for transfers between devices, on_device(): lax.psum(jnp.dot(attended_home, full_out, preferred_element_type=jnp.floa...  280 us
    psum x1, waiting for transfers between devices, on_device(): grad_normed_two = lax.psum(normed_two_part, 'mp')  278 us
    psum x1, waiting for transfers between devices, on_device(): lax.psum((normed_part, grad_gain_query, grad_gain_key), 'mp')  222 us
    psum x1, waiting for transfers between devices, on_device(): lax.psum(down_part.astype(jnp.bfloat16), 'mp').astype(jnp.float32)  149 us
    gather x12, local copies, waits for them, and re-layouts, pick_rows(): picked_rows = jnp.take(values, row_ids.reshape(-1), axis=0)  104 us
    reduce_scatter x1, waiting for transfers between devices, on_device(): lax.psum_scatter(grad_gate_w, 'dp', scatter_dimension=0, tiled=True)  96.8 us
    reduce_scatter x1, waiting for transfers between devices, on_device(): lax.psum_scatter(grad_down_w, 'dp', scatter_dimension=1, tiled=True)  96.8 us
    reduce_scatter x1, waiting for transfers between devices, on_device(): lax.psum_scatter(grad_up_w, 'dp', scatter_dimension=0, tiled=True)  96.7 us
  transfers between devices with their start and end apart: 24, of which 18 were waited for; matrix products, arithmetic and copies ran while one was open for 15% of the time, Pallas kernels for 0%

commit v1 on v0

v1 whole, which is shorter than its diff:
```python
import functools

import jax
import jax.numpy as jnp
from jax import lax
from jax.experimental import pallas as pl
from jax.experimental.pallas import tpu as pltpu
from jax.sharding import PartitionSpec as P

HD = 128
CHUNK = 256
EPSILON = 1e-06
ROPE_BASE = 1000000.0
SCALE = HD ** (-0.5)
BF = jnp.bfloat16
F32 = jnp.float32
VMEM_LIMIT = 56 * 1024 * 1024

NN = (((1,), (0,)), ((), ()))
NT = (((1,), (1,)), ((), ()))
TN = (((0,), (0,)), ((), ()))


def dot(a, b, dims=NN):
    return lax.dot_general(a, b, dims, preferred_element_type=F32)


def whole():
    return pl.BlockSpec(memory_space=pltpu.VMEM)


def smem():
    return pl.BlockSpec(memory_space=pltpu.SMEM)


def hbm():
    return pl.BlockSpec(memory_space=pl.ANY)


def params(**kw):
    return pltpu.CompilerParams(vmem_limit_bytes=VMEM_LIMIT, **kw)


def cost(flops, nbytes):
    return pl.CostEstimate(flops=int(flops), bytes_accessed=int(nbytes), transcendentals=0)


def rms_r(values):
    return lax.rsqrt(jnp.mean(values * values, axis=-1, keepdims=True) + EPSILON)


def qkv_kernel(nq, nk, pieces, x_ref, gain_ref, w_ref, cos_ref, sin_ref, gq_ref, gk_ref, normed_ref, lin_ref, rot_ref):
    x = x_ref[...].astype(F32)
    normed = (x * rms_r(x) * gain_ref[...]).astype(BF)
    normed_ref[...] = normed
    depth = x.shape[1] // pieces
    acc = jnp.zeros((x.shape[0], w_ref.shape[2]), F32)
    for p in range(pieces):
        acc = acc + dot(normed[:, p * depth : (p + 1) * depth], w_ref[p, :depth, :])
    cosine = cos_ref[...]
    sine = sin_ref[...]
    for h in range(nq + nk):
        v = acc[:, h * HD : (h + 1) * HD]
        gain = gq_ref[...] if h < nq else gk_ref[...]
        n = v * rms_r(v) * gain
        rot_ref[:, h * HD : (h + 1) * HD] = (n * cosine + pltpu.roll(n, HD // 2, 1) * sine).astype(BF)
    lin_ref[...] = acc[:, : (nq + nk) * HD]
    rot_ref[:, (nq + nk) * HD :] = acc[:, (nq + nk) * HD :].astype(BF)


def qkv_call(x, gain, w, cosine, sine, gq, gk, nq, nk):
    tok, d = x.shape
    pieces = w.shape[0]
    cols = w.shape[2]
    blk = lambda n: pl.BlockSpec((CHUNK, n), lambda i: (i, 0))
    full = lambda a: pl.BlockSpec(a.shape, lambda i: (0,) * a.ndim)
    lin = (nq + nk) * HD
    return pl.pallas_call(
        functools.partial(qkv_kernel, nq, nk, pieces),
        grid=(tok // CHUNK,),
        in_specs=[blk(d), full(gain), full(w), blk(HD), blk(HD), full(gq), full(gk)],
        out_specs=[blk(d), blk(lin), blk(cols)],
        out_shape=[
            jax.ShapeDtypeStruct((tok, d), BF),
            jax.ShapeDtypeStruct((tok, lin), F32),
            jax.ShapeDtypeStruct((tok, cols), BF),
        ],
        compiler_params=params(),
        cost_estimate=cost(2 * tok * d * cols * 1.5, 20e6),
    )(x, gain, w, cosine, sine, gq, gk)


def band(c):
    lo = max(c - 1, 0) * CHUNK
    return lo, (c + 1) * CHUNK - lo


def allowed(c, col_ref, row_ref):
    lo, width = band(c)
    same = col_ref[c * CHUNK : (c + 1) * CHUNK, :] == row_ref[:, lo : lo + width]
    t = lax.broadcasted_iota(jnp.int32, (CHUNK, width), 0) + c * CHUNK
    u = lax.broadcasted_iota(jnp.int32, (CHUNK, width), 1) + lo
    return same & (u <= t)


def attn_kernel(c, nq, nk, aliased, rot_ref, col_ref, row_ref, w_ref, *rest):
    att_ref, lse_ref, part_ref = rest[1:] if aliased else rest
    lo, width = band(c)
    mask = allowed(c, col_ref, row_ref)
    group = nq // nk
    heads = []
    lses = []
    for h in range(nq):
        q = rot_ref[c * CHUNK : (c + 1) * CHUNK, h * HD : (h + 1) * HD]
        j = h // group
        k = rot_ref[lo : lo + width, (nq + j) * HD : (nq + j + 1) * HD]
        v = rot_ref[lo : lo + width, (nq + nk + j) * HD : (nq + nk + j + 1) * HD]
        s = jnp.where(mask, dot(q, k, NT) * SCALE, -1e30)
        m = jnp.max(s, axis=-1, keepdims=True)
        e = jnp.exp(s - m)
        l = jnp.sum(e, axis=-1, keepdims=True)
        heads.append(dot((e / l).astype(BF), v).astype(BF))
        lses.append(m + jnp.log(l))
    att = jnp.concatenate(heads, axis=1)
    att_ref[...] = att
    lse_ref[...] = jnp.concatenate(lses, axis=1)
    pieces = w_ref.shape[0]
    width_d = w_ref.shape[2]
    for p in range(pieces):
        part_ref[:, p * width_d : (p + 1) * width_d] = dot(att, w_ref[p]).astype(BF)


def chunk_block(c, n):
    return pl.BlockSpec((CHUNK, n), lambda i: (c, 0))


def attn_call(c, rot, col, row, w_out, att, nq, nk):
    tok = rot.shape[0]
    d = w_out.shape[0] * w_out.shape[2]
    first = att is None
    args = [rot, col, row, w_out] + ([] if first else [att])
    full = lambda a: pl.BlockSpec(a.shape, lambda i: (0,) * a.ndim)
    return pl.pallas_call(
        functools.partial(attn_kernel, c, nq, nk, not first),
        grid=(1,),
        in_specs=[full(a) for a in args[:4]] + ([] if first else [hbm()]),
        out_specs=[
            chunk_block(c, nq * HD),
            pl.BlockSpec((CHUNK, nq), lambda i: (0, 0)),
            pl.BlockSpec((CHUNK, d), lambda i: (0, 0)),
        ],
        out_shape=[
            jax.ShapeDtypeStruct((tok, nq * HD), BF),
            jax.ShapeDtypeStruct((CHUNK, nq), F32),
            jax.ShapeDtypeStruct((CHUNK, d), BF),
        ],
        input_output_aliases={} if first else {4: 0},
        compiler_params=params(),
        cost_estimate=cost(2e9, 6e6),
    )(*args)


def mlp_kernel(
    pieces,
    n_alias,
    flag_ref,
    x_ref,
    t_ref,
    r_ref,
    cot_ref,
    gain_ref,
    wg_ref,
    wu_ref,
    wd_ref,
    *rest,
):
    mid_ref, n2_ref, prod_ref, gg_ref, gu_ref, down_ref, gnt_ref, acc_d, acc_g, n2 = rest[n_alias:]
    j = pl.program_id(0)
    wide = wd_ref.shape[2]

    @pl.when(j == 0)
    def _():
        branch = jnp.where(flag_ref[0] == 1, r_ref[...], t_ref[...]).astype(F32)
        mid = x_ref[...].astype(F32) + branch
        mid_ref[...] = mid
        n = (mid * rms_r(mid) * gain_ref[...]).astype(BF)
        n2[...] = n
        n2_ref[...] = n
        acc_d[...] = jnp.zeros_like(acc_d)
        acc_g[...] = jnp.zeros_like(acc_g)

    g = dot(n2[...], wg_ref[...])
    u = dot(n2[...], wu_ref[...])
    gp = jnp.zeros_like(g)
    for p in range(pieces):
        gp = gp + dot(cot_ref[:, p * wide : (p + 1) * wide], wd_ref[p], NT)
    s = 1.0 / (1.0 + jnp.exp(-g))
    prod = (g * s * u).astype(BF)
    prod_ref[...] = prod
    gg = (gp * u * s * (1.0 + g * (1.0 - s))).astype(BF)
    gu = (gp * g * s).astype(BF)
    gg_ref[...] = gg
    gu_ref[...] = gu
    acc_g[...] += dot(gg, wg_ref[...], NT) + dot(gu, wu_ref[...], NT)
    for p in range(pieces):
        acc_d[:, p * wide : (p + 1) * wide] += dot(prod, wd_ref[p])

    @pl.when(j == pl.num_programs(0) - 1)
    def _():
        down_ref[...] = acc_d[...].astype(BF)
        gnt_ref[...] = acc_g[...].astype(BF)


def mlp_call(c, flag, x, t, r, cot, gain, wg, wu, wd, kept):
    tok, d = x.shape
    ff = wg.shape[1]
    tile = 512 if ff % 512 == 0 else 256
    pieces = wd.shape[0]
    first = kept is None
    blk = chunk_block(c, d)
    own = pl.BlockSpec((CHUNK, d), lambda j: (0, 0))
    ffblk = pl.BlockSpec((CHUNK, tile), lambda j: (c, j))
    full = lambda a: pl.BlockSpec(a.shape, lambda j: (0,) * a.ndim)
    n_alias = 0 if first else 4
    out = pl.pallas_call(
        functools.partial(mlp_kernel, pieces, n_alias),
        grid=(ff // tile,),
        in_specs=[
            smem(),
            blk,
            own,
            own,
            blk,
            full(gain),
            pl.BlockSpec((d, tile), lambda j: (0, j)),
            pl.BlockSpec((d, tile), lambda j: (0, j)),
            pl.BlockSpec((pieces, tile, wd.shape[2]), lambda j: (0, j, 0)),
        ]
        + [hbm()] * n_alias,
        out_specs=[own, blk, ffblk, ffblk, ffblk, own, own],
        out_shape=[
            jax.ShapeDtypeStruct((CHUNK, d), F32),
            jax.ShapeDtypeStruct((tok, d), BF),
            jax.ShapeDtypeStruct((tok, ff), BF),
            jax.ShapeDtypeStruct((tok, ff), BF),
            jax.ShapeDtypeStruct((tok, ff), BF),
            jax.ShapeDtypeStruct((CHUNK, d), BF),
            jax.ShapeDtypeStruct((CHUNK, d), BF),
        ],
        scratch_shapes=[
            pltpu.VMEM((CHUNK, d), F32),
            pltpu.VMEM((CHUNK, d), F32),
            pltpu.VMEM((CHUNK, d), BF),
        ],
        input_output_aliases={} if first else {9: 1, 10: 2, 11: 3, 12: 4},
        compiler_params=params(),
        cost_estimate=cost(12 * CHUNK * d * ff * 1.3, 30e6),
    )(flag, x, t, r, cot, gain, wg, wu, wd, *([] if first else kept))
    return out[0], out[1:5], out[5], out[6]


def back_kernel(
    c,
    nq,
    nk,
    first,
    last,
    flag_ref,
    mid_ref,
    t_ref,
    r_ref,
    cot_ref,
    gain_ref,
    wo_ref,
    rot_ref,
    col_ref,
    row_ref,
    lse_ref,
    lin_ref,
    cos_ref,
    sin_ref,
    gq_ref,
    gk_ref,
    w_ref,
    *rest,
):
    if not first:
        carry_ref, rest = rest[0], rest[3:]
    gm_ref, gb_ref, gqkv_ref, part_ref, gain_out, head_out, carry_out = rest
    gnt = jnp.where(flag_ref[0] == 1, r_ref[...], t_ref[...]).astype(F32)
    mid = mid_ref[...]
    r2 = rms_r(mid)
    h = gnt * gain_ref[...]
    gm = (
        cot_ref[...].astype(F32)
        + r2 * h
        - mid * (r2 * r2 * r2 * jnp.mean(h * mid, axis=-1, keepdims=True))
    )
    gain_out[...] = jnp.sum(gnt * mid * r2, axis=0, keepdims=True)
    gm_ref[...] = gm
    gb = gm.astype(BF)
    gb_ref[...] = gb
    pieces = wo_ref.shape[0]
    wide = wo_ref.shape[2]
    ga = jnp.zeros((CHUNK, nq * HD), F32)
    for p in range(pieces):
        ga = ga + dot(gb[:, p * wide : (p + 1) * wide], wo_ref[p], NT)
    ga = ga.astype(BF)
    lo, width = band(c)
    mask = allowed(c, col_ref, row_ref)
    group = nq // nk
    cosine = cos_ref[...]
    sine = -sin_ref[...]

    def unrope(grad, lin, gain):
        gr = grad * cosine + pltpu.roll(grad, HD // 2, 1) * sine
        rr = rms_r(lin)
        hh = gr * gain
        out = rr * hh - lin * (rr * rr * rr * jnp.mean(hh * lin, axis=-1, keepdims=True))
        return out.astype(BF), jnp.sum(gr * lin * rr, axis=0, keepdims=True)

    sum_q = jnp.zeros((1, HD), F32)
    sum_k = jnp.zeros((1, HD), F32)
    outs = [None] * (nq + 2 * nk)
    for j in range(nk):
        k = rot_ref[lo : lo + width, (nq + j) * HD : (nq + j + 1) * HD]
        v = rot_ref[lo : lo + width, (nq + nk + j) * HD : (nq + nk + j + 1) * HD]
        dk = jnp.zeros((width, HD), F32)
        dv = jnp.zeros((width, HD), F32)
        for g in range(group):
            i = j * group + g
            q = rot_ref[c * CHUNK : (c + 1) * CHUNK, i * HD : (i + 1) * HD]
            gah = ga[:, i * HD : (i + 1) * HD]
            s = jnp.where(mask, dot(q, k, NT) * SCALE, -1e30)
            w = jnp.exp(s - lse_ref[:, i : i + 1])
            gw = dot(gah, v, NT)
            delta = jnp.sum(w * gw, axis=-1, keepdims=True)
            gs = (w * (gw - delta)).astype(BF)
            dq = (dot(gs, k) * SCALE).astype(BF).astype(F32)
            dk = dk + dot(gs, q, TN)
            dv = dv + dot(w.astype(BF), gah, TN)
            outs[i], part = unrope(dq, lin_ref[:, i * HD : (i + 1) * HD], gq_ref[...])
            sum_q = sum_q + part
        dk_own, dv_own = dk[width - CHUNK :], dv[width - CHUNK :]
        if not first:
            dk_own = dk_own + carry_ref[:, j * HD : (j + 1) * HD]
            dv_own = dv_own + carry_ref[:, (nk + j) * HD : (nk + j + 1) * HD]
        carry_out[:, j * HD : (j + 1) * HD] = dk[:CHUNK]
        carry_out[:, (nk + j) * HD : (nk + j + 1) * HD] = dv[:CHUNK]
        dk_own = (dk_own * SCALE).astype(BF).astype(F32)
        outs[nq + j], part = unrope(dk_own, lin_ref[:, (nq + j) * HD : (nq + j + 1) * HD], gk_ref[...])
        sum_k = sum_k + part
        outs[nq + nk + j] = dv_own.astype(BF)
    gqkv = jnp.concatenate(outs, axis=1)
    gqkv_ref[...] = gqkv
    head_out[0:1, :] = sum_q
    head_out[1:2, :] = sum_k
    depth = gb.shape[1] // w_ref.shape[0]
    for p in range(w_ref.shape[0]):
        part_ref[:, p * depth : (p + 1) * depth] = dot(gqkv, w_ref[p, :depth, :], NT).astype(BF)


def back_call(c, flag, mid, t, r, cot, gain, wo, rot, col, row, lse, lin, cosine, sine, gq, gk, w, kept, carry, nq, nk, last):
    tok, d = cot.shape
    first = carry is None
    full = lambda a: pl.BlockSpec(a.shape, lambda i: (0,) * a.ndim)
    args = [flag, mid, t, r, cot, gain, wo, rot, col, row, lse, lin, cosine, sine, gq, gk, w]
    specs = [smem()] + [full(a) for a in args[1:]]
    specs[4] = chunk_block(c, d)
    specs[11] = chunk_block(c, lin.shape[1])
    specs[12] = chunk_block(c, HD)
    specs[13] = chunk_block(c, HD)
    if not first:
        args += [carry, *kept]
        specs += [full(carry), hbm(), hbm()]
    own = lambda n: pl.BlockSpec((CHUNK, n), lambda i: (0, 0))
    cols = (nq + 2 * nk) * HD
    out = pl.pallas_call(
        functools.partial(back_kernel, c, nq, nk, first, last),
        grid=(1,),
        in_specs=specs,
        out_specs=[
            own(d),
            chunk_block(c, d),
            chunk_block(c, cols),
            own(d),
            pl.BlockSpec((1, d), lambda i: (0, 0)),
            pl.BlockSpec((2, HD), lambda i: (0, 0)),
            own(2 * nk * HD),
        ],
        out_shape=[
            jax.ShapeDtypeStruct((CHUNK, d), F32),
            jax.ShapeDtypeStruct((tok, d), BF),
            jax.ShapeDtypeStruct((tok, cols), BF),
            jax.ShapeDtypeStruct((CHUNK, d), BF),
            jax.ShapeDtypeStruct((1, d), F32),
            jax.ShapeDtypeStruct((2, HD), F32),
            jax.ShapeDtypeStruct((CHUNK, 2 * nk * HD), F32),
        ],
        input_output_aliases={} if first else {18: 1, 19: 2},
        compiler_params=params(),
        cost_estimate=cost(6e9, 20e6),
    )(*args)
    return out[0], out[1:3], out[3], out[4], out[5], out[6]


def input_kernel(aliased, flag_ref, x_ref, t_ref, r_ref, gm_ref, gain_ref, *rest):
    out_ref, gain_out = rest[1:] if aliased else rest
    gn = jnp.where(flag_ref[0] == 1, r_ref[...], t_ref[...]).astype(F32)
    x = x_ref[...].astype(F32)
    r1 = rms_r(x)
    h = gn * gain_ref[...]
    out_ref[...] = gm_ref[...] + r1 * h - x * (r1 * r1 * r1 * jnp.mean(h * x, axis=-1, keepdims=True))
    gain_out[...] = jnp.sum(gn * x * r1, axis=0, keepdims=True)


def input_call(c, flag, x, t, r, gm, gain, kept):
    tok, d = x.shape
    own = pl.BlockSpec((CHUNK, d), lambda i: (0, 0))
    first = kept is None
    return pl.pallas_call(
        functools.partial(input_kernel, not first),
        grid=(1,),
        in_specs=[smem(), chunk_block(c, d), own, own, own, pl.BlockSpec((1, d), lambda i: (0, 0))]
        + ([] if first else [hbm()]),
        out_specs=[chunk_block(c, d), pl.BlockSpec((1, d), lambda i: (0, 0))],
        out_shape=[jax.ShapeDtypeStruct((tok, d), F32), jax.ShapeDtypeStruct((1, d), F32)],
        input_output_aliases={} if first else {6: 0},
        compiler_params=params(),
        cost_estimate=cost(1e6, 8e6),
    )(flag, x, t, r, gm, gain, *([] if first else [kept]))


def output_kernel(aliased, flag_ref, mid_ref, t_ref, r_ref, *rest):
    out_ref = rest[-1]
    down = jnp.where(flag_ref[0] == 1, r_ref[...], t_ref[...]).astype(F32)
    out_ref[...] = (mid_ref[...] + down).astype(BF)


def output_call(c, flag, mid, t, r, kept, tok):
    d = mid.shape[1]
    own = pl.BlockSpec((CHUNK, d), lambda i: (0, 0))
    first = kept is None
    return pl.pallas_call(
        functools.partial(output_kernel, not first),
        grid=(1,),
        in_specs=[smem(), own, own, own] + ([] if first else [hbm()]),
        out_specs=chunk_block(c, d),
        out_shape=jax.ShapeDtypeStruct((tok, d), BF),
        input_output_aliases={} if first else {4: 0},
        compiler_params=params(),
        cost_estimate=cost(1e6, 5e6),
    )(flag, mid, t, r, *([] if first else [kept]))


def line_sum(x):
    n = lax.axis_size("mp")
    me = lax.axis_index("mp")
    half = n // 2
    for h in range(half - 1):
        x = x + lax.ppermute(x, "mp", [(h, h + 1), (n - 1 - h, n - 2 - h)])
    x = x + lax.ppermute(x, "mp", [(half - 1, half), (half, half - 1)])
    r = x
    for h in reversed(range(half - 1)):
        r = lax.ppermute(x, "mp", [(h + 1, h), (n - 2 - h, n - 1 - h)])
        if h:
            x = jnp.where((me == h) | (me == n - 1 - h), r, x)
    return x, r


def swap_sum(x, axis):
    n = lax.axis_size(axis)
    step = 1
    while step < n:
        x = x + lax.ppermute(x, axis, [(i, i ^ step) for i in range(n)])
        step *= 2
    return x


def own_sum(rows, axis):
    n = lax.axis_size(axis)
    me = lax.axis_index(axis)
    total = lax.dynamic_index_in_dim(rows, me, 0)
    for step in range(1, n):
        part = lax.dynamic_index_in_dim(rows, me ^ step, 0)
        total = total + lax.ppermute(part, axis, [(i, i ^ step) for i in range(n)])
    return total[0]


def on_device(
    hidden_in,
    cotangent,
    doc_lengths,
    w_query,
    w_key,
    w_value,
    w_out,
    w_gate,
    w_up,
    w_down,
    norm_attn,
    norm_mlp,
    norm_query,
    norm_key,
):
    n_dp = lax.axis_size("dp")
    dp = lax.axis_index("dp")
    mp = lax.axis_index("mp")
    n_mp = lax.axis_size("mp")
    tok, d = hidden_in.shape
    nq = w_query.shape[1] // HD
    nk = w_key.shape[1] // HD
    depth = w_query.shape[0]
    cols = (nq + 2 * nk) * HD
    small = norm_query.shape[0]
    flag = ((mp == 0) | (mp == n_mp - 1)).astype(jnp.int32).reshape(1)

    gains = jnp.concatenate([norm_attn, norm_mlp, norm_query, norm_key])
    per_row = cols
    n_rows = -(-gains.shape[0] // per_row)
    gain_rows = jnp.pad(gains, (0, 16 * per_row * -(-n_rows // 16) - gains.shape[0])).reshape(-1, per_row)
    w_qkv = jnp.concatenate([jnp.concatenate([w_query, w_key, w_value], axis=1), gain_rows], axis=0)
    w_qkv = lax.all_gather(w_qkv, "dp", axis=0)
    w_out = lax.all_gather(w_out, "dp", axis=0)
    w_gate = lax.all_gather(w_gate, "dp", axis=0, tiled=True)
    w_up = lax.all_gather(w_up, "dp", axis=0, tiled=True)
    w_down = lax.all_gather(w_down, "dp", axis=0)
    flat = w_qkv[:, depth:, :].reshape(n_dp, -1)[:, : gains.shape[0]].astype(F32)
    gain_attn = flat[:, :depth].reshape(1, d)
    gain_mlp = flat[:, depth : 2 * depth].reshape(1, d)
    gain_query = flat[:, 2 * depth : 2 * depth + small].reshape(1, HD)
    gain_key = flat[:, 2 * depth + small :].reshape(1, HD)

    lengths = lax.dynamic_index_in_dim(doc_lengths, dp, 0, keepdims=False)
    ends = jnp.cumsum(lengths)
    token = jnp.arange(tok, dtype=jnp.int32)
    passed = token[:, None] >= ends[None, :]
    doc = jnp.sum(passed.astype(jnp.int32), axis=1)
    position = token - jnp.sum(jnp.where(passed, lengths[None, :], 0), axis=1)
    inverse = ROPE_BASE ** (-(2.0 * jnp.arange(HD // 2, dtype=F32)) / HD)
    angles = position.astype(F32)[:, None] * inverse[None, :]
    cosine = jnp.cos(angles)
    sine = jnp.sin(angles)
    cosine = jnp.concatenate([cosine, cosine], axis=1)
    sine = jnp.concatenate([-sine, sine], axis=1)
    col = doc[:, None]
    row = doc[None, :]

    normed, lin, rot = qkv_call(hidden_in, gain_attn, w_qkv, cosine, sine, gain_query, gain_key, nq, nk)

    order = list(reversed(range(tok // CHUNK)))
    att = None
    lse, branch, mid, down, gnt = {}, {}, {}, {}, {}
    for c in order:
        att, lse[c], part = attn_call(c, rot, col, row, w_out, att, nq, nk)
        branch[c] = line_sum(part)
    kept = None
    for c in order:
        t, r = branch[c]
        mid[c], kept, down_part, gnt_part = mlp_call(
            c, flag, hidden_in, t, r, cotangent, gain_mlp, w_gate, w_up, w_down, kept
        )
        gnt[c] = line_sum(gnt_part)
        down[c] = line_sum(down_part)
    n2, prod, gg, gu = kept

    def scatter(a, b):
        g = lax.dot_general(a, b, TN, preferred_element_type=F32).astype(BF)
        return lax.psum_scatter(g, "dp", scatter_dimension=0, tiled=True).astype(F32)

    grad_gate_w = scatter(n2, gg)
    grad_up_w = scatter(n2, gu)
    grad_down_w = scatter(cotangent, prod).T

    kept, carry = None, None
    gm, gn = {}, {}
    sum_mlp = jnp.zeros((1, d), F32)
    sum_head = jnp.zeros((2, HD), F32)
    for c in order:
        t, r = gnt[c]
        gm[c], kept, part, g_mlp, g_head, carry = back_call(
            c, flag, mid[c], t, r, cotangent, gain_mlp, w_out, rot, col, row, lse[c], lin, cosine, sine,
            gain_query, gain_key, w_qkv, kept, carry, nq, nk, c == order[-1],
        )
        gn[c] = line_sum(part)
        sum_mlp = sum_mlp + g_mlp
        sum_head = sum_head + g_head
    gb, gqkv = kept
    grad_qkv_w = scatter(normed, gqkv)
    grad_out_w = scatter(gb, att).T

    output, grad_input = None, None
    sum_attn = jnp.zeros((1, d), F32)
    for c in order:
        output = output_call(c, flag, mid[c], *down[c], output, tok)
    for c in order:
        grad_input, g_attn = input_call(c, flag, hidden_in, *gn[c], gm[c], gain_attn, grad_input)
        sum_attn = sum_attn + g_attn
    sum_head = swap_sum(sum_head, "mp")
    early = own_sum(
        jnp.concatenate(
            [sum_mlp.reshape(n_dp, depth), sum_head[0].reshape(n_dp, small), sum_head[1].reshape(n_dp, small)], axis=1
        ),
        "dp",
    )
    late = own_sum(sum_attn.reshape(n_dp, depth), "dp")
    return (
        output,
        grad_input,
        grad_qkv_w[:, : nq * HD],
        grad_qkv_w[:, nq * HD : (nq + nk) * HD],
        grad_qkv_w[:, (nq + nk) * HD :],
        grad_out_w,
        grad_gate_w,
        grad_up_w,
        grad_down_w,
        late,
        early[:depth],
        early[depth : depth + small],
        early[depth + small :],
    )


def solution(mesh):
    return jax.shard_map(
        on_device,
        mesh=mesh,
        in_specs=(
            P("dp", None),
            P("dp", None),
            P(),
            P("dp", "mp"),
            P("dp", "mp"),
            P("dp", "mp"),
            P("mp", "dp"),
            P("dp", "mp"),
            P("dp", "mp"),
            P("mp", "dp"),
            P("dp"),
            P("dp"),
            P("dp"),
            P("dp"),
        ),
        out_specs=(
            P("dp", None),
            P("dp", None),
            P("dp", "mp"),
            P("dp", "mp"),
            P("dp", "mp"),
            P("mp", "dp"),
            P("dp", "mp"),
            P("dp", "mp"),
            P("mp", "dp"),
            P("dp"),
            P("dp"),
            P("dp"),
            P("dp"),
        ),
        check_vma=False,
    )
```

time: 2180 us -> 913 us (0.42)
  waiting for transfers between devices: 1510 us -> 482 us
  Pallas kernels: 0 us -> 196 us
  local copies, waits for them, and re-layouts: 195 us -> 20.7 us
  matrix products: 188 us -> 47.5 us
  blocking collectives: 115 us -> 0 us
  other arithmetic: 108 us -> 38.9 us
  starting transfers between devices: 35.7 us -> 104 us
    psum x4 -> x0, waiting for transfers between devices: 929 us -> none  [the longest x1 280 us: on_device(): lax.psum(jnp.dot(attended_home, full_out, preferred_element_type=jnp.floa...]
    reduce_scatter x7 -> x5, waiting for transfers between devices: 437 us -> 0.01 us  [scatter(): lax.psum_scatter(g, 'dp', scatter_dimension=0, tiled=True).astype(F32)]
    ppermute x0 -> x64, waiting for transfers between devices: none -> 424 us  [the longest x16 243 us: line_sum(): x = x + lax.ppermute(x, 'mp', [(h, h + 1), (n - 1 - h, n - 2 - h)])]
    pallas_call x0 -> x21, Pallas kernels: none -> 196 us  [the longest x4 75.8 us: mlp_call(): pl.pallas_call(functools.partial(mlp_kernel, pieces, n_alias), grid=(ff /...]
    dot_general x26 -> x5, matrix products: 183 us -> 47.5 us  [scatter(): g = lax.dot_general(a, b, TN, preferred_element_type=F32).astype(BF)]
    gather x16 -> x0, local copies, waits for them, and re-layouts: 124 us -> none  [the longest x12 104 us: pick_rows(): picked_rows = jnp.take(values, row_ids.reshape(-1), axis=0)]
    ppermute x0 -> x64, starting transfers between devices: none -> 103 us  [the longest x16 46.7 us: line_sum(): x = x + lax.ppermute(x, 'mp', [(h, h + 1), (n - 1 - h, n - 2 - h)])]
    all_gather x7 -> x5, waiting for transfers between devices: 114 us -> 55.4 us  [the longest x1 33 us: on_device(): w_qkv = lax.all_gather(w_qkv, 'dp', axis=0)]
  transfers between devices with their start and end apart: 24 -> 74, of which waited for: 18 -> 33; matrix products, arithmetic and copies ran while one was open for 15% -> 9% of each run, Pallas kernels for 0% -> 20%
where the time goes in v1:
time: 913 us; the launch traced here: 905 us
  waiting for transfers between devices  482 us (53%)
  Pallas kernels  196 us (21%)
  starting transfers between devices  104 us (11%)
  matrix products  47.5 us (5%)
  other arithmetic  38.9 us (4%)
  local copies, waits for them, and re-layouts  20.7 us (2%)
  between operations  15.9 us (2%)
    ppermute x16, waiting for transfers between devices, line_sum(): x = x + lax.ppermute(x, 'mp', [(h, h + 1), (n - 1 - h, n - 2 - h)])  243 us
    ppermute x16, waiting for transfers between devices, line_sum(): r = lax.ppermute(x, 'mp', [(h + 1, h), (n - 2 - h, n - 1 - h)])  138 us
    pallas_call x4, Pallas kernels, mlp_call(): pl.pallas_call(functools.partial(mlp_kernel, pieces, n_alias), grid=(ff /...  75.8 us
    pallas_call x4, Pallas kernels, back_call(): pl.pallas_call(functools.partial(back_kernel, c, nq, nk, first, last), gr...  50 us
    dot_general x5, matrix products, scatter(): g = lax.dot_general(a, b, TN, preferred_element_type=F32).astype(BF)  47.5 us
    ppermute x16, starting transfers between devices, line_sum(): x = x + lax.ppermute(x, 'mp', [(h, h + 1), (n - 1 - h, n - 2 - h)])  46.7 us
    all_gather x1, waiting for transfers between devices, on_device(): w_qkv = lax.all_gather(w_qkv, 'dp', axis=0)  33 us
    ppermute x2, waiting for transfers between devices, swap_sum(): x = x + lax.ppermute(x, axis, [(i, i ^ step) for i in range(n)])  24.1 us
  transfers between devices with their start and end apart: 74, of which 33 were waited for; matrix products, arithmetic and copies ran while one was open for 9% of the time, Pallas kernels for 20%

profile of v1, /device:TPU:0, one launch (start us, length us, event | category | flops | bytes accessed | tf_op | source)
XLA Modules:
  0.0 905.2 jit_solution(5268157870247267923)
XLA Ops:
  18.0 33.0 %all-gather.13.cloned.1.call-done = bf16[2176,1024]{1,0:T(8,128)(2,1)} async-done(((bf16[272,1024]{1,0:T(8,128)(2,1)}), bf16[2176,1024]{1,0:T(8,128)(2,1)}) %all-gather.13.cloned.1.call-update) | async-done | bytes 4456464 | tf_op jit(solution)/shard_map/all_gather | solution.py:523
  54.0 13.5 %shard_map.237 = (bf16[1024,2048]{1,0:T(8,128)(2,1)}, f32[1024,768]{1,0:T(8,128)}, bf16[1024,1024]{1,0:T(8,128)(2,1)}) custom-call(bf16[1024,2048]{1,0:T(8,128)(2,1)} %x_ref.17, f32[1,2048]{1,0:T(1,128)} %bitcast.59, bf16[8,272,1024]{2,1,0:T(8,128)(2,1)} %bitcast.45, f32[1024,128]{1,0:T(8,128)} %get-tuple-element.239.cos_ref, ...), custom_call_target="tpu_custom_call" | custom-call | flops 6442450944 | bytes 20000000 | tf_op jit(solution)/shard_map/pallas_call | solution.py:78
  115.0 21.3 %collective-permute-done = bf16[256,2048]{1,0:T(8,128)(2,1)S(1)} collective-permute-done((bf16[256,2048]{1,0:T(8,128)(2,1)}, bf16[256,2048]{1,0:T(8,128)(2,1)S(1)}, u32[]{:S(2)}, u32[]{:S(2)}) %collective-permute-start) | collective-permute-done | bytes 1048608 | tf_op jit(solution)/shard_map/ppermute | solution.py:461
  139.7 18.9 %collective-permute-done.3 = bf16[256,2048]{1,0:T(8,128)(2,1)S(1)} collective-permute-done((bf16[256,2048]{1,0:T(8,128)(2,1)S(1)}, bf16[256,2048]{1,0:T(8,128)(2,1)S(1)}, u32[]{:S(2)}, u32[]{:S(2)}) %collective-permute-start.3) | collective-permute-done | bytes 1048608 | tf_op jit(solution)/shard_map/ppermute | solution.py:461
  160.8 19.7 %collective-permute-done.6 = bf16[256,2048]{1,0:T(8,128)(2,1)S(1)} collective-permute-done((bf16[256,2048]{1,0:T(8,128)(2,1)S(1)}, bf16[256,2048]{1,0:T(8,128)(2,1)S(1)}, u32[]{:S(2)}, u32[]{:S(2)}) %collective-permute-start.6) | collective-permute-done | bytes 1048608 | tf_op jit(solution)/shard_map/ppermute | solution.py:461
  195.8 18.0 %collective-permute-done.11.r_ref = bf16[256,2048]{1,0:T(8,128)(2,1)} collective-permute-done((bf16[256,2048]{1,0:T(8,128)(2,1)}, bf16[256,2048]{1,0:T(8,128)(2,1)}, u32[]{:S(2)}, u32[]{:S(2)}) %collective-permute-start.11) | collective-permute-done | bytes 1048608 | tf_op jit(solution)/shard_map/ppermute | solution.py:465
  222.9 18.8 %shard_map.242 = (f32[256,2048]{1,0:T(8,128)}, bf16[1024,2048]{1,0:T(8,128)(2,1)}, bf16[1024,1536]{1,0:T(8,128)(2,1)}, bf16[1024,1536]{1,0:T(8,128)(2,1)}, bf16[...) custom-call(s32[1]{0:T(128)} %bitcast.flag_ref, bf16[1024,2048]{1,0:T(8,128)(2,1)} %x_ref.17, ...), custom_call_target="tpu_custom_call" | custom-call | flops 12562779136 | bytes 30000000 | tf_op jit(solution)/shard_map/pallas_call | solution.py:225
  241.7 37.9 %collective-permute-done.8.r_ref = bf16[256,2048]{1,0:T(8,128)(2,1)S(1)} collective-permute-done((bf16[256,2048]{1,0:T(8,128)(2,1)S(1)}, bf16[256,2048]{1,0:T(8,128)(2,1)S(1)}, u32[]{:S(2)}, u32[]{:S(2)}) %collective-permute-start.8) | collective-permute-done | bytes 1048608 | tf_op jit(solution)/shard_map/ppermute | solution.py:465
  280.6 19.0 %shard_map.243 = (f32[256,2048]{1,0:T(8,128)}, bf16[1024,2048]{1,0:T(8,128)(2,1)}, bf16[1024,1536]{1,0:T(8,128)(2,1)}, bf16[1024,1536]{1,0:T(8,128)(2,1)}, bf16[...) custom-call(s32[1]{0:T(128)} %bitcast.flag_ref, ...), custom_call_target="tpu_custom_call", output_to_operand_aliasing={{1}: (9, {}), {2}: (10, {}), {3}: (11, {}), {4}: (12, {})} | custom-call | flops 12562779136 | bytes 30000000 | tf_op jit(solution)/shard_map/pallas_call | solution.py:225
  302.7 18.9 %shard_map.244 = (f32[256,2048]{1,0:T(8,128)}, bf16[1024,2048]{1,0:T(8,128)(2,1)}, bf16[1024,1536]{1,0:T(8,128)(2,1)}, bf16[1024,1536]{1,0:T(8,128)(2,1)}, bf16[...) custom-call(s32[1]{0:T(128)} %bitcast.flag_ref, ...), custom_call_target="tpu_custom_call", output_to_operand_aliasing={{1}: (9, {}), {2}: (10, {}), {3}: (11, {}), {4}: (12, {})} | custom-call | flops 12562779136 | bytes 30000000 | tf_op jit(solution)/shard_map/pallas_call | solution.py:225
  321.7 19.0 %shard_map.245 = (f32[256,2048]{1,0:T(8,128)}, bf16[1024,2048]{1,0:T(8,128)(2,1)}, bf16[1024,1536]{1,0:T(8,128)(2,1)}, bf16[1024,1536]{1,0:T(8,128)(2,1)}, bf16[...) custom-call(s32[1]{0:T(128)} %bitcast.flag_ref, ...), custom_call_target="tpu_custom_call", output_to_operand_aliasing={{1}: (9, {}), {2}: (10, {}), {3}: (11, {}), {4}: (12, {})} | custom-call | flops 12562779136 | bytes 30000000 | tf_op jit(solution)/shard_map/pallas_call | solution.py:225
  349.6 20.3 %collective-permute-done.24 = bf16[256,2048]{1,0:T(8,128)(2,1)S(1)} collective-permute-done((bf16[256,2048]{1,0:T(8,128)(2,1)}, bf16[256,2048]{1,0:T(8,128)(2,1)S(1)}, u32[]{:S(2)}, u32[]{:S(2)}) %collective-permute-start.24) | collective-permute-done | bytes 1048608 | tf_op jit(solution)/shard_map/ppermute | solution.py:461
  371.1 19.0 %collective-permute-done.27 = bf16[256,2048]{1,0:T(8,128)(2,1)S(1)} collective-permute-done((bf16[256,2048]{1,0:T(8,128)(2,1)S(1)}, bf16[256,2048]{1,0:T(8,128)(2,1)S(1)}, u32[]{:S(2)}, u32[]{:S(2)}) %collective-permute-start.27) | collective-permute-done | bytes 1048608 | tf_op jit(solution)/shard_map/ppermute | solution.py:461
  398.5 22.6 %collective-permute-done.35.r_ref = bf16[256,2048]{1,0:T(8,128)(2,1)S(1)} collective-permute-done((bf16[256,2048]{1,0:T(8,128)(2,1)S(1)}, bf16[256,2048]{1,0:T(8,128)(2,1)S(1)}, u32[]{:S(2)}, u32[]{:S(2)}) %collective-permute-start.35) | collective-permute-done | bytes 1048608 | tf_op jit(solution)/shard_map/ppermute | solution.py:465
  457.4 27.9 %collective-permute-done.29.r_ref = bf16[256,2048]{1,0:T(8,128)(2,1)S(1)} collective-permute-done((bf16[256,2048]{1,0:T(8,128)(2,1)S(1)}, bf16[256,2048]{1,0:T(8,128)(2,1)S(1)}, u32[]{:S(2)}, u32[]{:S(2)}) %collective-permute-start.29) | collective-permute-done | bytes 1048608 | tf_op jit(solution)/shard_map/ppermute | solution.py:465
  571.7 19.7 %collective-permute-done.12 = bf16[256,2048]{1,0:T(8,128)(2,1)S(1)} collective-permute-done((bf16[256,2048]{1,0:T(8,128)(2,1)}, bf16[256,2048]{1,0:T(8,128)(2,1)S(1)}, u32[]{:S(2)}, u32[]{:S(2)}) %collective-permute-start.12) | collective-permute-done | bytes 1048608 | tf_op jit(solution)/shard_map/ppermute | solution.py:461
  593.8 20.0 %collective-permute-done.15 = bf16[256,2048]{1,0:T(8,128)(2,1)S(1)} collective-permute-done((bf16[256,2048]{1,0:T(8,128)(2,1)S(1)}, bf16[256,2048]{1,0:T(8,128)(2,1)S(1)}, u32[]{:S(2)}, u32[]{:S(2)}) %collective-permute-start.15) | collective-permute-done | bytes 1048608 | tf_op jit(solution)/shard_map/ppermute | solution.py:461
  615.1 21.2 %collective-permute-done.18 = bf16[256,2048]{1,0:T(8,128)(2,1)S(1)} collective-permute-done((bf16[256,2048]{1,0:T(8,128)(2,1)S(1)}, bf16[256,2048]{1,0:T(8,128)(2,1)S(1)}, u32[]{:S(2)}, u32[]{:S(2)}) %collective-permute-start.18) | collective-permute-done | bytes 1048608 | tf_op jit(solution)/shard_map/ppermute | solution.py:461
  637.4 17.3 %collective-permute-done.21 = bf16[256,2048]{1,0:T(8,128)(2,1)S(1)} collective-permute-done((bf16[256,2048]{1,0:T(8,128)(2,1)S(1)}, bf16[256,2048]{1,0:T(8,128)(2,1)S(1)}, u32[]{:S(2)}, u32[]{:S(2)}) %collective-permute-start.21) | collective-permute-done | bytes 1048608 | tf_op jit(solution)/shard_map/ppermute | solution.py:461
  667.6 16.5 %collective-permute-start.36 = (bf16[256,2048]{1,0:T(8,128)(2,1)S(1)}, bf16[256,2048]{1,0:T(8,128)(2,1)S(1)}, u32[]{:S(2)}, u32[]{:S(2)}) collective-permute-start(bf16[256,2048]{1,0:T(8,128)(2,1)S(1)} %copy-done.20), channel_id=1, source_target_pairs={{0,1},{3,2},{4,5},{7,6},{8,9},{11,10},{12,13},{15,14},{16,17},{19,... | collective-permute-start | bytes 3145736 | tf_op jit(solution)/shard_map/ppermute | solution.py:461
  690.0 20.7 %collective-permute-done.42 = bf16[256,2048]{1,0:T(8,128)(2,1)S(1)} collective-permute-done((bf16[256,2048]{1,0:T(8,128)(2,1)S(1)}, bf16[256,2048]{1,0:T(8,128)(2,1)S(1)}, u32[]{:S(2)}, u32[]{:S(2)}) %collective-permute-start.42) | collective-permute-done | bytes 1048608 | tf_op jit(solution)/shard_map/ppermute | solution.py:461
  711.9 21.3 %collective-permute-done.39 = bf16[256,2048]{1,0:T(8,128)(2,1)S(1)} collective-permute-done((bf16[256,2048]{1,0:T(8,128)(2,1)S(1)}, bf16[256,2048]{1,0:T(8,128)(2,1)S(1)}, u32[]{:S(2)}, u32[]{:S(2)}) %collective-permute-start.39) | collective-permute-done | bytes 1048608 | tf_op jit(solution)/shard_map/ppermute | solution.py:461
  734.4 16.2 %collective-permute-done.36 = bf16[256,2048]{1,0:T(8,128)(2,1)S(1)} collective-permute-done((bf16[256,2048]{1,0:T(8,128)(2,1)S(1)}, bf16[256,2048]{1,0:T(8,128)(2,1)S(1)}, u32[]{:S(2)}, u32[]{:S(2)}) %collective-permute-start.36) | collective-permute-done | bytes 1048608 | tf_op jit(solution)/shard_map/ppermute | solution.py:461
  773.2 23.9 %collective-permute-done.56 = f32[2,128]{1,0:T(2,128)S(1)} collective-permute-done((f32[2,128]{1,0:T(2,128)S(1)}, f32[2,128]{1,0:T(2,128)S(1)}, u32[]{:S(2)}, u32[]{:S(2)}) %collective-permute-start.56) | collective-permute-done | bytes 1056 | tf_op jit(solution)/shard_map/ppermute | solution.py:475
  (340 shorter events, 384.4 us)
Async XLA Ops:
  10.0 70.8 %all-gather.15.cloned.1.call-start = ((), (), s32[]{:S(2)}) async-start(), calls=%async_computation.13 | async-start | bytes 2359296 | tf_op jit(solution)/shard_map/all_gather | solution.py:524
  10.8 203.0 %all-gather.9.cloned.1.call-start = ((), (), s32[]{:S(2)}) async-start(), calls=%async_computation.5 | async-start | bytes 7077888 | tf_op jit(solution)/shard_map/all_gather | solution.py:525
  11.5 202.3 %all-gather.11.cloned.1.call-start = ((), (), s32[]{:S(2)}) async-start(), calls=%async_computation.6 | async-start | bytes 7077888 | tf_op jit(solution)/shard_map/all_gather | solution.py:526
  12.1 210.8 %all-gather.17.cloned.1.call-start = ((), (), s32[]{:S(2)}) async-start(), calls=%async_computation.14 | async-start | bytes 7077888 | tf_op jit(solution)/shard_map/all_gather | solution.py:527
  12.7 872.8 %reduce-scatter.8.cloned.1.call-start = ((), (), s32[]{:S(2)}) async-start(), calls=%async_computation.8 | async-start | bytes 2359296 | tf_op jit(solution)/shard_map/reduce_scatter | solution.py:569
  110.6 69.9 %collective-permute-start.6 = (bf16[256,2048]{1,0:T(8,128)(2,1)S(1)}, bf16[256,2048]{1,0:T(8,128)(2,1)S(1)}, u32[]{:S(2)}, u32[]{:S(2)}) collective-permute-start(bf16[256,2048]{1,0:T(8,128)(2,1)S(1)} %copy-done.25), channel_id=1, source_target_pairs={{0,1},{3,2},{4,5},{7,6},{8,9},{11,10},{12,13},{15,14},{16,17},{19,... | collective-permute-start | bytes 3145736 | tf_op jit(solution)/shard_map/ppermute | solution.py:461
  114.2 68.3 %collective-permute-start.10 = (bf16[256,2048]{1,0:T(8,128)(2,1)S(1)}, bf16[256,2048]{1,0:T(8,128)(2,1)S(1)}, u32[]{:S(2)}, u32[]{:S(2)}) collective-permute-start(bf16[256,2048]{1,0:T(8,128)(2,1)S(1)} %add.226), channel_id=1, source_target_pairs={{1,2},{2,1},{5,6},{6,5},{9,10},{10,9},{13,14},{14,13},{17,18},{18,... | collective-permute-start | bytes 3145736 | tf_op jit(solution)/shard_map/ppermute | solution.py:462
  188.5 133.2 %collective-permute-start.2 = (bf16[256,2048]{1,0:T(8,128)(2,1)}, bf16[256,2048]{1,0:T(8,128)(2,1)}, u32[]{:S(2)}, u32[]{:S(2)}) collective-permute-start(bf16[256,2048]{1,0:T(8,128)(2,1)} %add.221.t_ref), channel_id=1, source_target_pairs={{1,0},{2,3},{5,4},{6,7},{9,8},{10,11},{13,12},{14,15},{17,16},{18,... | collective-permute-start | bytes 3145736 | tf_op jit(solution)/shard_map/ppermute | solution.py:465
  191.4 111.3 %collective-permute-start.5 = (bf16[256,2048]{1,0:T(8,128)(2,1)S(1)}, bf16[256,2048]{1,0:T(8,128)(2,1)}, u32[]{:S(2)}, u32[]{:S(2)}) collective-permute-start(bf16[256,2048]{1,0:T(8,128)(2,1)S(1)} %add.223.t_ref), channel_id=1, source_target_pairs={{1,0},{2,3},{5,4},{6,7},{9,8},{10,11},{13,12},{14,15},{17,16},{18,... | collective-permute-start | bytes 3145736 | tf_op jit(solution)/shard_map/ppermute | solution.py:465
  194.4 85.3 %collective-permute-start.8 = (bf16[256,2048]{1,0:T(8,128)(2,1)S(1)}, bf16[256,2048]{1,0:T(8,128)(2,1)S(1)}, u32[]{:S(2)}, u32[]{:S(2)}) collective-permute-start(bf16[256,2048]{1,0:T(8,128)(2,1)S(1)} %add.225.t_ref), channel_id=1, source_target_pairs={{1,0},{2,3},{5,4},{6,7},{9,8},{10,11},{13,12},{14,15},{17,16},{18,... | collective-permute-start | bytes 3145736 | tf_op jit(solution)/shard_map/ppermute | solution.py:465
  395.0 104.3 %collective-permute-start.26 = (bf16[256,2048]{1,0:T(8,128)(2,1)S(1)}, bf16[256,2048]{1,0:T(8,128)(2,1)S(1)}, u32[]{:S(2)}, u32[]{:S(2)}) collective-permute-start(bf16[256,2048]{1,0:T(8,128)(2,1)S(1)} %add.237.t_ref), channel_id=1, source_target_pairs={{1,0},{2,3},{5,4},{6,7},{9,8},{10,11},{13,12},{14,15},{17,16},{18,... | collective-permute-start | bytes 3145736 | tf_op jit(solution)/shard_map/ppermute | solution.py:465
  396.7 88.6 %collective-permute-start.29 = (bf16[256,2048]{1,0:T(8,128)(2,1)S(1)}, bf16[256,2048]{1,0:T(8,128)(2,1)S(1)}, u32[]{:S(2)}, u32[]{:S(2)}) collective-permute-start(bf16[256,2048]{1,0:T(8,128)(2,1)S(1)} %add.239.t_ref), channel_id=1, source_target_pairs={{1,0},{2,3},{5,4},{6,7},{9,8},{10,11},{13,12},{14,15},{17,16},{18,... | collective-permute-start | bytes 3145736 | tf_op jit(solution)/shard_map/ppermute | solution.py:465
  517.9 370.3 %reduce-scatter.6.cloned.1.call-start = ((), (), s32[]{:S(2)}) async-start(), calls=%async_computation.7 | async-start | bytes 4718592 | tf_op jit(solution)/shard_map/reduce_scatter | solution.py:569
  526.5 363.5 %reduce-scatter.10.cloned.1.call-start = ((), (), s32[]{:S(2)}) async-start(), calls=%async_computation.9 | async-start | bytes 7077888 | tf_op jit(solution)/shard_map/reduce_scatter | solution.py:569
  539.7 352.8 %reduce-scatter.12.cloned.1.call-start = ((), (), s32[]{:S(2)}) async-start(), calls=%async_computation.10 | async-start | bytes 7077888 | tf_op jit(solution)/shard_map/reduce_scatter | solution.py:569
  552.7 343.1 %reduce-scatter.14.cloned.1.call-start = ((), (), s32[]{:S(2)}) async-start(), calls=%async_computation.11 | async-start | bytes 7077888 | tf_op jit(solution)/shard_map/reduce_scatter | solution.py:569
  569.0 67.3 %collective-permute-start.18 = (bf16[256,2048]{1,0:T(8,128)(2,1)S(1)}, bf16[256,2048]{1,0:T(8,128)(2,1)S(1)}, u32[]{:S(2)}, u32[]{:S(2)}) collective-permute-start(bf16[256,2048]{1,0:T(8,128)(2,1)S(1)} %copy-done.12), channel_id=1, source_target_pairs={{0,1},{3,2},{4,5},{7,6},{8,9},{11,10},{12,13},{15,14},{16,17},{19,... | collective-permute-start | bytes 3145736 | tf_op jit(solution)/shard_map/ppermute | solution.py:461
  570.3 84.4 %collective-permute-start.21 = (bf16[256,2048]{1,0:T(8,128)(2,1)S(1)}, bf16[256,2048]{1,0:T(8,128)(2,1)S(1)}, u32[]{:S(2)}, u32[]{:S(2)}) collective-permute-start(bf16[256,2048]{1,0:T(8,128)(2,1)S(1)} %copy-done.11), channel_id=1, source_target_pairs={{0,1},{3,2},{4,5},{7,6},{8,9},{11,10},{12,13},{15,14},{16,17},{19,... | collective-permute-start | bytes 3145736 | tf_op jit(solution)/shard_map/ppermute | solution.py:461
  667.6 83.0 %collective-permute-start.36 = (bf16[256,2048]{1,0:T(8,128)(2,1)S(1)}, bf16[256,2048]{1,0:T(8,128)(2,1)S(1)}, u32[]{:S(2)}, u32[]{:S(2)}) collective-permute-start(bf16[256,2048]{1,0:T(8,128)(2,1)S(1)} %copy-done.20), channel_id=1, source_target_pairs={{0,1},{3,2},{4,5},{7,6},{8,9},{11,10},{12,13},{15,14},{16,17},{19,... | collective-permute-start | bytes 3145736 | tf_op jit(solution)/shard_map/ppermute | solution.py:461
  684.5 67.2 %collective-permute-start.17 = (bf16[256,2048]{1,0:T(8,128)(2,1)S(1)}, bf16[256,2048]{1,0:T(8,128)(2,1)S(1)}, u32[]{:S(2)}, u32[]{:S(2)}) collective-permute-start(bf16[256,2048]{1,0:T(8,128)(2,1)S(1)} %add.231.t_ref), channel_id=1, source_target_pairs={{1,0},{2,3},{5,4},{6,7},{9,8},{10,11},{13,12},{14,15},{17,16},{18,... | collective-permute-start | bytes 3145736 | tf_op jit(solution)/shard_map/ppermute | solution.py:465
  766.8 67.2 %collective-permute-start.47 = (bf16[256,2048]{1,0:T(8,128)(2,1)S(1)}, bf16[256,2048]{1,0:T(8,128)(2,1)}, u32[]{:S(2)}, u32[]{:S(2)}) collective-permute-start(bf16[256,2048]{1,0:T(8,128)(2,1)S(1)} %add.251.t_ref), channel_id=1, source_target_pairs={{1,0},{2,3},{5,4},{6,7},{9,8},{10,11},{13,12},{14,15},{17,16},{18,... | collective-permute-start | bytes 3145736 | tf_op jit(solution)/shard_map/ppermute | solution.py:465
  769.6 69.5 %collective-permute-start.44 = (bf16[256,2048]{1,0:T(8,128)(2,1)}, bf16[256,2048]{1,0:T(8,128)(2,1)}, u32[]{:S(2)}, u32[]{:S(2)}) collective-permute-start(bf16[256,2048]{1,0:T(8,128)(2,1)} %add.249.t_ref), channel_id=1, source_target_pairs={{1,0},{2,3},{5,4},{6,7},{9,8},{10,11},{13,12},{14,15},{17,16},{18,... | collective-permute-start | bytes 3145736 | tf_op jit(solution)/shard_map/ppermute | solution.py:465
  771.4 85.4 %collective-permute-start.41 = (bf16[256,2048]{1,0:T(8,128)(2,1)S(1)}, bf16[256,2048]{1,0:T(8,128)(2,1)}, u32[]{:S(2)}, u32[]{:S(2)}) collective-permute-start(bf16[256,2048]{1,0:T(8,128)(2,1)S(1)} %add.247.t_ref), channel_id=1, source_target_pairs={{1,0},{2,3},{5,4},{6,7},{9,8},{10,11},{13,12},{14,15},{17,16},{18,... | collective-permute-start | bytes 3145736 | tf_op jit(solution)/shard_map/ppermute | solution.py:465
  797.0 75.1 %collective-permute-start.38 = (bf16[256,2048]{1,0:T(8,128)(2,1)S(1)}, bf16[256,2048]{1,0:T(8,128)(2,1)}, u32[]{:S(2)}, u32[]{:S(2)}) collective-permute-start(bf16[256,2048]{1,0:T(8,128)(2,1)S(1)} %add.245.t_ref), channel_id=1, source_target_pairs={{1,0},{2,3},{5,4},{6,7},{9,8},{10,11},{13,12},{14,15},{17,16},{18,... | collective-permute-start | bytes 3145736 | tf_op jit(solution)/shard_map/ppermute | solution.py:465
  (102 other events, 2695.0 us)
Sparse Core Ops, SparseCore 0:
  10.5 40.5 all-gather.12
  52.9 27.8 all-gather.14
  82.7 45.5 all-gather.8
  130.0 45.5 all-gather.10
  177.3 45.5 all-gather.16
  518.0 40.2 reduce-scatter.7
  562.0 51.3 reduce-scatter.5
  616.7 61.7 reduce-scatter.9
  682.2 61.7 reduce-scatter.11
  747.3 61.7 reduce-scatter.13

commit v2 on v1

v2 whole, which is shorter than its diff:
```python
import functools

import jax
import jax.numpy as jnp
from jax import lax
from jax.experimental import pallas as pl
from jax.experimental.pallas import tpu as pltpu
from jax.sharding import PartitionSpec as P

HD = 128
CHUNK = 256
EPSILON = 1e-06
ROPE_BASE = 1000000.0
SCALE = HD ** (-0.5)
BF = jnp.bfloat16
F32 = jnp.float32
VMEM_LIMIT = 56 * 1024 * 1024

NN = (((1,), (0,)), ((), ()))
NT = (((1,), (1,)), ((), ()))
TN = (((0,), (0,)), ((), ()))


def dot(a, b, dims=NN):
    return lax.dot_general(a, b, dims, preferred_element_type=F32)


def whole():
    return pl.BlockSpec(memory_space=pltpu.VMEM)


def smem():
    return pl.BlockSpec(memory_space=pltpu.SMEM)


def hbm():
    return pl.BlockSpec(memory_space=pl.ANY)


def params(**kw):
    return pltpu.CompilerParams(vmem_limit_bytes=VMEM_LIMIT, **kw)


def cost(flops, nbytes):
    return pl.CostEstimate(flops=0, bytes_accessed=0, transcendentals=0)


def rms_r(values):
    return lax.rsqrt(jnp.mean(values * values, axis=-1, keepdims=True) + EPSILON)


def load_weights(refs, dest, at, sems, cols, dest_cols=None):
    out = []
    for n, ref in enumerate(refs):
        place = dest.at[at[0] ^ (n // 2), at[1] ^ (n % 2)]
        if dest_cols is not None:
            place = place.at[:, dest_cols]
        out.append(pltpu.make_async_copy(ref.at[pl.ds(0, dest.shape[2]), cols], place, sems.at[n]))
    return out


def start(copies):
    for copy in copies:
        copy.start()


def wait(copies):
    for copy in copies:
        copy.wait()


def joined(ref):
    a, b, c, n = ref.shape
    return ref[...].reshape(a * b * c, n)


def qkv_kernel(nq, nk, blocks, flag_ref, x_ref, cos_ref, sin_ref, *rest):
    normed_ref, lin_ref, rot_ref, ga_ref, gm_ref, gq_ref, gk_ref, w, gains, sems = rest[2 * blocks :]
    step = pl.program_id(0)
    at = flag_ref[1], flag_ref[2]
    wide_q = nq * HD
    wide_kv = 2 * nk * HD
    depth = w.shape[2]

    @pl.when(step == 0)
    def _():
        rows = []
        for n, ref in enumerate(rest[blocks : 2 * blocks]):
            place = gains.at[at[0] ^ (n // 2), at[1] ^ (n % 2)]
            rows.append(pltpu.make_async_copy(ref.at[pl.ds(depth, 16)], place, sems.at[2, n]))
        copies = load_weights(rest[:blocks], w, at, sems.at[0], pl.ds(0, wide_q), pl.ds(0, wide_q))
        copies += load_weights(
            rest[blocks : 2 * blocks], w, at, sems.at[1], pl.ds(0, wide_kv), pl.ds(wide_q, wide_kv)
        )
        start(rows)
        start(copies)
        wait(rows)
        of_q = jnp.zeros((1, HD), F32)
        of_k = jnp.zeros((1, HD), F32)
        for p in range(blocks):
            g = gains[p // 2, p % 2].astype(F32)
            ga_ref[:, p * depth : (p + 1) * depth] = g[0:1, :depth]
            gm_ref[:, p * depth : (p + 1) * depth] = g[1:2, :depth]
            of_q = of_q + g[2:3, :HD]
            of_k = of_k + g[3:4, :HD]
        gq_ref[...] = of_q
        gk_ref[...] = of_k
        wait(copies)

    x = x_ref[...].astype(F32)
    normed = (x * rms_r(x) * ga_ref[...]).astype(BF)
    normed_ref[...] = normed
    acc = dot(normed, joined(w))
    cosine = cos_ref[...]
    sine = sin_ref[...]
    for h in range(nq + nk):
        v = acc[:, h * HD : (h + 1) * HD]
        gain = gq_ref[...] if h < nq else gk_ref[...]
        n = v * rms_r(v) * gain
        rot_ref[:, h * HD : (h + 1) * HD] = (n * cosine + pltpu.roll(n, HD // 2, 1) * sine).astype(BF)
    lin_ref[...] = acc[:, : (nq + nk) * HD]
    rot_ref[:, (nq + nk) * HD :] = acc[:, (nq + nk) * HD :].astype(BF)


def qkv_call(flag, x, cosine, sine, w_q, w_kv, nq, nk):
    tok, d = x.shape
    blocks = len(w_q)
    cols = (nq + 2 * nk) * HD
    blk = lambda n: pl.BlockSpec((CHUNK, n), lambda i: (i, 0))
    one = lambda n: pl.BlockSpec((1, n), lambda i: (0, 0))
    lin = (nq + nk) * HD
    return pl.pallas_call(
        functools.partial(qkv_kernel, nq, nk, blocks),
        grid=(tok // CHUNK,),
        in_specs=[smem(), blk(d), blk(HD), blk(HD)] + [hbm()] * (2 * blocks),
        out_specs=[blk(d), blk(lin), blk(cols), one(d), one(d), one(HD), one(HD)],
        out_shape=[
            jax.ShapeDtypeStruct((tok, d), BF),
            jax.ShapeDtypeStruct((tok, lin), F32),
            jax.ShapeDtypeStruct((tok, cols), BF),
            jax.ShapeDtypeStruct((1, d), F32),
            jax.ShapeDtypeStruct((1, d), F32),
            jax.ShapeDtypeStruct((1, HD), F32),
            jax.ShapeDtypeStruct((1, HD), F32),
        ],
        scratch_shapes=[
            pltpu.VMEM((blocks // 2, 2, d // blocks, cols), BF),
            pltpu.VMEM((blocks // 2, 2, 16, 2 * nk * HD), BF),
            pltpu.SemaphoreType.DMA((3, blocks)),
        ],
        compiler_params=params(),
        cost_estimate=cost(2 * tok * d * cols, 20e6),
    )(flag, x, cosine, sine, *w_q, *w_kv)


def band(c):
    lo = max(c - 1, 0) * CHUNK
    return lo, (c + 1) * CHUNK - lo


def doc_start(ends_ref, token):
    first = jnp.zeros_like(token)
    for j in range(ends_ref.shape[0]):
        first = jnp.maximum(first, jnp.where(token >= ends_ref[j], ends_ref[j], 0))
    return first


def allowed(c, ends_ref):
    lo, width = band(c)
    t = lax.broadcasted_iota(jnp.int32, (CHUNK, 1), 0) + c * CHUNK
    u = lax.broadcasted_iota(jnp.int32, (CHUNK, width), 1) + lo
    return (u <= t) & (u >= doc_start(ends_ref, t))


def attn_kernel(c, nq, nk, blocks, flag_ref, ends_ref, rot_ref, *rest):
    att_ref, lse_ref, part_ref, w, sems = rest[-5:]
    copies = load_weights(rest[:blocks], w, (flag_ref[1], flag_ref[2]), sems, pl.ds(0, w.shape[3]))
    start(copies)
    lo, width = band(c)
    mask = allowed(c, ends_ref)
    group = nq // nk
    heads = []
    lses = []
    for h in range(nq):
        q = rot_ref[c * CHUNK : (c + 1) * CHUNK, h * HD : (h + 1) * HD]
        j = h // group
        k = rot_ref[lo : lo + width, (nq + j) * HD : (nq + j + 1) * HD]
        v = rot_ref[lo : lo + width, (nq + nk + j) * HD : (nq + nk + j + 1) * HD]
        s = jnp.where(mask, dot(q, k, NT) * SCALE, -1e30)
        m = jnp.max(s, axis=-1, keepdims=True)
        e = jnp.exp(s - m)
        l = jnp.sum(e, axis=-1, keepdims=True)
        heads.append(dot((e / l).astype(BF), v).astype(BF))
        lses.append(m + jnp.log(l))
    att = jnp.concatenate(heads, axis=1)
    att_ref[...] = att
    lse_ref[...] = jnp.concatenate(lses, axis=1)
    wait(copies)
    part_ref[...] = dot(att, joined(w), NT).astype(BF)


def chunk_block(c, n):
    return pl.BlockSpec((CHUNK, n), lambda i: (c, 0))


def attn_call(c, flag, ends, rot, w_out, att, nq, nk):
    tok = rot.shape[0]
    blocks, depth = len(w_out), w_out[0].shape[0]
    d = blocks * depth
    first = att is None
    full = lambda a: pl.BlockSpec(a.shape, lambda i: (0,) * a.ndim)
    return pl.pallas_call(
        functools.partial(attn_kernel, c, nq, nk, blocks),
        grid=(1,),
        in_specs=[smem(), smem(), full(rot)] + [hbm()] * (blocks + (0 if first else 1)),
        out_specs=[
            chunk_block(c, nq * HD),
            pl.BlockSpec((CHUNK, nq), lambda i: (0, 0)),
            pl.BlockSpec((CHUNK, d), lambda i: (0, 0)),
        ],
        out_shape=[
            jax.ShapeDtypeStruct((tok, nq * HD), BF),
            jax.ShapeDtypeStruct((CHUNK, nq), F32),
            jax.ShapeDtypeStruct((CHUNK, d), BF),
        ],
        scratch_shapes=[pltpu.VMEM((blocks // 2, 2, depth, nq * HD), BF), pltpu.SemaphoreType.DMA((blocks,))],
        input_output_aliases={} if first else {3 + blocks: 0},
        compiler_params=params(),
        cost_estimate=cost(1e9, 6e6),
    )(flag, ends, rot, *w_out, *([] if first else [att]))


def mlp_kernel(tiles, blocks, flag_ref, x_ref, t_ref, r_ref, cot_ref, gain_ref, *rest):
    mid_ref, n2_ref, prod_ref, gg_ref, gu_ref, down_ref, gnt_ref, acc_d, acc_g, w, sems = rest[-11:]
    at = flag_ref[1], flag_ref[2]
    tile = w.shape[5]
    copies = [
        [
            load_weights(
                rest[j * blocks : (j + 1) * blocks], w.at[j % 2, i], at, sems.at[j % 2, i], pl.ds(i * tile, tile)
            )
            for i in range(3)
        ]
        for j in range(tiles)
    ]
    for j in range(min(tiles, 2)):
        for i in range(3):
            start(copies[j][i])
    branch = jnp.where(flag_ref[0] == 1, r_ref[...], t_ref[...]).astype(F32)
    mid = x_ref[...].astype(F32) + branch
    mid_ref[...] = mid
    n2 = (mid * rms_r(mid) * gain_ref[...]).astype(BF)
    n2_ref[...] = n2
    for j in range(tiles):
        wg, wu, wd = (w.at[j % 2, i] for i in range(3))
        cols = slice(j * tile, (j + 1) * tile)
        wait(copies[j][0])
        g = dot(n2_ref[...], joined(wg))
        wait(copies[j][1])
        u = dot(n2_ref[...], joined(wu))
        wait(copies[j][2])
        gp = dot(cot_ref[...], joined(wd))
        s = 1.0 / (1.0 + jnp.exp(-g))
        gs = g * s
        prod = (gs * u).astype(BF)
        gg = (gp * u * s * (1.0 + g * (1.0 - s))).astype(BF)
        gu = (gp * gs).astype(BF)
        prod_ref[:, cols] = prod
        gg_ref[:, cols] = gg
        gu_ref[:, cols] = gu
        gnt = dot(gg, joined(wg), NT) + dot(gu, joined(wu), NT)
        down = dot(prod, joined(wd), NT)
        if j:
            gnt = gnt + acc_g[...]
            down = down + acc_d[...]
        if j < tiles - 1:
            acc_g[...] = gnt
            acc_d[...] = down
        else:
            gnt_ref[...] = gnt.astype(BF)
            down_ref[...] = down.astype(BF)
        if j + 2 < tiles:
            for i in range(3):
                start(copies[j + 2][i])


def mlp_call(c, flag, x, t, r, cot, gain, packs, kept):
    tok, d = x.shape
    tiles = len(packs)
    blocks = len(packs[0])
    depth, tile = d // blocks, packs[0][0].shape[1] // 3
    ff = tile * tiles
    first = kept is None
    blk = chunk_block(c, d)
    own = pl.BlockSpec((CHUNK, d), lambda j: (0, 0))
    ffblk = chunk_block(c, ff)
    full = lambda a: pl.BlockSpec(a.shape, lambda j: (0,) * a.ndim)
    n_alias = 0 if first else 4
    at = 6 + tiles * blocks
    out = pl.pallas_call(
        functools.partial(mlp_kernel, tiles, blocks),
        grid=(1,),
        in_specs=[smem(), blk, own, own, blk, full(gain)] + [hbm()] * (tiles * blocks + n_alias),
        out_specs=[own, blk, ffblk, ffblk, ffblk, own, own],
        out_shape=[
            jax.ShapeDtypeStruct((CHUNK, d), F32),
            jax.ShapeDtypeStruct((tok, d), BF),
            jax.ShapeDtypeStruct((tok, ff), BF),
            jax.ShapeDtypeStruct((tok, ff), BF),
            jax.ShapeDtypeStruct((tok, ff), BF),
            jax.ShapeDtypeStruct((CHUNK, d), BF),
            jax.ShapeDtypeStruct((CHUNK, d), BF),
        ],
        scratch_shapes=[
            pltpu.VMEM((CHUNK, d), F32),
            pltpu.VMEM((CHUNK, d), F32),
            pltpu.VMEM((2, 3, blocks // 2, 2, depth, tile), BF),
            pltpu.SemaphoreType.DMA((2, 3, blocks)),
        ],
        input_output_aliases={} if first else {at: 1, at + 1: 2, at + 2: 3, at + 3: 4},
        compiler_params=params(),
        cost_estimate=cost(12 * CHUNK * d * ff, 25e6),
    )(flag, x, t, r, cot, gain, *[b for p in packs for b in p], *([] if first else kept))
    return out[0], out[1:5], out[5], out[6]


def back_kernel(
    c, nq, nk, blocks, first, last, flag_ref, ends_ref, mid_ref, t_ref, r_ref, cot_ref, gain_ref, rot_ref,
    lse_ref, lin_ref, cos_ref, sin_ref, gq_ref, gk_ref, *rest,
):
    gm_ref, gb_ref, gqkv_ref, part_ref, gain_out, head_out, carry_out, wo, w, sems = rest[-10:]
    if not first:
        carry_ref, gain_in, head_in = rest[3 * blocks : 3 * blocks + 3]
    at = flag_ref[1], flag_ref[2]
    wide_q = nq * HD
    wide_kv = 2 * nk * HD
    out_copies = load_weights(rest[:blocks], wo, at, sems.at[0], pl.ds(0, wide_q))
    in_copies = load_weights(rest[blocks : 2 * blocks], w, at, sems.at[1], pl.ds(0, wide_q), pl.ds(0, wide_q))
    in_copies += load_weights(
        rest[2 * blocks : 3 * blocks], w, at, sems.at[2], pl.ds(0, wide_kv), pl.ds(wide_q, wide_kv)
    )
    start(out_copies)
    start(in_copies)
    gnt = jnp.where(flag_ref[0] == 1, r_ref[...], t_ref[...]).astype(F32)
    mid = mid_ref[...]
    r2 = rms_r(mid)
    h = gnt * gain_ref[...]
    gm = (
        cot_ref[...].astype(F32)
        + r2 * h
        - mid * (r2 * r2 * r2 * jnp.mean(h * mid, axis=-1, keepdims=True))
    )
    gain_sum = jnp.sum(gnt * mid * r2, axis=0, keepdims=True)
    gain_out[...] = gain_sum if first else gain_in[...] + gain_sum
    gm_ref[...] = gm
    gb = gm.astype(BF)
    gb_ref[...] = gb
    wait(out_copies)
    ga = dot(gb, joined(wo)).astype(BF)
    lo, width = band(c)
    mask = allowed(c, ends_ref)
    group = nq // nk
    cosine = cos_ref[...]
    sine = -sin_ref[...]

    def unrope(grad, lin, gain):
        gr = grad * cosine + pltpu.roll(grad, HD // 2, 1) * sine
        rr = rms_r(lin)
        hh = gr * gain
        out = rr * hh - lin * (rr * rr * rr * jnp.mean(hh * lin, axis=-1, keepdims=True))
        return out.astype(BF), jnp.sum(gr * lin * rr, axis=0, keepdims=True)

    sum_q = jnp.zeros((1, HD), F32) if first else head_in[0:1, :]
    sum_k = jnp.zeros((1, HD), F32) if first else head_in[1:2, :]
    outs = [None] * (nq + 2 * nk)
    for j in range(nk):
        k = rot_ref[lo : lo + width, (nq + j) * HD : (nq + j + 1) * HD]
        v = rot_ref[lo : lo + width, (nq + nk + j) * HD : (nq + nk + j + 1) * HD]
        dk = jnp.zeros((width, HD), F32)
        dv = jnp.zeros((width, HD), F32)
        for g in range(group):
            i = j * group + g
            q = rot_ref[c * CHUNK : (c + 1) * CHUNK, i * HD : (i + 1) * HD]
            gah = ga[:, i * HD : (i + 1) * HD]
            s = jnp.where(mask, dot(q, k, NT) * SCALE, -1e30)
            p = jnp.exp(s - lse_ref[:, i : i + 1])
            gw = dot(gah, v, NT)
            delta = jnp.sum(p * gw, axis=-1, keepdims=True)
            gs = (p * (gw - delta)).astype(BF)
            dq = (dot(gs, k) * SCALE).astype(BF).astype(F32)
            dk = dk + dot(gs, q, TN)
            dv = dv + dot(p.astype(BF), gah, TN)
            outs[i], part = unrope(dq, lin_ref[:, i * HD : (i + 1) * HD], gq_ref[...])
            sum_q = sum_q + part
        dk_own, dv_own = dk[width - CHUNK :], dv[width - CHUNK :]
        if not first:
            dk_own = dk_own + carry_ref[:, j * HD : (j + 1) * HD]
            dv_own = dv_own + carry_ref[:, (nk + j) * HD : (nk + j + 1) * HD]
        carry_out[:, j * HD : (j + 1) * HD] = dk[:CHUNK]
        carry_out[:, (nk + j) * HD : (nk + j + 1) * HD] = dv[:CHUNK]
        dk_own = (dk_own * SCALE).astype(BF).astype(F32)
        outs[nq + j], part = unrope(dk_own, lin_ref[:, (nq + j) * HD : (nq + j + 1) * HD], gk_ref[...])
        sum_k = sum_k + part
        outs[nq + nk + j] = dv_own.astype(BF)
    gqkv = jnp.concatenate(outs, axis=1)
    gqkv_ref[...] = gqkv
    head_out[0:1, :] = sum_q
    head_out[1:2, :] = sum_k
    wait(in_copies)
    part_ref[:CHUNK, :] = dot(gqkv, joined(w), NT).astype(BF)
    if last:
        part_ref[CHUNK:, :] = jnp.zeros((16, part_ref.shape[1]), BF)
        both = jnp.concatenate([sum_q, sum_k], axis=1)
        part_ref[CHUNK:, : 2 * HD] = jnp.broadcast_to(both, (16, 2 * HD)).astype(BF)


def back_call(
    c, flag, ends, mid, t, r, cot, gain, rot, lse, lin, cosine, sine, gq, gk, w_out, w_q, w_kv, kept, carry, nq, nk, last
):
    tok, d = cot.shape
    first = carry is None
    full = lambda a: pl.BlockSpec(a.shape, lambda i: (0,) * a.ndim)
    args = [flag, ends, mid, t, r, cot, gain, rot, lse, lin, cosine, sine, gq, gk]
    specs = [smem(), smem()] + [full(a) for a in args[2:]]
    specs[5] = chunk_block(c, d)
    specs[9] = chunk_block(c, lin.shape[1])
    specs[10] = chunk_block(c, HD)
    specs[11] = chunk_block(c, HD)
    blocks = len(w_out)
    args += [*w_out, *w_q, *w_kv]
    specs += [hbm()] * (3 * blocks)
    if not first:
        args += [*carry, *kept]
        specs += [full(a) for a in carry] + [hbm(), hbm()]
    own = lambda n: pl.BlockSpec((CHUNK, n), lambda i: (0, 0))
    cols = (nq + 2 * nk) * HD
    depth = d // blocks
    rows = CHUNK + (16 if last else 0)
    out = pl.pallas_call(
        functools.partial(back_kernel, c, nq, nk, blocks, first, last),
        grid=(1,),
        in_specs=specs,
        out_specs=[
            own(d),
            chunk_block(c, d),
            chunk_block(c, cols),
            pl.BlockSpec((rows, d), lambda i: (0, 0)),
            pl.BlockSpec((1, d), lambda i: (0, 0)),
            pl.BlockSpec((2, HD), lambda i: (0, 0)),
            own(2 * nk * HD),
        ],
        out_shape=[
            jax.ShapeDtypeStruct((CHUNK, d), F32),
            jax.ShapeDtypeStruct((tok, d), BF),
            jax.ShapeDtypeStruct((tok, cols), BF),
            jax.ShapeDtypeStruct((rows, d), BF),
            jax.ShapeDtypeStruct((1, d), F32),
            jax.ShapeDtypeStruct((2, HD), F32),
            jax.ShapeDtypeStruct((CHUNK, 2 * nk * HD), F32),
        ],
        scratch_shapes=[
            pltpu.VMEM((blocks // 2, 2, depth, nq * HD), BF),
            pltpu.VMEM((blocks // 2, 2, depth, cols), BF),
            pltpu.SemaphoreType.DMA((3, blocks)),
        ],
        input_output_aliases={} if first else {17 + 3 * blocks: 1, 18 + 3 * blocks: 2},
        compiler_params=params(),
        cost_estimate=cost(3e9, 15e6),
    )(*args)
    return out[0], out[1:3], out[3], (out[6], out[4], out[5])


def grad_kernel(counts, *refs):
    out_ref = refs[-1]
    at = 0
    b_refs = iter(refs[len(counts) : -1])
    for a_ref, count in zip(refs, counts):
        for _ in range(count):
            b_ref = next(b_refs)
            out_ref[:, at : at + b_ref.shape[1]] = dot(a_ref[...], b_ref[...], TN).astype(BF)
            at += b_ref.shape[1]


def grad_call(n_dp, *pairs):
    tok, d = pairs[0][0].shape
    depth = d // n_dp
    bs = [b for _, group in pairs for b in group]
    cols = sum(b.shape[1] for b in bs)
    return pl.pallas_call(
        functools.partial(grad_kernel, [len(group) for _, group in pairs]),
        grid=(n_dp,),
        in_specs=[pl.BlockSpec((tok, depth), lambda i: (0, i)) for _ in pairs]
        + [pl.BlockSpec(b.shape, lambda i: (0, 0)) for b in bs],
        out_specs=pl.BlockSpec((depth, cols), lambda i: (i, 0)),
        out_shape=jax.ShapeDtypeStruct((d, cols), BF),
        compiler_params=params(),
        cost_estimate=cost(2 * tok * d * cols, 10e6),
    )(*[a for a, _ in pairs], *bs)


def input_kernel(first, last, flag_ref, x_ref, t_ref, r_ref, gm_ref, gain_ref, *rest):
    if not first:
        gain_in = rest[0]
    out_ref, gain_out = rest[-3:-1] if last else rest[-2:]
    got = jnp.where(flag_ref[0] == 1, r_ref[...], t_ref[...]).astype(F32)
    gn = got[:CHUNK]
    if last:
        rest[-1][...] = got[CHUNK : CHUNK + 8, : 2 * HD]
    x = x_ref[...].astype(F32)
    r1 = rms_r(x)
    h = gn * gain_ref[...]
    out_ref[...] = gm_ref[...] + r1 * h - x * (r1 * r1 * r1 * jnp.mean(h * x, axis=-1, keepdims=True))
    gain_sum = jnp.sum(gn * x * r1, axis=0, keepdims=True)
    gain_out[...] = gain_sum if first else gain_in[...] + gain_sum


def input_call(c, flag, x, t, r, gm, gain, kept, last):
    tok, d = x.shape
    own = pl.BlockSpec((CHUNK, d), lambda i: (0, 0))
    got = pl.BlockSpec(t.shape, lambda i: (0, 0))
    one = pl.BlockSpec((1, d), lambda i: (0, 0))
    first = kept is None
    return pl.pallas_call(
        functools.partial(input_kernel, first, last),
        grid=(1,),
        in_specs=[smem(), chunk_block(c, d), got, got, own, one] + ([] if first else [one, hbm()]),
        out_specs=[chunk_block(c, d), one] + ([pl.BlockSpec((8, 2 * HD), lambda i: (0, 0))] if last else []),
        out_shape=[jax.ShapeDtypeStruct((tok, d), F32), jax.ShapeDtypeStruct((1, d), F32)]
        + ([jax.ShapeDtypeStruct((8, 2 * HD), F32)] if last else []),
        input_output_aliases={} if first else {7: 0},
        compiler_params=params(),
        cost_estimate=cost(1e6, 8e6),
    )(flag, x, t, r, gm, gain, *([] if first else [kept[1], kept[0]]))


def output_kernel(aliased, flag_ref, mid_ref, t_ref, r_ref, *rest):
    out_ref = rest[-1]
    down = jnp.where(flag_ref[0] == 1, r_ref[...], t_ref[...]).astype(F32)
    out_ref[...] = (mid_ref[...] + down).astype(BF)


def output_call(c, flag, mid, t, r, kept, tok):
    d = mid.shape[1]
    own = pl.BlockSpec((CHUNK, d), lambda i: (0, 0))
    first = kept is None
    return pl.pallas_call(
        functools.partial(output_kernel, not first),
        grid=(1,),
        in_specs=[smem(), own, own, own] + ([] if first else [hbm()]),
        out_specs=chunk_block(c, d),
        out_shape=jax.ShapeDtypeStruct((tok, d), BF),
        input_output_aliases={} if first else {4: 0},
        compiler_params=params(),
        cost_estimate=cost(1e6, 5e6),
    )(flag, mid, t, r, *([] if first else [kept]))


def line_sum(line, x):
    n = lax.axis_size("mp")
    me = lax.axis_index("mp")
    half = n // 2
    for h in range(half - 1):
        r = lax.ppermute(x, "mp", [(h, h + 1), (n - 1 - h, n - 2 - h)])
        yield
        x = line(jnp.add, x, r)
    r = lax.ppermute(x, "mp", [(half - 1, half), (half, half - 1)])
    yield
    x = line(jnp.add, x, r)
    r = x
    for h in reversed(range(half - 1)):
        r = lax.ppermute(x, "mp", [(h + 1, h), (n - 2 - h, n - 1 - h)])
        if h:
            yield
            x = line(jnp.where, (me == h) | (me == n - 1 - h), r, x)
    return x, r


class Sum:
    def __init__(self, line, x):
        self.steps = line_sum(line, x)
        self.result = None
        self.step()

    def step(self):
        try:
            if self.result is None:
                next(self.steps)
        except StopIteration as done:
            self.result = done.value

    def total(self):
        while self.result is None:
            self.step()
        return self.result


class Line:
    def __init__(self):
        self.last = None

    def after(self, *args):
        if self.last is None:
            return args
        leaves, tree = jax.tree.flatten(args)
        leaves = lax.optimization_barrier((*leaves, self.last))[:-1]
        return jax.tree.unflatten(tree, leaves)

    def hold(self, arrays):
        self.last = lax.optimization_barrier((self.last, jax.tree.leaves(arrays)))[0]

    def __call__(self, f, *args, **kw):
        out = f(*self.after(*args), **kw)
        self.last = jax.tree.leaves(out)[-1]
        return out


SWAP = [(0, 1), (1, 0)]
DP = ("chip", "core")


class Gather:
    def __init__(self, x, low_first):
        self.n = lax.axis_size("chip")
        bits = [1 << b for b in range(self.n.bit_length() - 1)]
        self.bits = bits if low_first else bits[::-1]
        self.own = {0: x}
        self.swapped = {0: lax.ppermute(x, "core", SWAP)}
        self.level = 0

    def step(self):
        bit = self.bits[self.level]
        self.level += 1
        new = {
            r ^ bit: lax.ppermute(b, "chip", [(i, i ^ bit) for i in range(self.n)]) for r, b in self.own.items()
        }
        self.own |= new
        return list(new.values())

    def swap(self):
        for r, b in self.own.items():
            if r not in self.swapped:
                self.swapped[r] = lax.ppermute(b, "core", SWAP)

    def blocks(self):
        while self.level < len(self.bits):
            self.step()
        self.swap()
        return [b[r] for r in range(self.n) for b in (self.own, self.swapped)]


def in_order(stacked, index):
    n = stacked.shape[0]
    bit = 1
    while bit < n:
        parts = stacked.reshape(n // (2 * bit), 2, bit, *stacked.shape[1:])
        stacked = jnp.where(index & bit, parts[:, ::-1], parts).reshape(stacked.shape)
        bit *= 2
    return stacked


def own_sum(rows, index):
    rows = in_order(rows, index)
    half = rows.shape[0] // 2
    while half:
        if half > 1:
            pairs = [(i, i ^ (half // 2)) for i in range(lax.axis_size("chip"))]
            got = lax.ppermute(rows[half:], "chip", pairs)
        else:
            got = lax.ppermute(rows[half:], "core", SWAP)
        rows = rows[:half] + got
        half //= 2
    return rows[0]


def on_device(
    hidden_in,
    cotangent,
    doc_lengths,
    w_query,
    w_key,
    w_value,
    w_out,
    w_gate,
    w_up,
    w_down,
    norm_attn,
    norm_mlp,
    norm_query,
    norm_key,
):
    chips = lax.axis_size("chip")
    n_dp = 2 * chips
    core_id = lax.axis_index("core")
    dp = 2 * lax.axis_index("chip") + core_id
    mp = lax.axis_index("mp")
    n_mp = lax.axis_size("mp")
    tok, d = hidden_in.shape
    nq = w_query.shape[1] // HD
    nk = w_key.shape[1] // HD
    depth = w_query.shape[0]
    small = norm_query.shape[0]
    flag = jnp.stack([((mp == 0) | (mp == n_mp - 1)).astype(jnp.int32), lax.axis_index("chip"), core_id])

    wide = 2 * nk * HD
    widen = lambda v: jnp.pad(v, (0, wide - v.shape[0]))[None]
    placed = lambda v: widen(lax.dynamic_update_slice(jnp.zeros(HD, BF), v, (dp * small,)))
    gain_rows = jnp.concatenate([widen(norm_attn), widen(norm_mlp), placed(norm_query), placed(norm_key)])
    gain_rows = jnp.pad(gain_rows, ((0, 12), (0, 0)))
    w_kv = Gather(jnp.concatenate([jnp.concatenate([w_key, w_value], axis=1), gain_rows], axis=0), True)
    w_q = Gather(w_query, False)
    w_out = Gather(w_out.T, True)
    down_t = w_down.T
    tile = w_gate.shape[1] // 2
    packs = [
        Gather(jnp.concatenate([w[:, j * tile : (j + 1) * tile] for w in (w_gate, w_up, down_t)], axis=1), j == 0)
        for j in range(2)
    ]

    lengths = lax.dynamic_index_in_dim(doc_lengths, dp, 0, keepdims=False)
    ends = jnp.cumsum(lengths)
    ends = ends.astype(jnp.int32)
    token = jnp.arange(tok, dtype=jnp.int32)
    begin = jnp.max(jnp.where(token[:, None] >= ends[None, :], ends[None, :], 0), axis=1)
    position = token - begin
    inverse = ROPE_BASE ** (-(2.0 * jnp.arange(HD // 2, dtype=F32)) / HD)
    angles = position.astype(F32)[:, None] * inverse[None, :]
    cosine = jnp.cos(angles)
    sine = jnp.sin(angles)
    cosine = jnp.concatenate([cosine, cosine], axis=1)
    sine = jnp.concatenate([-sine, sine], axis=1)

    line = Line()

    def steps(*sums):
        for s in sums:
            s.step()

    w_q, w_kv = w_q.blocks(), w_kv.blocks()
    w_out_blocks = w_out.blocks()
    first_packs = [p.step() for p in packs]
    normed, lin, rot, gain_attn, gain_mlp, gain_query, gain_key = line(
        lambda ready, *a: qkv_call(*a, nq=nq, nk=nk), w_out_blocks[::2], flag, hidden_in, cosine, sine, w_q, w_kv
    )

    order = list(reversed(range(tok // CHUNK)))
    att = None
    lse, branch, mid, down, gnt, gn = {}, {}, {}, {}, {}, {}
    ready = first_packs
    for c in order:
        att, lse[c], part = line(
            lambda ready, *a, c=c: attn_call(c, *a, nq=nq, nk=nk), ready, flag, ends, rot, w_out_blocks, att
        )
        branch[c] = Sum(line, part)
        ready = None
    for p in packs:
        while p.level < len(p.bits):
            p.step()

    c0, c1, c2, c3 = order
    state = {"mlp": None, "back": None, "carry": None, "input": None, "output": None}
    gm = {}

    def run_mlp(c):
        t, r = branch[c].total()
        mid[c], state["mlp"], down[c], gnt_part = line(
            functools.partial(mlp_call, c), flag, hidden_in, t, r, cotangent, gain_mlp,
            [p.blocks() for p in packs], state["mlp"],
        )
        gnt[c] = Sum(line, gnt_part)

    def run_back(c):
        t, r = gnt[c].total()
        gm[c], state["back"], part, state["carry"] = line(
            functools.partial(back_call, c, nq=nq, nk=nk, last=c == c3), flag, ends, mid[c], t, r, cotangent,
            gain_mlp, rot, lse[c], lin, cosine, sine, gain_query, gain_key, w_out_blocks, w_q, w_kv,
            state["back"], state["carry"],
        )
        gn[c] = Sum(line, part)

    def run_input(c):
        t, r = gn[c].total()
        state["input"] = line(
            functools.partial(input_call, c, last=c == c3), flag, hidden_in, t, r, gm[c], gain_attn, state["input"]
        )

    def run_output(c):
        t, r = down[c].total()
        state["output"] = line(functools.partial(output_call, c, tok=tok), flag, mid[c], t, r, state["output"])

    def start_down(*cs):
        for c in cs:
            down[c] = Sum(line, line.after(down[c])[0])

    def scatter(*pairs):
        g = line(lambda pairs: grad_call(n_dp, *pairs), pairs)
        return lax.psum_scatter(g, DP, scatter_dimension=0, tiled=True)

    steps(branch[c0])
    line.hold([list(p.own.values()) for p in packs])
    steps(branch[c1], branch[c0], branch[c2], branch[c1])
    run_mlp(c0)
    steps(branch[c3], branch[c2])
    run_mlp(c1)
    steps(gnt[c0], branch[c3])
    run_mlp(c2)
    steps(gnt[c1], gnt[c0])
    run_mlp(c3)
    n2, prod, gg, gu = state["mlp"]
    steps(gnt[c2], gnt[c1])
    run_back(c0)
    steps(gnt[c3], gnt[c2])
    run_back(c1)
    g_mlp = scatter((n2, (gg, gu)), (cotangent, (prod,)))
    steps(gn[c0], gnt[c3])
    run_back(c2)
    steps(gn[c1], gn[c0])
    run_back(c3)
    gb, gqkv = state["back"]
    start_down(c0, c1, c2, c3)
    g_attn = scatter((normed, (gqkv,)), (gb, (att,)))
    steps(gn[c2], gn[c1])
    run_input(c0)
    steps(gn[c3], gn[c2])
    run_input(c1)
    steps(down[c0], gn[c3])
    run_input(c2)
    steps(down[c1], down[c0])
    run_input(c3)
    grad_input, sum_attn, sum_head = state["input"]
    steps(down[c2], down[c1])
    run_output(c0)
    steps(down[c3], down[c2])
    run_output(c1)
    steps(down[c3])
    run_output(c2)
    run_output(c3)

    sums = own_sum(
        jnp.concatenate(
            [sum_attn.reshape(n_dp, depth), state["carry"][1].reshape(n_dp, depth)]
            + [sum_head[0, i * HD : (i + 1) * HD].reshape(n_dp, small) for i in range(2)],
            axis=1,
        ),
        dp,
    )
    g_mlp = g_mlp.astype(F32)
    g_attn = g_attn.astype(F32)
    ff = w_gate.shape[1]
    kv = nk * HD
    q = nq * HD
    return (
        state["output"],
        grad_input,
        g_attn[:, :q],
        g_attn[:, q : q + kv],
        g_attn[:, q + kv : q + 2 * kv],
        g_attn[:, q + 2 * kv :].T,
        g_mlp[:, :ff],
        g_mlp[:, ff : 2 * ff],
        g_mlp[:, 2 * ff :].T,
        sums[:depth],
        sums[depth : 2 * depth],
        sums[2 * depth : 2 * depth + small],
        sums[2 * depth + small :],
    )


def solution(mesh):
    n_dp, n_mp = mesh.devices.shape
    mesh = jax.sharding.Mesh(mesh.devices.reshape(n_dp // 2, 2, n_mp), ("chip", "core", "mp"))
    rows = P(DP, None)
    weight = P(DP, "mp")
    turned = P("mp", DP)
    gain = P(DP)
    return jax.shard_map(
        on_device,
        mesh=mesh,
        in_specs=(rows, rows, P(), weight, weight, weight, turned, weight, weight, turned, gain, gain, gain, gain),
        out_specs=(rows, rows, weight, weight, weight, turned, weight, weight, turned, gain, gain, gain, gain),
        check_vma=False,
    )
```

time: 913 us -> 730 us (0.80)
  waiting for transfers between devices: 482 us -> 203 us
  starting transfers between devices: 104 us -> 177 us
  matrix products: 47.5 us -> 0 us
  Pallas kernels: 196 us -> 233 us
  other arithmetic: 38.9 us -> 56.2 us
  local copies, waits for them, and re-layouts: 20.7 us -> 32.9 us
    ppermute x48 -> x70, waiting for transfers between devices: 286 us -> 147 us  [the longest x16 79.3 us: line_sum(): r = lax.ppermute(x, 'mp', [(h, h + 1), (n - 1 - h, n - 2 - h)])]
    ppermute x16, waiting for transfers between devices: 138 us -> 55.4 us  [line_sum(): r = lax.ppermute(x, 'mp', [(h + 1, h), (n - 2 - h, n - 1 - h)])]
    ppermute x48 -> x70, starting transfers between devices: 81.6 us -> 154 us  [the longest x16 113 us: line_sum(): r = lax.ppermute(x, 'mp', [(h, h + 1), (n - 1 - h, n - 2 - h)])]
    all_gather x5 -> x0, waiting for transfers between devices: 55.4 us -> none  [the longest x1 33 us: on_device(): w_qkv = lax.all_gather(w_qkv, 'dp', axis=0)]
    dot_general x5 -> x0, matrix products: 47.5 us -> none  [scatter(): g = lax.dot_general(a, b, TN, preferred_element_type=F32).astype(BF)]
    pallas_call x17 -> x19, Pallas kernels: 183 us -> 220 us  [the longest x4 76.7 us: mlp_call(): pl.pallas_call(functools.partial(mlp_kernel, tiles, blocks), grid=(1,), i...]
    add x39 -> x35, other arithmetic: 24.3 us -> 44.7 us  [the longest x32 44.6 us: __call__(): out = f(*self.after(*args), **kw)]
    unnamed x110 -> x162, local copies, waits for them, and re-layouts: 13.7 us -> 19.6 us
  transfers between devices with their start and end apart: 74 -> 88, of which waited for: 33 -> 25; matrix products, arithmetic and copies ran while one was open for 9% -> 9% of each run, Pallas kernels for 20% -> 29%
where the time goes in v2:
time: 730 us; the launch traced here: 718 us
  Pallas kernels  233 us (32%)
  waiting for transfers between devices  203 us (28%)
  starting transfers between devices  177 us (24%)
  other arithmetic  56.2 us (8%)
  local copies, waits for them, and re-layouts  32.9 us (5%)
  between operations  16.2 us (2%)
    ppermute x16, starting transfers between devices, line_sum(): r = lax.ppermute(x, 'mp', [(h, h + 1), (n - 1 - h, n - 2 - h)])  113 us
    ppermute x16, waiting for transfers between devices, line_sum(): r = lax.ppermute(x, 'mp', [(h, h + 1), (n - 1 - h, n - 2 - h)])  79.3 us
    pallas_call x4, Pallas kernels, mlp_call(): pl.pallas_call(functools.partial(mlp_kernel, tiles, blocks), grid=(1,), i...  76.7 us
    ppermute x15, waiting for transfers between devices, step(): lax.ppermute(b, 'chip', [(i, i ^ bit) for i in range(self.n)])  62.1 us
    ppermute x16, waiting for transfers between devices, line_sum(): r = lax.ppermute(x, 'mp', [(h + 1, h), (n - 2 - h, n - 1 - h)])  55.4 us
    pallas_call x4, Pallas kernels, back_call(): pl.pallas_call(functools.partial(back_kernel, c, nq, nk, blocks, first, l...  47 us
    add x32, other arithmetic, __call__(): out = f(*self.after(*args), **kw)  44.6 us
    pallas_call x2, Pallas kernels, grad_call(): pl.pallas_call(functools.partial(grad_kernel, [len(group) for _, group in...  39.8 us
  transfers between devices with their start and end apart: 88, of which 25 were waited for; matrix products, arithmetic and copies ran while one was open for 9% of the time, Pallas kernels for 29%

profile of v2, /device:TPU:0, one launch (start us, length us, event | category | flops | bytes accessed | tf_op | source)
XLA Modules:
  0.0 718.5 jit_solution(12991342914205123776)
XLA Ops:
  40.3 29.5 %collective-permute-done.5.rest_6_.rest_14_ = bf16[256,512]{1,0:T(8,128)(2,1)S(1)} collective-permute-done((bf16[256,512]{1,0:T(8,128)(2,1)S(1)}, bf16[256,512]{1,0:T(8,128)(2,1)S(1)}, u32[]{:S(2)}, u32[]{:S(2)}) %collective-permute-start.5) | collective-permute-done | bytes 262176 | tf_op jit(solution)/shard_map/ppermute | solution.py:634
  85.4 12.5 %shard_map.237 = (bf16[1024,2048]{1,0:T(8,128)(2,1)}, f32[1024,768]{1,0:T(8,128)}, bf16[1024,1024]{1,0:T(8,128)(2,1)}, f32[1,2048]{1,0:T(1,128)}, f32[1,2048]{1,...) custom-call(s32[3]{0:T(128)} %pad_add_fusion.flag_ref, bf16[1024,2048]{1,0:T(8,128)(2,1)} %x_ref.9, ...), custom_call_target="tpu_custom_call" | custom-call | tf_op jit(solution)/shard_map/pallas_call | solution.py:132
  97.9 8.3 %collective-permute-done.22.rest_12_ = bf16[256,2304]{1,0:T(8,128)(2,1)S(1)} collective-permute-done((bf16[256,2304]{1,0:T(8,128)(2,1)S(1)}, bf16[256,2304]{1,0:T(8,128)(2,1)S(1)}, u32[]{:S(2)}, u32[]{:S(2)}) %collective-permute-start.22) | collective-permute-done | bytes 1179680 | tf_op jit(solution)/shard_map/ppermute | solution.py:634
  121.5 9.6 %collective-permute-done.30.rest_4_ = bf16[256,2304]{1,0:T(8,128)(2,1)} collective-permute-done((bf16[256,2304]{1,0:T(8,128)(2,1)S(1)}, bf16[256,2304]{1,0:T(8,128)(2,1)}, u32[]{:S(2)}, u32[]{:S(2)}) %collective-permute-start.30) | collective-permute-done | bytes 1179680 | tf_op jit(solution)/shard_map/ppermute | solution.py:634
  144.9 22.4 %collective-permute-done.24 = bf16[256,2048]{1,0:T(8,128)(2,1)} collective-permute-done((bf16[256,2048]{1,0:T(8,128)(2,1)S(1)}, bf16[256,2048]{1,0:T(8,128)(2,1)}, u32[]{:S(2)}, u32[]{:S(2)}) %collective-permute-start.24) | collective-permute-done | bytes 1048608 | tf_op jit(solution)/shard_map/ppermute | solution.py:563
  167.3 20.9 %collective-permute-done.41 = bf16[256,2048]{1,0:T(8,128)(2,1)} collective-permute-done((bf16[256,2048]{1,0:T(8,128)(2,1)}, bf16[256,2048]{1,0:T(8,128)(2,1)}, u32[]{:S(2)}, u32[]{:S(2)}) %collective-permute-start.41) | collective-permute-done | bytes 1048608 | tf_op jit(solution)/shard_map/ppermute | solution.py:563
  200.1 33.7 %collective-permute-start.23 = (bf16[256,2048]{1,0:T(8,128)(2,1)}, bf16[256,2048]{1,0:T(8,128)(2,1)}, u32[]{:S(2)}, u32[]{:S(2)}) collective-permute-start(bf16[256,2048]{1,0:T(8,128)(2,1)} %get-tuple-element.626), channel_id=1, source_target_pairs={{0,1},{3,2},{4,5},{7,6},{8,9},{11,10},{12,13},{15,14},{16,17},{19,... | collective-permute-start | bytes 3145736 | tf_op jit(solution)/shard_map/ppermute | solution.py:563
  239.0 14.6 %collective-permute-done.27.r_ref = bf16[256,2048]{1,0:T(8,128)(2,1)S(1)} collective-permute-done((bf16[256,2048]{1,0:T(8,128)(2,1)S(1)}, bf16[256,2048]{1,0:T(8,128)(2,1)S(1)}, u32[]{:S(2)}, u32[]{:S(2)}) %collective-permute-start.27) | collective-permute-done | bytes 1048608 | tf_op jit(solution)/shard_map/ppermute | solution.py:571
  254.5 19.1 %shard_map.242 = (f32[256,2048]{1,0:T(8,128)}, bf16[1024,2048]{1,0:T(8,128)(2,1)}, bf16[1024,1536]{1,0:T(8,128)(2,1)}, bf16[1024,1536]{1,0:T(8,128)(2,1)}, bf16[...) custom-call(s32[3]{0:T(128)} %pad_add_fusion.flag_ref, bf16[1024,2048]{1,0:T(8,128)(2,1)} %x_ref.9, ...), custom_call_target="tpu_custom_call" | custom-call | tf_op jit(solution)/shard_map/pallas_call | solution.py:300
  273.7 7.5 %collective-permute-start.43 = (bf16[256,2048]{1,0:T(8,128)(2,1)}, bf16[256,2048]{1,0:T(8,128)(2,1)}, u32[]{:S(2)}, u32[]{:S(2)}) collective-permute-start(bf16[256,2048]{1,0:T(8,128)(2,1)} %get-tuple-element.661), channel_id=1, source_target_pairs={{0,1},{3,2},{4,5},{7,6},{8,9},{11,10},{12,13},{15,14},{16,17},{19,... | collective-permute-start | bytes 3145736 | tf_op jit(solution)/shard_map/ppermute | solution.py:563
  288.9 19.2 %shard_map.243 = (f32[256,2048]{1,0:T(8,128)}, bf16[1024,2048]{1,0:T(8,128)(2,1)}, bf16[1024,1536]{1,0:T(8,128)(2,1)}, bf16[1024,1536]{1,0:T(8,128)(2,1)}, bf16[...) custom-call(s32[3]{0:T(128)} %pad_add_fusion.flag_ref, ...), custom_call_target="tpu_custom_call", output_to_operand_aliasing={{1}: (22, {}), {2}: (23, {}), {3}: (24, {}), {4}: (25, {})} | custom-call | tf_op jit(solution)/shard_map/pallas_call | solution.py:300
  321.3 19.2 %shard_map.244 = (f32[256,2048]{1,0:T(8,128)}, bf16[1024,2048]{1,0:T(8,128)(2,1)}, bf16[1024,1536]{1,0:T(8,128)(2,1)}, bf16[1024,1536]{1,0:T(8,128)(2,1)}, bf16[...) custom-call(s32[3]{0:T(128)} %pad_add_fusion.flag_ref, ...), custom_call_target="tpu_custom_call", output_to_operand_aliasing={{1}: (22, {}), {2}: (23, {}), {3}: (24, {}), {4}: (25, {})} | custom-call | tf_op jit(solution)/shard_map/pallas_call | solution.py:300
  352.6 19.2 %shard_map.245 = (f32[256,2048]{1,0:T(8,128)}, bf16[1024,2048]{1,0:T(8,128)(2,1)}, bf16[1024,1536]{1,0:T(8,128)(2,1)}, bf16[1024,1536]{1,0:T(8,128)(2,1)}, bf16[...) custom-call(s32[3]{0:T(128)} %pad_add_fusion.flag_ref, ...), custom_call_target="tpu_custom_call", output_to_operand_aliasing={{1}: (22, {}), {2}: (23, {}), {3}: (24, {}), {4}: (25, {})} | custom-call | tf_op jit(solution)/shard_map/pallas_call | solution.py:300
  381.8 11.8 %shard_map.246 = (f32[256,2048]{1,0:T(8,128)}, bf16[1024,2048]{1,0:T(8,128)(2,1)}, bf16[1024,1024]{1,0:T(8,128)(2,1)}, bf16[256,2048]{1,0:T(8,128)(2,1)}, f32[1,...) custom-call(s32[3]{0:T(128)} %pad_add_fusion.flag_ref, s32[8]{0:T(128)} %bitcast.43, ...), custom_call_target="tpu_custom_call" | custom-call | tf_op jit(solution)/shard_map/pallas_call | solution.py:439
  406.5 12.0 %shard_map.247 = (f32[256,2048]{1,0:T(8,128)}, bf16[1024,2048]{1,0:T(8,128)(2,1)}, bf16[1024,1024]{1,0:T(8,128)(2,1)}, bf16[256,2048]{1,0:T(8,128)(2,1)}, f32[1,...) custom-call(s32[3]{0:T(128)} %pad_add_fusion.flag_ref, ...), custom_call_target="tpu_custom_call", output_to_operand_aliasing={{1}: (41, {}), {2}: (42, {})} | custom-call | tf_op jit(solution)/shard_map/pallas_call | solution.py:439
  424.1 26.8 %shard_map.248 = bf16[2048,4608]{1,0:T(8,128)(2,1)} custom-call(bf16[1024,2048]{1,0:T(8,128)(2,1)} %get-tuple-element.839.refs_0_, bf16[1024,2048]{1,0:T(8,128)(2,1)} %cot_ref.7, bf16[1024,1536]{1,0:T(8,128)(2,1)} %get-tuple-element.841.refs_2_, bf16[1024,1536]{1,0:T(8,128)(2,1)} %get-tuple-element.842.refs_3_, bf16[1024,1536]{1,0:T(8,128)(2,1)} %get-tuple-element.843.refs_4_), custom_call_target="tpu_custom_call" | custom-call | tf_op jit(solution)/shard_map/pallas_call | solution.py:489
  458.6 12.0 %shard_map.249 = (f32[256,2048]{1,0:T(8,128)}, bf16[1024,2048]{1,0:T(8,128)(2,1)}, bf16[1024,1024]{1,0:T(8,128)(2,1)}, bf16[256,2048]{1,0:T(8,128)(2,1)}, f32[1,...) custom-call(s32[3]{0:T(128)} %pad_add_fusion.flag_ref, ...), custom_call_target="tpu_custom_call", output_to_operand_aliasing={{1}: (41, {}), {2}: (42, {})} | custom-call | tf_op jit(solution)/shard_map/pallas_call | solution.py:439
  479.6 11.2 %shard_map.250 = (f32[256,2048]{1,0:T(8,128)}, bf16[1024,2048]{1,0:T(8,128)(2,1)}, bf16[1024,1024]{1,0:T(8,128)(2,1)}, bf16[272,2048]{1,0:T(8,128)(2,1)}, f32[1,...) custom-call(s32[3]{0:T(128)} %pad_add_fusion.flag_ref, ...), custom_call_target="tpu_custom_call", output_to_operand_aliasing={{1}: (41, {}), {2}: (42, {})} | custom-call | tf_op jit(solution)/shard_map/pallas_call | solution.py:439
  490.8 13.0 %shard_map.251 = bf16[2048,1536]{1,0:T(8,128)(2,1)} custom-call(bf16[1024,2048]{1,0:T(8,128)(2,1)} %get-tuple-element.960.refs_0_, bf16[1024,2048]{1,0:T(8,128)(2,1)} %get-tuple-element.961.refs_1_, bf16[1024,1024]{1,0:T(8,128)(2,1)} %get-tuple-element.962.refs_2_, bf16[1024,512]{1,0:T(8,128)(2,1)} %get-tuple-element.963.refs_3_), custom_call_target="tpu_custom_call" | custom-call | tf_op jit(solution)/shard_map/pallas_call | solution.py:489
  511.1 18.9 %collective-permute-done.65 = bf16[256,2048]{1,0:T(8,128)(2,1)S(1)} collective-permute-done((bf16[256,2048]{1,0:T(8,128)(2,1)}, bf16[256,2048]{1,0:T(8,128)(2,1)S(1)}, u32[]{:S(2)}, u32[]{:S(2)}) %collective-permute-start.65) | collective-permute-done | bytes 1048608 | tf_op jit(solution)/shard_map/ppermute | solution.py:563
  581.1 8.1 %collective-permute-start.76 = (bf16[256,2048]{1,0:T(8,128)(2,1)}, bf16[256,2048]{1,0:T(8,128)(2,1)}, u32[]{:S(2)}, u32[]{:S(2)}) collective-permute-start(bf16[256,2048]{1,0:T(8,128)(2,1)} %get-tuple-element.1027), channel_id=1, source_target_pairs={{0,1},{3,2},{4,5},{7,6},{8,9},{11,10},{12,13},{15,14},{16,17},{19,... | collective-permute-start | bytes 3145736 | tf_op jit(solution)/shard_map/ppermute | solution.py:563
  646.7 7.7 %collective-permute-done.79.r_ref = bf16[256,2048]{1,0:T(8,128)(2,1)} collective-permute-done((bf16[256,2048]{1,0:T(8,128)(2,1)S(1)}, bf16[256,2048]{1,0:T(8,128)(2,1)}, u32[]{:S(2)}, u32[]{:S(2)}) %collective-permute-start.79) | collective-permute-done | bytes 1048608 | tf_op jit(solution)/shard_map/ppermute | solution.py:571
  667.0 9.7 %collective-permute-done.82.r_ref = bf16[256,2048]{1,0:T(8,128)(2,1)S(1)} collective-permute-done((bf16[256,2048]{1,0:T(8,128)(2,1)S(1)}, bf16[256,2048]{1,0:T(8,128)(2,1)S(1)}, u32[]{:S(2)}, u32[]{:S(2)}) %collective-permute-start.82) | collective-permute-done | bytes 1048608 | tf_op jit(solution)/shard_map/ppermute | solution.py:571
  681.0 13.0 %collective-permute-done.81.r_ref = bf16[256,2048]{1,0:T(8,128)(2,1)S(1)} collective-permute-done((bf16[256,2048]{1,0:T(8,128)(2,1)S(1)}, bf16[256,2048]{1,0:T(8,128)(2,1)S(1)}, u32[]{:S(2)}, u32[]{:S(2)}) %collective-permute-start.81) | collective-permute-done | bytes 1048608 | tf_op jit(solution)/shard_map/ppermute | solution.py:571
  (426 shorter events, 322.5 us)
Async XLA Ops:
  7.2 691.2 %reduce-scatter.3.cloned.1.call-start = ((), (), s32[]{:S(2)}) async-start(), calls=%async_computation.2 | async-start | bytes 7077888 | tf_op jit(solution)/shard_map/reduce_scatter | solution.py:796
  37.2 43.5 %collective-permute-start.21 = (bf16[256,2304]{1,0:T(8,128)(2,1)S(1)}, bf16[256,2304]{1,0:T(8,128)(2,1)}, u32[]{:S(2)}, u32[]{:S(2)}) collective-permute-start(bf16[256,2304]{1,0:T(8,128)(2,1)S(1)} %pad_maximum_fusion.rest_0_), channel_id=1, source_target_pairs={{0,8},{8,0},{16,24},{24,16},{1,9},{9,1},{17,25},{25,17},{2,10},{10... | collective-permute-start | bytes 3538952 | tf_op jit(solution)/shard_map/ppermute | solution.py:634
  77.9 53.2 %collective-permute-start.30 = (bf16[256,2304]{1,0:T(8,128)(2,1)S(1)}, bf16[256,2304]{1,0:T(8,128)(2,1)}, u32[]{:S(2)}, u32[]{:S(2)}) collective-permute-start(bf16[256,2304]{1,0:T(8,128)(2,1)S(1)} %pad_maximum_fusion.rest_0_), channel_id=1, source_target_pairs={{0,16},{8,24},{16,0},{24,8},{1,17},{9,25},{17,1},{25,9},{2,18},{10... | collective-permute-start | bytes 3538952 | tf_op jit(solution)/shard_map/ppermute | solution.py:634
  80.2 55.4 %collective-permute-start.35 = (bf16[256,2304]{1,0:T(8,128)(2,1)S(1)}, bf16[256,2304]{1,0:T(8,128)(2,1)}, u32[]{:S(2)}, u32[]{:S(2)}) collective-permute-start(bf16[256,2304]{1,0:T(8,128)(2,1)S(1)} %pad_maximum_fusion.1.rest_8_), channel_id=1, source_target_pairs={{0,8},{8,0},{16,24},{24,16},{1,9},{9,1},{17,25},{25,17},{2,10},{10... | collective-permute-start | bytes 3538952 | tf_op jit(solution)/shard_map/ppermute | solution.py:634
  80.7 55.4 %collective-permute-start.28 = (bf16[256,2304]{1,0:T(8,128)(2,1)S(1)}, bf16[256,2304]{1,0:T(8,128)(2,1)}, u32[]{:S(2)}, u32[]{:S(2)}) collective-permute-start(bf16[256,2304]{1,0:T(8,128)(2,1)S(1)} %pad_maximum_fusion.rest_0_), channel_id=1, source_target_pairs={{0,4},{4,0},{1,5},{5,1},{2,6},{6,2},{3,7},{7,3},{8,12},{12,8},{9,1... | collective-permute-start | bytes 3538952 | tf_op jit(solution)/shard_map/ppermute | solution.py:627
  80.7 61.3 %collective-permute-start.34 = (bf16[256,2304]{1,0:T(8,128)(2,1)S(1)}, bf16[256,2304]{1,0:T(8,128)(2,1)}, u32[]{:S(2)}, u32[]{:S(2)}) collective-permute-start(bf16[256,2304]{1,0:T(8,128)(2,1)S(1)} %pad_maximum_fusion.1.rest_8_), channel_id=1, source_target_pairs={{0,4},{4,0},{1,5},{5,1},{2,6},{6,2},{3,7},{7,3},{8,12},{12,8},{9,1... | collective-permute-start | bytes 3538952 | tf_op jit(solution)/shard_map/ppermute | solution.py:627
  135.6 52.5 %collective-permute-start.32 = (bf16[256,2304]{1,0:T(8,128)(2,1)}, bf16[256,2304]{1,0:T(8,128)(2,1)S(1)}, u32[]{:S(2)}, u32[]{:S(2)}) collective-permute-start(bf16[256,2304]{1,0:T(8,128)(2,1)} %collective-permute-done.21.rest_2_), channel_id=1, source_target_pairs={{0,16},{8,24},{16,0},{24,8},{1,17},{9,25},{17,1},{25,9},{2,18},{10... | collective-permute-start | bytes 3538952 | tf_op jit(solution)/shard_map/ppermute | solution.py:634
  136.1 59.6 %collective-permute-start.38 = (bf16[256,2304]{1,0:T(8,128)(2,1)S(1)}, bf16[256,2304]{1,0:T(8,128)(2,1)S(1)}, u32[]{:S(2)}, u32[]{:S(2)}) collective-permute-start(bf16[256,2304]{1,0:T(8,128)(2,1)S(1)} %collective-permute-done.22.rest_12_), channel_id=1, source_target_pairs={{0,8},{8,0},{16,24},{24,16},{1,9},{9,1},{17,25},{25,17},{2,10},{10... | collective-permute-start | bytes 3538952 | tf_op jit(solution)/shard_map/ppermute | solution.py:634
  142.1 46.1 %collective-permute-start.41 = (bf16[256,2048]{1,0:T(8,128)(2,1)}, bf16[256,2048]{1,0:T(8,128)(2,1)}, u32[]{:S(2)}, u32[]{:S(2)}) collective-permute-start(bf16[256,2048]{1,0:T(8,128)(2,1)} %get-tuple-element.599), channel_id=1, source_target_pairs={{0,1},{3,2},{4,5},{7,6},{8,9},{11,10},{12,13},{15,14},{16,17},{19,... | collective-permute-start | bytes 3145736 | tf_op jit(solution)/shard_map/ppermute | solution.py:563
  144.9 51.6 %collective-permute-start.29 = (bf16[256,2304]{1,0:T(8,128)(2,1)}, bf16[256,2304]{1,0:T(8,128)(2,1)S(1)}, u32[]{:S(2)}, u32[]{:S(2)}) collective-permute-start(bf16[256,2304]{1,0:T(8,128)(2,1)} %collective-permute-done.21.rest_2_), channel_id=1, source_target_pairs={{0,4},{4,0},{1,5},{5,1},{2,6},{6,2},{3,7},{7,3},{8,12},{12,8},{9,1... | collective-permute-start | bytes 3538952 | tf_op jit(solution)/shard_map/ppermute | solution.py:642
  196.5 41.0 %collective-permute-start.33 = (bf16[256,2304]{1,0:T(8,128)(2,1)S(1)}, bf16[256,2304]{1,0:T(8,128)(2,1)S(1)}, u32[]{:S(2)}, u32[]{:S(2)}) collective-permute-start(bf16[256,2304]{1,0:T(8,128)(2,1)S(1)} %collective-permute-done.32.rest_6_), channel_id=1, source_target_pairs={{0,4},{4,0},{1,5},{5,1},{2,6},{6,2},{3,7},{7,3},{8,12},{12,8},{9,1... | collective-permute-start | bytes 3538952 | tf_op jit(solution)/shard_map/ppermute | solution.py:642
  197.0 41.9 %collective-permute-start.39 = (bf16[256,2304]{1,0:T(8,128)(2,1)S(1)}, bf16[256,2304]{1,0:T(8,128)(2,1)S(1)}, u32[]{:S(2)}, u32[]{:S(2)}) collective-permute-start(bf16[256,2304]{1,0:T(8,128)(2,1)S(1)} %collective-permute-done.38.rest_14_), channel_id=1, source_target_pairs={{0,4},{4,0},{1,5},{5,1},{2,6},{6,2},{3,7},{7,3},{8,12},{12,8},{9,1... | collective-permute-start | bytes 3538952 | tf_op jit(solution)/shard_map/ppermute | solution.py:642
  198.8 54.7 %collective-permute-start.27 = (bf16[256,2048]{1,0:T(8,128)(2,1)S(1)}, bf16[256,2048]{1,0:T(8,128)(2,1)S(1)}, u32[]{:S(2)}, u32[]{:S(2)}) collective-permute-start(bf16[256,2048]{1,0:T(8,128)(2,1)S(1)} %add.135.t_ref), channel_id=1, source_target_pairs={{1,0},{2,3},{5,4},{6,7},{9,8},{10,11},{13,12},{14,15},{17,16},{18,... | collective-permute-start | bytes 3145736 | tf_op jit(solution)/shard_map/ppermute | solution.py:571
  200.1 81.0 %collective-permute-start.23 = (bf16[256,2048]{1,0:T(8,128)(2,1)}, bf16[256,2048]{1,0:T(8,128)(2,1)}, u32[]{:S(2)}, u32[]{:S(2)}) collective-permute-start(bf16[256,2048]{1,0:T(8,128)(2,1)} %get-tuple-element.626), channel_id=1, source_target_pairs={{0,1},{3,2},{4,5},{7,6},{8,9},{11,10},{12,13},{15,14},{16,17},{19,... | collective-permute-start | bytes 3145736 | tf_op jit(solution)/shard_map/ppermute | solution.py:563
  235.4 49.3 %collective-permute-start.45 = (bf16[256,2048]{1,0:T(8,128)(2,1)S(1)}, bf16[256,2048]{1,0:T(8,128)(2,1)}, u32[]{:S(2)}, u32[]{:S(2)}) collective-permute-start(bf16[256,2048]{1,0:T(8,128)(2,1)S(1)} %add.136), channel_id=1, source_target_pairs={{1,2},{2,1},{5,6},{6,5},{9,10},{10,9},{13,14},{14,13},{17,18},{18,... | collective-permute-start | bytes 3145736 | tf_op jit(solution)/shard_map/ppermute | solution.py:566
  237.5 50.4 %collective-permute-start.44 = (bf16[256,2048]{1,0:T(8,128)(2,1)S(1)}, bf16[256,2048]{1,0:T(8,128)(2,1)S(1)}, u32[]{:S(2)}, u32[]{:S(2)}) collective-permute-start(bf16[256,2048]{1,0:T(8,128)(2,1)S(1)} %add.137.t_ref), channel_id=1, source_target_pairs={{1,0},{2,3},{5,4},{6,7},{9,8},{10,11},{13,12},{14,15},{17,16},{18,... | collective-permute-start | bytes 3145736 | tf_op jit(solution)/shard_map/ppermute | solution.py:571
  393.6 57.4 %collective-permute-start.55 = (bf16[256,2048]{1,0:T(8,128)(2,1)}, bf16[256,2048]{1,0:T(8,128)(2,1)}, u32[]{:S(2)}, u32[]{:S(2)}) collective-permute-start(bf16[256,2048]{1,0:T(8,128)(2,1)} %get-tuple-element.844), channel_id=1, source_target_pairs={{0,1},{3,2},{4,5},{7,6},{8,9},{11,10},{12,13},{15,14},{16,17},{19,... | collective-permute-start | bytes 3145736 | tf_op jit(solution)/shard_map/ppermute | solution.py:563
  402.7 51.9 %collective-permute-start.54 = (bf16[256,2048]{1,0:T(8,128)(2,1)S(1)}, bf16[256,2048]{1,0:T(8,128)(2,1)}, u32[]{:S(2)}, u32[]{:S(2)}) collective-permute-start(bf16[256,2048]{1,0:T(8,128)(2,1)S(1)} %add.146), channel_id=1, source_target_pairs={{1,2},{2,1},{5,6},{6,5},{9,10},{10,9},{13,14},{14,13},{17,18},{18,... | collective-permute-start | bytes 3145736 | tf_op jit(solution)/shard_map/ppermute | solution.py:566
  404.8 52.9 %collective-permute-start.59 = (bf16[256,2048]{1,0:T(8,128)(2,1)S(1)}, bf16[256,2048]{1,0:T(8,128)(2,1)S(1)}, u32[]{:S(2)}, u32[]{:S(2)}) collective-permute-start(bf16[256,2048]{1,0:T(8,128)(2,1)S(1)} %add.147.t_ref), channel_id=1, source_target_pairs={{1,0},{2,3},{5,4},{6,7},{9,8},{10,11},{13,12},{14,15},{17,16},{18,... | collective-permute-start | bytes 3145736 | tf_op jit(solution)/shard_map/ppermute | solution.py:571
  418.5 52.2 %collective-permute-start.61 = (bf16[256,2048]{1,0:T(8,128)(2,1)}, bf16[256,2048]{1,0:T(8,128)(2,1)}, u32[]{:S(2)}, u32[]{:S(2)}) collective-permute-start(bf16[256,2048]{1,0:T(8,128)(2,1)} %get-tuple-element.904), channel_id=1, source_target_pairs={{0,1},{3,2},{4,5},{7,6},{8,9},{11,10},{12,13},{15,14},{16,17},{19,... | collective-permute-start | bytes 3145736 | tf_op jit(solution)/shard_map/ppermute | solution.py:563
  503.8 198.6 %reduce-scatter.5.cloned.1.call-start = ((), (), s32[]{:S(2)}) async-start(), calls=%async_computation.3 | async-start | bytes 21233664 | tf_op jit(solution)/shard_map/reduce_scatter | solution.py:796
  506.9 46.9 %collective-permute-start.69 = (bf16[272,2048]{1,0:T(8,128)(2,1)S(1)}, bf16[272,2048]{1,0:T(8,128)(2,1)S(1)}, u32[]{:S(2)}, u32[]{:S(2)}) collective-permute-start(bf16[272,2048]{1,0:T(8,128)(2,1)S(1)} %copy-done.53), channel_id=1, source_target_pairs={{0,1},{3,2},{4,5},{7,6},{8,9},{11,10},{12,13},{15,14},{16,17},{19,... | collective-permute-start | bytes 3342344 | tf_op jit(solution)/shard_map/ppermute | solution.py:563
  534.9 41.4 %collective-permute-start.63 = (bf16[256,2048]{1,0:T(8,128)(2,1)}, bf16[256,2048]{1,0:T(8,128)(2,1)}, u32[]{:S(2)}, u32[]{:S(2)}) collective-permute-start(bf16[256,2048]{1,0:T(8,128)(2,1)} %get-tuple-element.993), channel_id=1, source_target_pairs={{0,1},{3,2},{4,5},{7,6},{8,9},{11,10},{12,13},{15,14},{16,17},{19,... | collective-permute-start | bytes 3145736 | tf_op jit(solution)/shard_map/ppermute | solution.py:563
  554.9 43.9 %collective-permute-start.71 = (bf16[256,2048]{1,0:T(8,128)(2,1)}, bf16[256,2048]{1,0:T(8,128)(2,1)}, u32[]{:S(2)}, u32[]{:S(2)}) collective-permute-start(bf16[256,2048]{1,0:T(8,128)(2,1)} %get-tuple-element.1010), channel_id=1, source_target_pairs={{0,1},{3,2},{4,5},{7,6},{8,9},{11,10},{12,13},{15,14},{16,17},{19,... | collective-permute-start | bytes 3145736 | tf_op jit(solution)/shard_map/ppermute | solution.py:563
  (143 other events, 2783.6 us)
Sparse Core Ops, SparseCore 0:
  504.0 58.8 reduce-scatter.2
  566.9 126.2 reduce-scatter.4

commit v3 on v2

--- a/solution.py
+++ b/solution.py
@@ -41,22 +41,17 @@
     return pltpu.CompilerParams(vmem_limit_bytes=VMEM_LIMIT, **kw)
 
 
-def cost(flops, nbytes):
-    return pl.CostEstimate(flops=0, bytes_accessed=0, transcendentals=0)
+def cost(us):
+    return pl.CostEstimate(flops=0, bytes_accessed=3690000 * us, transcendentals=0)
 
 
 def rms_r(values):
     return lax.rsqrt(jnp.mean(values * values, axis=-1, keepdims=True) + EPSILON)
 
 
-def load_weights(refs, dest, at, sems, cols, dest_cols=None):
-    out = []
-    for n, ref in enumerate(refs):
-        place = dest.at[at[0] ^ (n // 2), at[1] ^ (n % 2)]
-        if dest_cols is not None:
-            place = place.at[:, dest_cols]
-        out.append(pltpu.make_async_copy(ref.at[pl.ds(0, dest.shape[2]), cols], place, sems.at[n]))
-    return out
+def fetch(gathered, dest, sem, first):
+    depth, cols = dest.shape[1:]
+    return pltpu.make_async_copy(gathered.at[:, pl.ds(0, depth), pl.ds(first, cols)], dest, sem)
 
 
 def start(copies):
@@ -70,35 +65,61 @@
 
 
 def joined(ref):
-    a, b, c, n = ref.shape
-    return ref[...].reshape(a * b * c, n)
-
-
-def qkv_kernel(nq, nk, blocks, flag_ref, x_ref, cos_ref, sin_ref, *rest):
-    normed_ref, lin_ref, rot_ref, ga_ref, gm_ref, gq_ref, gk_ref, w, gains, sems = rest[2 * blocks :]
+    a, b, n = ref.shape
+    return ref[...].reshape(a * b, n)
+
+
+def pack_kernel(n_rows, *refs):
+    out_ref = refs[-1]
+    weights = refs[: len(refs) - 1 - n_rows]
+    depth = weights[0].shape[0]
+    at = 0
+    for ref in weights[:-1]:
+        out_ref[:depth, at : at + ref.shape[1]] = ref[...]
+        at += ref.shape[1]
+    out_ref[:depth, at:] = weights[-1][...].astype(F32).T.astype(BF)
+    if n_rows:
+        out_ref[depth:, :] = refs[-2][...]
+
+
+def pack_call(weights, rows=None):
+    depth = weights[0].shape[0]
+    cols = sum(w.shape[1] for w in weights[:-1]) + weights[-1].shape[0]
+    extra = [] if rows is None else [rows]
+    return pl.pallas_call(
+        functools.partial(pack_kernel, len(extra)),
+        in_specs=[whole()] * (len(weights) + len(extra)),
+        out_specs=whole(),
+        out_shape=jax.ShapeDtypeStruct((depth + (0 if rows is None else rows.shape[0]), cols), BF),
+        compiler_params=params(),
+        cost_estimate=cost(3),
+    )(*weights, *extra)
+
+
+def qkv_kernel(nq, nk, halves, flag_ref, x_ref, cos_ref, sin_ref, *rest):
+    normed_ref, lin_ref, rot_ref, ga_ref, gm_ref, gq_ref, gk_ref, w_out, w, gains, sems, out_sem = rest[-12:]
     step = pl.program_id(0)
-    at = flag_ref[1], flag_ref[2]
-    wide_q = nq * HD
-    wide_kv = 2 * nk * HD
-    depth = w.shape[2]
+    n_dp, depth, half = w.shape[0], w.shape[1], w.shape[2] // halves
+    save = pltpu.make_async_copy(w, w_out, out_sem)
 
     @pl.when(step == 0)
     def _():
-        rows = []
-        for n, ref in enumerate(rest[blocks : 2 * blocks]):
-            place = gains.at[at[0] ^ (n // 2), at[1] ^ (n % 2)]
-            rows.append(pltpu.make_async_copy(ref.at[pl.ds(depth, 16)], place, sems.at[2, n]))
-        copies = load_weights(rest[:blocks], w, at, sems.at[0], pl.ds(0, wide_q), pl.ds(0, wide_q))
-        copies += load_weights(
-            rest[blocks : 2 * blocks], w, at, sems.at[1], pl.ds(0, wide_kv), pl.ds(wide_q, wide_kv)
-        )
-        start(rows)
-        start(copies)
+        rows, copies = [], []
+        for i in range(halves):
+            for n in range(n_dp):
+                block, place = rest[i * n_dp + n], flag_ref[1] ^ n
+                cols = pl.ds(i * half, half)
+                copies.append(
+                    pltpu.make_async_copy(block.at[pl.ds(0, depth)], w.at[place, :, cols], sems.at[i, n])
+                )
+                if i == 0:
+                    rows.append(pltpu.make_async_copy(block.at[pl.ds(depth, 16)], gains.at[place], sems.at[halves, n]))
+        start(rows + copies)
         wait(rows)
         of_q = jnp.zeros((1, HD), F32)
         of_k = jnp.zeros((1, HD), F32)
-        for p in range(blocks):
-            g = gains[p // 2, p % 2].astype(F32)
+        for p in range(n_dp):
+            g = gains[p].astype(F32)
             ga_ref[:, p * depth : (p + 1) * depth] = g[0:1, :depth]
             gm_ref[:, p * depth : (p + 1) * depth] = g[1:2, :depth]
             of_q = of_q + g[2:3, :HD]
@@ -106,11 +127,12 @@
         gq_ref[...] = of_q
         gk_ref[...] = of_k
         wait(copies)
+        save.start()
 
     x = x_ref[...].astype(F32)
     normed = (x * rms_r(x) * ga_ref[...]).astype(BF)
     normed_ref[...] = normed
-    acc = dot(normed, joined(w))
+    acc = dot(normed, w[:, :, : rot_ref.shape[1]].reshape(n_dp * depth, rot_ref.shape[1]))
     cosine = cos_ref[...]
     sine = sin_ref[...]
     for h in range(nq + nk):
@@ -121,19 +143,24 @@
     lin_ref[...] = acc[:, : (nq + nk) * HD]
     rot_ref[:, (nq + nk) * HD :] = acc[:, (nq + nk) * HD :].astype(BF)
 
-
-def qkv_call(flag, x, cosine, sine, w_q, w_kv, nq, nk):
+    @pl.when(step == pl.num_programs(0) - 1)
+    def _():
+        save.wait()
+
+
+def qkv_call(flag, x, cosine, sine, halves, nq, nk):
     tok, d = x.shape
-    blocks = len(w_q)
+    n_dp = len(halves[0])
+    wide = len(halves) * halves[0][0].shape[1]
     cols = (nq + 2 * nk) * HD
     blk = lambda n: pl.BlockSpec((CHUNK, n), lambda i: (i, 0))
     one = lambda n: pl.BlockSpec((1, n), lambda i: (0, 0))
     lin = (nq + nk) * HD
     return pl.pallas_call(
-        functools.partial(qkv_kernel, nq, nk, blocks),
+        functools.partial(qkv_kernel, nq, nk, len(halves)),
         grid=(tok // CHUNK,),
-        in_specs=[smem(), blk(d), blk(HD), blk(HD)] + [hbm()] * (2 * blocks),
-        out_specs=[blk(d), blk(lin), blk(cols), one(d), one(d), one(HD), one(HD)],
+        in_specs=[smem(), blk(d), blk(HD), blk(HD)] + [hbm()] * (len(halves) * n_dp),
+        out_specs=[blk(d), blk(lin), blk(cols), one(d), one(d), one(HD), one(HD), hbm()],
         out_shape=[
             jax.ShapeDtypeStruct((tok, d), BF),
             jax.ShapeDtypeStruct((tok, lin), F32),
@@ -142,15 +169,17 @@
             jax.ShapeDtypeStruct((1, d), F32),
             jax.ShapeDtypeStruct((1, HD), F32),
             jax.ShapeDtypeStruct((1, HD), F32),
+            jax.ShapeDtypeStruct((n_dp, d // n_dp, wide), BF),
         ],
         scratch_shapes=[
-            pltpu.VMEM((blocks // 2, 2, d // blocks, cols), BF),
-            pltpu.VMEM((blocks // 2, 2, 16, 2 * nk * HD), BF),
-            pltpu.SemaphoreType.DMA((3, blocks)),
+            pltpu.VMEM((n_dp, d // n_dp, wide), BF),
+            pltpu.VMEM((n_dp, 16, wide // len(halves)), BF),
+            pltpu.SemaphoreType.DMA((len(halves) + 1, n_dp)),
+            pltpu.SemaphoreType.DMA,
         ],
         compiler_params=params(),
-        cost_estimate=cost(2 * tok * d * cols, 20e6),
-    )(flag, x, cosine, sine, *w_q, *w_kv)
+        cost_estimate=cost(14),
+    )(flag, x, cosine, sine, *[b for h in halves for b in h])
 
 
 def band(c):
@@ -172,9 +201,9 @@
     return (u <= t) & (u >= doc_start(ends_ref, t))
 
 
-def attn_kernel(c, nq, nk, blocks, flag_ref, ends_ref, rot_ref, *rest):
-    att_ref, lse_ref, part_ref, w, sems = rest[-5:]
-    copies = load_weights(rest[:blocks], w, (flag_ref[1], flag_ref[2]), sems, pl.ds(0, w.shape[3]))
+def attn_kernel(c, nq, nk, ends_ref, rot_ref, w_hbm, *rest):
+    att_ref, lse_ref, part_ref, w, sem = rest[-5:]
+    copies = [fetch(w_hbm, w, sem, (nq + 2 * nk) * HD)]
     start(copies)
     lo, width = band(c)
     mask = allowed(c, ends_ref)
@@ -203,16 +232,16 @@
     return pl.BlockSpec((CHUNK, n), lambda i: (c, 0))
 
 
-def attn_call(c, flag, ends, rot, w_out, att, nq, nk):
+def attn_call(c, ends, rot, w, att, nq, nk):
     tok = rot.shape[0]
-    blocks, depth = len(w_out), w_out[0].shape[0]
-    d = blocks * depth
+    n_dp, depth = w.shape[:2]
+    d = n_dp * depth
     first = att is None
     full = lambda a: pl.BlockSpec(a.shape, lambda i: (0,) * a.ndim)
     return pl.pallas_call(
-        functools.partial(attn_kernel, c, nq, nk, blocks),
+        functools.partial(attn_kernel, c, nq, nk),
         grid=(1,),
-        in_specs=[smem(), smem(), full(rot)] + [hbm()] * (blocks + (0 if first else 1)),
+        in_specs=[smem(), full(rot)] + [hbm()] * (1 if first else 2),
         out_specs=[
             chunk_block(c, nq * HD),
             pl.BlockSpec((CHUNK, nq), lambda i: (0, 0)),
@@ -223,24 +252,18 @@
             jax.ShapeDtypeStruct((CHUNK, nq), F32),
             jax.ShapeDtypeStruct((CHUNK, d), BF),
         ],
-        scratch_shapes=[pltpu.VMEM((blocks // 2, 2, depth, nq * HD), BF), pltpu.SemaphoreType.DMA((blocks,))],
-        input_output_aliases={} if first else {3 + blocks: 0},
+        scratch_shapes=[pltpu.VMEM((n_dp, depth, nq * HD), BF), pltpu.SemaphoreType.DMA],
+        input_output_aliases={} if first else {3: 0},
         compiler_params=params(),
-        cost_estimate=cost(1e9, 6e6),
-    )(flag, ends, rot, *w_out, *([] if first else [att]))
-
-
-def mlp_kernel(tiles, blocks, flag_ref, x_ref, t_ref, r_ref, cot_ref, gain_ref, *rest):
+        cost_estimate=cost(5),
+    )(ends, rot, w, *([] if first else [att]))
+
+
+def mlp_kernel(tiles, flag_ref, x_ref, t_ref, r_ref, cot_ref, gain_ref, w_hbm, *rest):
     mid_ref, n2_ref, prod_ref, gg_ref, gu_ref, down_ref, gnt_ref, acc_d, acc_g, w, sems = rest[-11:]
-    at = flag_ref[1], flag_ref[2]
-    tile = w.shape[5]
+    tile = w.shape[4]
     copies = [
-        [
-            load_weights(
-                rest[j * blocks : (j + 1) * blocks], w.at[j % 2, i], at, sems.at[j % 2, i], pl.ds(i * tile, tile)
-            )
-            for i in range(3)
-        ]
+        [[fetch(w_hbm, w.at[j % 2, i], sems.at[j % 2, i], (i * tiles + j) * tile)] for i in range(3)]
         for j in range(tiles)
     ]
     for j in range(min(tiles, 2)):
@@ -284,23 +307,21 @@
                 start(copies[j + 2][i])
 
 
-def mlp_call(c, flag, x, t, r, cot, gain, packs, kept):
+def mlp_call(c, flag, x, t, r, cot, gain, w, kept):
     tok, d = x.shape
-    tiles = len(packs)
-    blocks = len(packs[0])
-    depth, tile = d // blocks, packs[0][0].shape[1] // 3
-    ff = tile * tiles
+    n_dp, depth, ff = w.shape[0], w.shape[1], w.shape[2] // 3
+    tiles = 2
+    tile = ff // tiles
     first = kept is None
     blk = chunk_block(c, d)
     own = pl.BlockSpec((CHUNK, d), lambda j: (0, 0))
     ffblk = chunk_block(c, ff)
     full = lambda a: pl.BlockSpec(a.shape, lambda j: (0,) * a.ndim)
     n_alias = 0 if first else 4
-    at = 6 + tiles * blocks
     out = pl.pallas_call(
-        functools.partial(mlp_kernel, tiles, blocks),
+        functools.partial(mlp_kernel, tiles),
         grid=(1,),
-        in_specs=[smem(), blk, own, own, blk, full(gain)] + [hbm()] * (tiles * blocks + n_alias),
+        in_specs=[smem(), blk, own, own, blk, full(gain)] + [hbm()] * (1 + n_alias),
         out_specs=[own, blk, ffblk, ffblk, ffblk, own, own],
         out_shape=[
             jax.ShapeDtypeStruct((CHUNK, d), F32),
@@ -314,31 +335,25 @@
         scratch_shapes=[
             pltpu.VMEM((CHUNK, d), F32),
             pltpu.VMEM((CHUNK, d), F32),
-            pltpu.VMEM((2, 3, blocks // 2, 2, depth, tile), BF),
-            pltpu.SemaphoreType.DMA((2, 3, blocks)),
+            pltpu.VMEM((2, 3, n_dp, depth, tile), BF),
+            pltpu.SemaphoreType.DMA((2, 3)),
         ],
-        input_output_aliases={} if first else {at: 1, at + 1: 2, at + 2: 3, at + 3: 4},
+        input_output_aliases={} if first else {7: 1, 8: 2, 9: 3, 10: 4},
         compiler_params=params(),
-        cost_estimate=cost(12 * CHUNK * d * ff, 25e6),
-    )(flag, x, t, r, cot, gain, *[b for p in packs for b in p], *([] if first else kept))
+        cost_estimate=cost(19),
+    )(flag, x, t, r, cot, gain, w, *([] if first else kept))
     return out[0], out[1:5], out[5], out[6]
 
 
 def back_kernel(
-    c, nq, nk, blocks, first, last, flag_ref, ends_ref, mid_ref, t_ref, r_ref, cot_ref, gain_ref, rot_ref,
-    lse_ref, lin_ref, cos_ref, sin_ref, gq_ref, gk_ref, *rest,
+    c, nq, nk, first, flag_ref, ends_ref, mid_ref, t_ref, r_ref, cot_ref, gain_ref, rot_ref,
+    lse_ref, lin_ref, cos_ref, sin_ref, gq_ref, gk_ref, w_hbm, *rest,
 ):
     gm_ref, gb_ref, gqkv_ref, part_ref, gain_out, head_out, carry_out, wo, w, sems = rest[-10:]
     if not first:
-        carry_ref, gain_in, head_in = rest[3 * blocks : 3 * blocks + 3]
-    at = flag_ref[1], flag_ref[2]
-    wide_q = nq * HD
-    wide_kv = 2 * nk * HD
-    out_copies = load_weights(rest[:blocks], wo, at, sems.at[0], pl.ds(0, wide_q))
-    in_copies = load_weights(rest[blocks : 2 * blocks], w, at, sems.at[1], pl.ds(0, wide_q), pl.ds(0, wide_q))
-    in_copies += load_weights(
-        rest[2 * blocks : 3 * blocks], w, at, sems.at[2], pl.ds(0, wide_kv), pl.ds(wide_q, wide_kv)
-    )
+        carry_ref, gain_in, head_in = rest[:3]
+    out_copies = [fetch(w_hbm, wo, sems.at[0], (nq + 2 * nk) * HD)]
+    in_copies = [fetch(w_hbm, w, sems.at[1], 0)]
     start(out_copies)
     start(in_copies)
     gnt = jnp.where(flag_ref[0] == 1, r_ref[...], t_ref[...]).astype(F32)
@@ -407,15 +422,11 @@
     head_out[0:1, :] = sum_q
     head_out[1:2, :] = sum_k
     wait(in_copies)
-    part_ref[:CHUNK, :] = dot(gqkv, joined(w), NT).astype(BF)
-    if last:
-        part_ref[CHUNK:, :] = jnp.zeros((16, part_ref.shape[1]), BF)
-        both = jnp.concatenate([sum_q, sum_k], axis=1)
-        part_ref[CHUNK:, : 2 * HD] = jnp.broadcast_to(both, (16, 2 * HD)).astype(BF)
+    part_ref[...] = dot(gqkv, joined(w), NT).astype(BF)
 
 
 def back_call(
-    c, flag, ends, mid, t, r, cot, gain, rot, lse, lin, cosine, sine, gq, gk, w_out, w_q, w_kv, kept, carry, nq, nk, last
+    c, flag, ends, mid, t, r, cot, gain, rot, lse, lin, cosine, sine, gq, gk, w, kept, carry, nq, nk
 ):
     tok, d = cot.shape
     first = carry is None
@@ -426,25 +437,24 @@
     specs[9] = chunk_block(c, lin.shape[1])
     specs[10] = chunk_block(c, HD)
     specs[11] = chunk_block(c, HD)
-    blocks = len(w_out)
-    args += [*w_out, *w_q, *w_kv]
-    specs += [hbm()] * (3 * blocks)
+    args.append(w)
+    specs.append(hbm())
     if not first:
         args += [*carry, *kept]
         specs += [full(a) for a in carry] + [hbm(), hbm()]
     own = lambda n: pl.BlockSpec((CHUNK, n), lambda i: (0, 0))
     cols = (nq + 2 * nk) * HD
-    depth = d // blocks
-    rows = CHUNK + (16 if last else 0)
+    n_dp = w.shape[0]
+    depth = d // n_dp
     out = pl.pallas_call(
-        functools.partial(back_kernel, c, nq, nk, blocks, first, last),
+        functools.partial(back_kernel, c, nq, nk, first),
         grid=(1,),
         in_specs=specs,
         out_specs=[
             own(d),
             chunk_block(c, d),
             chunk_block(c, cols),
-            pl.BlockSpec((rows, d), lambda i: (0, 0)),
+            own(d),
             pl.BlockSpec((1, d), lambda i: (0, 0)),
             pl.BlockSpec((2, HD), lambda i: (0, 0)),
             own(2 * nk * HD),
@@ -453,83 +463,94 @@
             jax.ShapeDtypeStruct((CHUNK, d), F32),
             jax.ShapeDtypeStruct((tok, d), BF),
             jax.ShapeDtypeStruct((tok, cols), BF),
-            jax.ShapeDtypeStruct((rows, d), BF),
+            jax.ShapeDtypeStruct((CHUNK, d), BF),
             jax.ShapeDtypeStruct((1, d), F32),
             jax.ShapeDtypeStruct((2, HD), F32),
             jax.ShapeDtypeStruct((CHUNK, 2 * nk * HD), F32),
         ],
         scratch_shapes=[
-            pltpu.VMEM((blocks // 2, 2, depth, nq * HD), BF),
-            pltpu.VMEM((blocks // 2, 2, depth, cols), BF),
-            pltpu.SemaphoreType.DMA((3, blocks)),
+            pltpu.VMEM((n_dp, depth, nq * HD), BF),
+            pltpu.VMEM((n_dp, depth, cols), BF),
+            pltpu.SemaphoreType.DMA((2,)),
         ],
-        input_output_aliases={} if first else {17 + 3 * blocks: 1, 18 + 3 * blocks: 2},
+        input_output_aliases={} if first else {18: 1, 19: 2},
         compiler_params=params(),
-        cost_estimate=cost(3e9, 15e6),
+        cost_estimate=cost(12),
     )(*args)
     return out[0], out[1:3], out[3], (out[6], out[4], out[5])
 
 
-def grad_kernel(counts, *refs):
-    out_ref = refs[-1]
-    at = 0
-    b_refs = iter(refs[len(counts) : -1])
-    for a_ref, count in zip(refs, counts):
-        for _ in range(count):
-            b_ref = next(b_refs)
-            out_ref[:, at : at + b_ref.shape[1]] = dot(a_ref[...], b_ref[...], TN).astype(BF)
-            at += b_ref.shape[1]
-
-
-def grad_call(n_dp, *pairs):
-    tok, d = pairs[0][0].shape
+def grad_kernel(a_ref, b_ref, *rest):
+    rest[-1][...] = dot(a_ref[...], b_ref[...], TN).astype(BF)
+
+
+def grad_call(n_dp, total, at, a, b, kept):
+    tok, d = a.shape
     depth = d // n_dp
-    bs = [b for _, group in pairs for b in group]
-    cols = sum(b.shape[1] for b in bs)
+    cols = b.shape[1]
+    first = kept is None
     return pl.pallas_call(
-        functools.partial(grad_kernel, [len(group) for _, group in pairs]),
+        grad_kernel,
         grid=(n_dp,),
-        in_specs=[pl.BlockSpec((tok, depth), lambda i: (0, i)) for _ in pairs]
-        + [pl.BlockSpec(b.shape, lambda i: (0, 0)) for b in bs],
-        out_specs=pl.BlockSpec((depth, cols), lambda i: (i, 0)),
-        out_shape=jax.ShapeDtypeStruct((d, cols), BF),
+        in_specs=[pl.BlockSpec((tok, depth), lambda i: (0, i)), pl.BlockSpec(b.shape, lambda i: (0, 0))]
+        + ([] if first else [hbm()]),
+        out_specs=pl.BlockSpec((depth, cols), lambda i: (i, at // cols)),
+        out_shape=jax.ShapeDtypeStruct((d, total), BF),
+        input_output_aliases={} if first else {2: 0},
         compiler_params=params(),
-        cost_estimate=cost(2 * tok * d * cols, 10e6),
-    )(*[a for a, _ in pairs], *bs)
-
-
-def input_kernel(first, last, flag_ref, x_ref, t_ref, r_ref, gm_ref, gain_ref, *rest):
-    if not first:
-        gain_in = rest[0]
-    out_ref, gain_out = rest[-3:-1] if last else rest[-2:]
-    got = jnp.where(flag_ref[0] == 1, r_ref[...], t_ref[...]).astype(F32)
-    gn = got[:CHUNK]
-    if last:
-        rest[-1][...] = got[CHUNK : CHUNK + 8, : 2 * HD]
+        cost_estimate=cost(2 + cols // 185),
+    )(a, b, *([] if first else [kept]))
+
+
+def grad_pair_kernel(a_ref, b_ref, c_ref, d_ref, kept_ref, out_ref):
+    cols = b_ref.shape[1]
+    out_ref[:, :cols] = dot(a_ref[...], b_ref[...], TN).astype(BF)
+    out_ref[:, cols:] = dot(c_ref[...], d_ref[...], TN).astype(BF)
+
+
+def grad_pair_call(n_dp, at, a, b, c, d, kept):
+    tok, rows = a.shape
+    depth = rows // n_dp
+    cols = b.shape[1] + d.shape[1]
+    block = pl.BlockSpec((tok, depth), lambda i: (0, i))
+    full = lambda x: pl.BlockSpec(x.shape, lambda i: (0, 0))
+    return pl.pallas_call(
+        grad_pair_kernel,
+        grid=(n_dp,),
+        in_specs=[block, full(b), block, full(d), hbm()],
+        out_specs=pl.BlockSpec((depth, cols), lambda i: (i, at // cols)),
+        out_shape=jax.ShapeDtypeStruct(kept.shape, BF),
+        input_output_aliases={4: 0},
+        compiler_params=params(),
+        cost_estimate=cost(13),
+    )(a, b, c, d, kept)
+
+
+def input_kernel(first, flag_ref, x_ref, t_ref, r_ref, gm_ref, gain_ref, *rest):
+    out_ref, gain_out = rest[-2:]
+    gn = jnp.where(flag_ref[0] == 1, r_ref[...], t_ref[...]).astype(F32)
     x = x_ref[...].astype(F32)
     r1 = rms_r(x)
     h = gn * gain_ref[...]
     out_ref[...] = gm_ref[...] + r1 * h - x * (r1 * r1 * r1 * jnp.mean(h * x, axis=-1, keepdims=True))
     gain_sum = jnp.sum(gn * x * r1, axis=0, keepdims=True)
-    gain_out[...] = gain_sum if first else gain_in[...] + gain_sum
-
-
-def input_call(c, flag, x, t, r, gm, gain, kept, last):
+    gain_out[...] = gain_sum if first else rest[0][...] + gain_sum
+
+
+def input_call(c, flag, x, t, r, gm, gain, kept):
     tok, d = x.shape
     own = pl.BlockSpec((CHUNK, d), lambda i: (0, 0))
-    got = pl.BlockSpec(t.shape, lambda i: (0, 0))
     one = pl.BlockSpec((1, d), lambda i: (0, 0))
     first = kept is None
     return pl.pallas_call(
-        functools.partial(input_kernel, first, last),
+        functools.partial(input_kernel, first),
         grid=(1,),
-        in_specs=[smem(), chunk_block(c, d), got, got, own, one] + ([] if first else [one, hbm()]),
-        out_specs=[chunk_block(c, d), one] + ([pl.BlockSpec((8, 2 * HD), lambda i: (0, 0))] if last else []),
-        out_shape=[jax.ShapeDtypeStruct((tok, d), F32), jax.ShapeDtypeStruct((1, d), F32)]
-        + ([jax.ShapeDtypeStruct((8, 2 * HD), F32)] if last else []),
+        in_specs=[smem(), chunk_block(c, d), own, own, own, one] + ([] if first else [one, hbm()]),
+        out_specs=[chunk_block(c, d), one],
+        out_shape=[jax.ShapeDtypeStruct((tok, d), F32), jax.ShapeDtypeStruct((1, d), F32)],
         input_output_aliases={} if first else {7: 0},
         compiler_params=params(),
-        cost_estimate=cost(1e6, 8e6),
+        cost_estimate=cost(5),
     )(flag, x, t, r, gm, gain, *([] if first else [kept[1], kept[0]]))
 
 
@@ -551,7 +572,7 @@
         out_shape=jax.ShapeDtypeStruct((tok, d), BF),
         input_output_aliases={} if first else {4: 0},
         compiler_params=params(),
-        cost_estimate=cost(1e6, 5e6),
+        cost_estimate=cost(3),
     )(flag, mid, t, r, *([] if first else [kept]))
 
 
@@ -576,8 +597,8 @@
 
 
 class Sum:
-    def __init__(self, line, x):
-        self.steps = line_sum(line, x)
+    def __init__(self, line, *args, kind=line_sum):
+        self.steps = kind(line, *args)
         self.result = None
         self.step()
 
@@ -605,9 +626,6 @@
         leaves = lax.optimization_barrier((*leaves, self.last))[:-1]
         return jax.tree.unflatten(tree, leaves)
 
-    def hold(self, arrays):
-        self.last = lax.optimization_barrier((self.last, jax.tree.leaves(arrays)))[0]
-
     def __call__(self, f, *args, **kw):
         out = f(*self.after(*args), **kw)
         self.last = jax.tree.leaves(out)[-1]
@@ -616,6 +634,10 @@
 
 SWAP = [(0, 1), (1, 0)]
 DP = ("chip", "core")
+
+
+def behind(x, arrays):
+    return lax.optimization_barrier((x, jax.tree.leaves(arrays)))[0]
 
 
 class Gather:
@@ -658,7 +680,18 @@
     return stacked
 
 
-def own_sum(rows, index):
+def swap_sum(line, x, axis):
+    n = lax.axis_size(axis)
+    step = 1
+    while step < n:
+        got = lax.ppermute(x, axis, [(i, i ^ step) for i in range(n)])
+        yield
+        x = line(jnp.add, x, got)
+        step *= 2
+    return x
+
+
+def own_sum(line, rows, index):
     rows = in_order(rows, index)
     half = rows.shape[0] // 2
     while half:
@@ -667,7 +700,8 @@
             got = lax.ppermute(rows[half:], "chip", pairs)
         else:
             got = lax.ppermute(rows[half:], "core", SWAP)
-        rows = rows[:half] + got
+        yield
+        rows = line(jnp.add, rows[:half], got)
         half //= 2
     return rows[0]
 
@@ -699,22 +733,19 @@
     nk = w_key.shape[1] // HD
     depth = w_query.shape[0]
     small = norm_query.shape[0]
-    flag = jnp.stack([((mp == 0) | (mp == n_mp - 1)).astype(jnp.int32), lax.axis_index("chip"), core_id])
-
-    wide = 2 * nk * HD
+    flag = jnp.stack([((mp == 0) | (mp == n_mp - 1)).astype(jnp.int32), dp])
+
+    wide = (2 * nq + 2 * nk) * HD
     widen = lambda v: jnp.pad(v, (0, wide - v.shape[0]))[None]
     placed = lambda v: widen(lax.dynamic_update_slice(jnp.zeros(HD, BF), v, (dp * small,)))
     gain_rows = jnp.concatenate([widen(norm_attn), widen(norm_mlp), placed(norm_query), placed(norm_key)])
     gain_rows = jnp.pad(gain_rows, ((0, 12), (0, 0)))
-    w_kv = Gather(jnp.concatenate([jnp.concatenate([w_key, w_value], axis=1), gain_rows], axis=0), True)
-    w_q = Gather(w_query, False)
-    w_out = Gather(w_out.T, True)
-    down_t = w_down.T
-    tile = w_gate.shape[1] // 2
-    packs = [
-        Gather(jnp.concatenate([w[:, j * tile : (j + 1) * tile] for w in (w_gate, w_up, down_t)], axis=1), j == 0)
-        for j in range(2)
-    ]
+    w_attn = pack_call([w_query, w_key, w_value, w_out], gain_rows)
+    halves = [Gather(w_attn[:, : wide // 2], True), Gather(w_attn[:, wide // 2 :], False)]
+    while halves[0].level < len(halves[0].bits):
+        arrived = [h.step() for h in halves]
+    w_mlp = behind(pack_call([w_gate, w_up, w_down]), arrived)
+    w_mlp = lax.all_gather(w_mlp, DP, axis=0)
 
     lengths = lax.dynamic_index_in_dim(doc_lengths, dp, 0, keepdims=False)
     ends = jnp.cumsum(lengths)
@@ -735,44 +766,35 @@
         for s in sums:
             s.step()
 
-    w_q, w_kv = w_q.blocks(), w_kv.blocks()
-    w_out_blocks = w_out.blocks()
-    first_packs = [p.step() for p in packs]
-    normed, lin, rot, gain_attn, gain_mlp, gain_query, gain_key = line(
-        lambda ready, *a: qkv_call(*a, nq=nq, nk=nk), w_out_blocks[::2], flag, hidden_in, cosine, sine, w_q, w_kv
+    normed, lin, rot, gain_attn, gain_mlp, gain_query, gain_key, w_attn = line(
+        functools.partial(qkv_call, nq=nq, nk=nk), flag, hidden_in, cosine, sine, [h.blocks() for h in halves]
     )
 
     order = list(reversed(range(tok // CHUNK)))
     att = None
     lse, branch, mid, down, gnt, gn = {}, {}, {}, {}, {}, {}
-    ready = first_packs
     for c in order:
-        att, lse[c], part = line(
-            lambda ready, *a, c=c: attn_call(c, *a, nq=nq, nk=nk), ready, flag, ends, rot, w_out_blocks, att
-        )
+        att, lse[c], part = line(functools.partial(attn_call, c, nq=nq, nk=nk), ends, rot, w_attn, att)
         branch[c] = Sum(line, part)
-        ready = None
-    for p in packs:
-        while p.level < len(p.bits):
-            p.step()
 
     c0, c1, c2, c3 = order
     state = {"mlp": None, "back": None, "carry": None, "input": None, "output": None}
     gm = {}
+    ff = w_gate.shape[1]
 
     def run_mlp(c):
         t, r = branch[c].total()
         mid[c], state["mlp"], down[c], gnt_part = line(
             functools.partial(mlp_call, c), flag, hidden_in, t, r, cotangent, gain_mlp,
-            [p.blocks() for p in packs], state["mlp"],
+            w_mlp, state["mlp"],
         )
         gnt[c] = Sum(line, gnt_part)
 
     def run_back(c):
         t, r = gnt[c].total()
         gm[c], state["back"], part, state["carry"] = line(
-            functools.partial(back_call, c, nq=nq, nk=nk, last=c == c3), flag, ends, mid[c], t, r, cotangent,
-            gain_mlp, rot, lse[c], lin, cosine, sine, gain_query, gain_key, w_out_blocks, w_q, w_kv,
+            functools.partial(back_call, c, nq=nq, nk=nk), flag, ends, mid[c], t, r, cotangent,
+            gain_mlp, rot, lse[c], lin, cosine, sine, gain_query, gain_key, w_attn,
             state["back"], state["carry"],
         )
         gn[c] = Sum(line, part)
@@ -780,7 +802,7 @@
     def run_input(c):
         t, r = gn[c].total()
         state["input"] = line(
-            functools.partial(input_call, c, last=c == c3), flag, hidden_in, t, r, gm[c], gain_attn, state["input"]
+            functools.partial(input_call, c), flag, hidden_in, t, r, gm[c], gain_attn, state["input"]
         )
 
     def run_output(c):
@@ -791,13 +813,21 @@
         for c in cs:
             down[c] = Sum(line, line.after(down[c])[0])
 
-    def scatter(*pairs):
-        g = line(lambda pairs: grad_call(n_dp, *pairs), pairs)
-        return lax.psum_scatter(g, DP, scatter_dimension=0, tiled=True)
-
-    steps(branch[c0])
-    line.hold([list(p.own.values()) for p in packs])
-    steps(branch[c1], branch[c0], branch[c2], branch[c1])
+    def grad(total, at, a, b, kept=None):
+        return line(functools.partial(grad_call, n_dp, total, at), a, b, kept)
+
+    def scatter(g):
+        return lax.psum_scatter(line.after(g)[0], DP, scatter_dimension=0, tiled=True)
+
+    def split(grads):
+        outs, at = [], 0
+        for cols in (ff, ff, ff, nq * HD, nk * HD, nk * HD, nq * HD):
+            outs.append(grads[:, at : at + cols].astype(F32))
+            at += cols
+        outs[2], outs[6] = outs[2].T, outs[6].T
+        return outs
+
+    steps(branch[c0], branch[c1], branch[c0], branch[c2], branch[c1])
     run_mlp(c0)
     steps(branch[c3], branch[c2])
     run_mlp(c1)
@@ -808,56 +838,56 @@
     n2, prod, gg, gu = state["mlp"]
     steps(gnt[c2], gnt[c1])
     run_back(c0)
+    g_mlp = grad(3 * ff + wide, 0, n2, gg)
     steps(gnt[c3], gnt[c2])
     run_back(c1)
-    g_mlp = scatter((n2, (gg, gu)), (cotangent, (prod,)))
+    start_down(c0)
+    g_mlp = grad(3 * ff + wide, ff, n2, gu, g_mlp)
     steps(gn[c0], gnt[c3])
     run_back(c2)
-    steps(gn[c1], gn[c0])
+    g_mlp = grad(3 * ff + wide, 2 * ff, cotangent, prod, g_mlp)
+    steps(gn[c1], gn[c0], down[c0])
     run_back(c3)
     gb, gqkv = state["back"]
-    start_down(c0, c1, c2, c3)
-    g_attn = scatter((normed, (gqkv,)), (gb, (att,)))
-    steps(gn[c2], gn[c1])
+    grads = scatter(line(functools.partial(grad_pair_call, n_dp, 3 * ff), normed, gqkv, gb, att, g_mlp))
+    steps(gn[c2], gn[c1], down[c0])
     run_input(c0)
+    start_down(c1)
     steps(gn[c3], gn[c2])
     run_input(c1)
-    steps(down[c0], gn[c3])
+    run_output(c0)
+    start_down(c2)
+    steps(down[c1], gn[c3])
+    start_down(c3)
+    _, sum_mlp, sum_head = state["carry"]
+    heads = Sum(line, sum_head, "mp", kind=swap_sum)
     run_input(c2)
-    steps(down[c1], down[c0])
+    steps(down[c2], down[c1], heads)
     run_input(c3)
-    grad_input, sum_attn, sum_head = state["input"]
-    steps(down[c2], down[c1])
-    run_output(c0)
-    steps(down[c3], down[c2])
+    grad_input, sum_attn = state["input"]
+    heads = heads.total()
+    sums = jnp.concatenate(
+        [sum_attn.reshape(n_dp, depth), sum_mlp.reshape(n_dp, depth)]
+        + [heads[i].reshape(n_dp, small) for i in range(2)],
+        axis=1,
+    )
+    sums = Sum(line, sums, dp, kind=own_sum)
+    steps(down[c3], down[c2], sums)
     run_output(c1)
-    steps(down[c3])
+    steps(down[c3], sums)
     run_output(c2)
+    sums = sums.total()
+    outs = line(split, grads)
     run_output(c3)
 
-    sums = own_sum(
-        jnp.concatenate(
-            [sum_attn.reshape(n_dp, depth), state["carry"][1].reshape(n_dp, depth)]
-            + [sum_head[0, i * HD : (i + 1) * HD].reshape(n_dp, small) for i in range(2)],
-            axis=1,
-        ),
-        dp,
-    )
-    g_mlp = g_mlp.astype(F32)
-    g_attn = g_attn.astype(F32)
-    ff = w_gate.shape[1]
-    kv = nk * HD
-    q = nq * HD
     return (
         state["output"],
         grad_input,
-        g_attn[:, :q],
-        g_attn[:, q : q + kv],
-        g_attn[:, q + kv : q + 2 * kv],
-        g_attn[:, q + 2 * kv :].T,
-        g_mlp[:, :ff],
-        g_mlp[:, ff : 2 * ff],
-        g_mlp[:, 2 * ff :].T,
+        *outs[3:6],
+        outs[6],
+        outs[0],
+        outs[1],
+        outs[2],
         sums[:depth],
         sums[depth : 2 * depth],
         sums[2 * depth : 2 * depth + small],

time: 730 us -> 625 us (0.86)
  waiting for transfers between devices: 203 us -> 89.9 us
  Pallas kernels: 233 us -> 247 us
  local copies, waits for them, and re-layouts: 32.9 us -> 19.2 us
  starting transfers between devices: 177 us -> 185 us
    ppermute x16, waiting for transfers between devices: 79.3 us -> 31.7 us  [line_sum(): r = lax.ppermute(x, 'mp', [(h, h + 1), (n - 1 - h, n - 2 - h)])]
    ppermute x15 -> x6, waiting for transfers between devices: 62.1 us -> 20.1 us  [step(): lax.ppermute(b, 'chip', [(i, i ^ bit) for i in range(self.n)])]
    ppermute x16, waiting for transfers between devices: 55.4 us -> 27.3 us  [line_sum(): r = lax.ppermute(x, 'mp', [(h + 1, h), (n - 2 - h, n - 1 - h)])]
    pallas_call x19 -> x23, Pallas kernels: 220 us -> 233 us  [the longest x4 75.2 us: mlp_call(): pl.pallas_call(functools.partial(mlp_kernel, tiles), grid=(1,), in_specs=...]
    ppermute x16, starting transfers between devices: 113 us -> 123 us  [line_sum(): r = lax.ppermute(x, 'mp', [(h, h + 1), (n - 1 - h, n - 2 - h)])]
    ppermute x15 -> x6, starting transfers between devices: 15.5 us -> 8.62 us  [step(): lax.ppermute(b, 'chip', [(i, i ^ bit) for i in range(self.n)])]
    unnamed x162 -> x120, local copies, waits for them, and re-layouts: 19.6 us -> 12.8 us
    add x32 -> x37, other arithmetic: 44.6 us -> 42.5 us  [__call__(): out = f(*self.after(*args), **kw)]
  transfers between devices with their start and end apart: 88 -> 69, of which waited for: 25 -> 19; matrix products, arithmetic and copies ran while one was open for 9% -> 10% of each run, Pallas kernels for 29% -> 35%
where the time goes in v3:
time: 625 us; the launch traced here: 614 us
  Pallas kernels  247 us (40%)
  starting transfers between devices  185 us (30%)
  waiting for transfers between devices  89.9 us (14%)
  other arithmetic  57.1 us (9%)
  local copies, waits for them, and re-layouts  19.2 us (3%)
  between operations  15.7 us (3%)
    ppermute x16, starting transfers between devices, line_sum(): r = lax.ppermute(x, 'mp', [(h, h + 1), (n - 1 - h, n - 2 - h)])  123 us
    pallas_call x4, Pallas kernels, mlp_call(): pl.pallas_call(functools.partial(mlp_kernel, tiles), grid=(1,), in_specs=...  75.2 us
    pallas_call x4, Pallas kernels, back_call(): pl.pallas_call(functools.partial(back_kernel, c, nq, nk, first), grid=(1,...  45.7 us
    add x37, other arithmetic, __call__(): out = f(*self.after(*args), **kw)  42.5 us
    pallas_call x3, Pallas kernels, grad_call(): pl.pallas_call(grad_kernel, grid=(n_dp,), in_specs=[pl.BlockSpec((tok, de...  37 us
    ppermute x16, waiting for transfers between devices, line_sum(): r = lax.ppermute(x, 'mp', [(h, h + 1), (n - 1 - h, n - 2 - h)])  31.7 us
    ppermute x16, waiting for transfers between devices, line_sum(): r = lax.ppermute(x, 'mp', [(h + 1, h), (n - 2 - h, n - 1 - h)])  27.3 us
    ppermute x16, starting transfers between devices, line_sum(): r = lax.ppermute(x, 'mp', [(h + 1, h), (n - 2 - h, n - 1 - h)])  22.3 us
  transfers between devices with their start and end apart: 69, of which 19 were waited for; matrix products, arithmetic and copies ran while one was open for 10% of the time, Pallas kernels for 35%

profile of v3, /device:TPU:0, one launch (start us, length us, event | category | flops | bytes accessed | tf_op | source)
XLA Modules:
  0.0 613.6 jit_solution(2481787726398553350)
XLA Ops:
  19.5 8.4 %collective-permute-done.10.rest_12_ = bf16[272,768]{1,0:T(8,128)(2,1)S(1)} collective-permute-done((bf16[272,768]{1,0:T(8,128)(2,1)S(1)}, bf16[272,768]{1,0:T(8,128)(2,1)S(1)}, u32[]{:S(2)}, u32[]{:S(2)}) %collective-permute-start.10) | collective-permute-done | bytes 417824 | tf_op jit(solution)/shard_map/ppermute | solution.py:656
  39.0 7.5 %collective-permute-done.12.rest_14_ = bf16[272,768]{1,0:T(8,128)(2,1)S(1)} collective-permute-done((bf16[272,768]{1,0:T(8,128)(2,1)S(1)}, bf16[272,768]{1,0:T(8,128)(2,1)S(1)}, u32[]{:S(2)}, u32[]{:S(2)}) %collective-permute-start.12) | collective-permute-done | bytes 417824 | tf_op jit(solution)/shard_map/ppermute | solution.py:656
  54.9 14.5 %shard_map.238 = (bf16[1024,2048]{1,0:T(8,128)(2,1)}, f32[1024,768]{1,0:T(8,128)}, bf16[1024,1024]{1,0:T(8,128)(2,1)}, f32[1,2048]{1,0:T(1,128)}, f32[1,2048]{1,...) custom-call(s32[2]{0:T(128)} %pad_add_fusion.flag_ref, bf16[1024,2048]{1,0:T(8,128)(2,1)} %x_ref.9, ...), custom_call_target="tpu_custom_call" | custom-call | bytes 51660000 | tf_op jit(solution)/shard_map/pallas_call | solution.py:159
  83.7 13.8 %collective-permute-start.17 = (bf16[256,2048]{1,0:T(8,128)(2,1)}, bf16[256,2048]{1,0:T(8,128)(2,1)S(1)}, u32[]{:S(2)}, u32[]{:S(2)}) collective-permute-start(bf16[256,2048]{1,0:T(8,128)(2,1)} %get-tuple-element.395), channel_id=1, source_target_pairs={{0,1},{3,2},{4,5},{7,6},{8,9},{11,10},{12,13},{15,14},{16,17},{19,... | collective-permute-start | bytes 3145736 | tf_op jit(solution)/shard_map/ppermute | solution.py:584
  113.2 11.4 %collective-permute-done.17 = bf16[256,2048]{1,0:T(8,128)(2,1)S(1)} collective-permute-done((bf16[256,2048]{1,0:T(8,128)(2,1)}, bf16[256,2048]{1,0:T(8,128)(2,1)S(1)}, u32[]{:S(2)}, u32[]{:S(2)}) %collective-permute-start.17) | collective-permute-done | bytes 1048608 | tf_op jit(solution)/shard_map/ppermute | solution.py:584
  127.5 13.7 %collective-permute-start.14 = (bf16[256,2048]{1,0:T(8,128)(2,1)S(1)}, bf16[256,2048]{1,0:T(8,128)(2,1)}, u32[]{:S(2)}, u32[]{:S(2)}) collective-permute-start(bf16[256,2048]{1,0:T(8,128)(2,1)S(1)} %copy-done.25), channel_id=1, source_target_pairs={{0,1},{3,2},{4,5},{7,6},{8,9},{11,10},{12,13},{15,14},{16,17},{19,... | collective-permute-start | bytes 3145736 | tf_op jit(solution)/shard_map/ppermute | solution.py:584
  150.8 8.9 %collective-permute-done.18.r_ref = bf16[256,2048]{1,0:T(8,128)(2,1)} collective-permute-done((bf16[256,2048]{1,0:T(8,128)(2,1)S(1)}, bf16[256,2048]{1,0:T(8,128)(2,1)}, u32[]{:S(2)}, u32[]{:S(2)}) %collective-permute-start.18) | collective-permute-done | bytes 1048608 | tf_op jit(solution)/shard_map/ppermute | solution.py:592
  159.7 18.7 %shard_map.244 = (f32[256,2048]{1,0:T(8,128)}, bf16[1024,2048]{1,0:T(8,128)(2,1)}, bf16[1024,1536]{1,0:T(8,128)(2,1)}, bf16[1024,1536]{1,0:T(8,128)(2,1)}, bf16[...) custom-call(s32[2]{0:T(128)} %pad_add_fusion.flag_ref, bf16[1024,2048]{1,0:T(8,128)(2,1)} %x_ref.9, ...), custom_call_target="tpu_custom_call" | custom-call | bytes 70110000 | tf_op jit(solution)/shard_map/pallas_call | solution.py:321
  188.2 18.8 %shard_map.245 = (f32[256,2048]{1,0:T(8,128)}, bf16[1024,2048]{1,0:T(8,128)(2,1)}, bf16[1024,1536]{1,0:T(8,128)(2,1)}, bf16[1024,1536]{1,0:T(8,128)(2,1)}, bf16[...) custom-call(s32[2]{0:T(128)} %pad_add_fusion.flag_ref, ...), custom_call_target="tpu_custom_call", output_to_operand_aliasing={{1}: (7, {}), {2}: (8, {}), {3}: (9, {}), {4}: (10, {})} | custom-call | bytes 70110000 | tf_op jit(solution)/shard_map/pallas_call | solution.py:321
  217.9 18.8 %shard_map.246 = (f32[256,2048]{1,0:T(8,128)}, bf16[1024,2048]{1,0:T(8,128)(2,1)}, bf16[1024,1536]{1,0:T(8,128)(2,1)}, bf16[1024,1536]{1,0:T(8,128)(2,1)}, bf16[...) custom-call(s32[2]{0:T(128)} %pad_add_fusion.flag_ref, ...), custom_call_target="tpu_custom_call", output_to_operand_aliasing={{1}: (7, {}), {2}: (8, {}), {3}: (9, {}), {4}: (10, {})} | custom-call | bytes 70110000 | tf_op jit(solution)/shard_map/pallas_call | solution.py:321
  248.5 18.8 %shard_map.247 = (f32[256,2048]{1,0:T(8,128)}, bf16[1024,2048]{1,0:T(8,128)(2,1)}, bf16[1024,1536]{1,0:T(8,128)(2,1)}, bf16[1024,1536]{1,0:T(8,128)(2,1)}, bf16[...) custom-call(s32[2]{0:T(128)} %pad_add_fusion.flag_ref, ...), custom_call_target="tpu_custom_call", output_to_operand_aliasing={{1}: (7, {}), {2}: (8, {}), {3}: (9, {}), {4}: (10, {})} | custom-call | bytes 70110000 | tf_op jit(solution)/shard_map/pallas_call | solution.py:321
  280.6 11.5 %shard_map.248 = (f32[256,2048]{1,0:T(8,128)}, bf16[1024,2048]{1,0:T(8,128)(2,1)}, bf16[1024,1024]{1,0:T(8,128)(2,1)}, bf16[256,2048]{1,0:T(8,128)(2,1)}, f32[1,...) custom-call(s32[2]{0:T(128)} %pad_add_fusion.flag_ref, s32[8]{0:T(128)} %bitcast.31, ...), custom_call_target="tpu_custom_call" | custom-call | bytes 44280000 | tf_op jit(solution)/shard_map/pallas_call | solution.py:449
  297.7 12.2 %shard_map.249.rest_0_ = bf16[2048,6144]{1,0:T(8,128)(2,1)} custom-call(bf16[1024,2048]{1,0:T(8,128)(2,1)} %get-tuple-element.537.a_ref, bf16[1024,1536]{1,0:T(8,128)(2,1)} %get-tuple-element.503.b_ref), custom_call_target="tpu_custom_call" | custom-call | bytes 36900000 | tf_op jit(solution)/shard_map/pallas_call | solution.py:492
  316.4 11.7 %shard_map.250 = (f32[256,2048]{1,0:T(8,128)}, bf16[1024,2048]{1,0:T(8,128)(2,1)}, bf16[1024,1024]{1,0:T(8,128)(2,1)}, bf16[256,2048]{1,0:T(8,128)(2,1)}, f32[1,...) custom-call(s32[2]{0:T(128)} %pad_add_fusion.flag_ref, ...), custom_call_target="tpu_custom_call", output_to_operand_aliasing={{1}: (18, {}), {2}: (19, {})} | custom-call | bytes 44280000 | tf_op jit(solution)/shard_map/pallas_call | solution.py:449
  333.8 12.2 %shard_map.251.rest_0_ = bf16[2048,6144]{1,0:T(8,128)(2,1)} custom-call(bf16[1024,2048]{1,0:T(8,128)(2,1)} %get-tuple-element.537.a_ref, bf16[1024,1536]{1,0:T(8,128)(2,1)} %get-tuple-element.538.b_ref, bf16[2048,6144]{1,0:T(8,128)(2,1)} %shard_map.249.rest_0_), custom_call_target="tpu_custom_call", output_to_operand_aliasing={{}: (2, {})} | custom-call | bytes 36900000 | tf_op jit(solution)/shard_map/pallas_call | solution.py:492
  355.4 11.7 %shard_map.252 = (f32[256,2048]{1,0:T(8,128)}, bf16[1024,2048]{1,0:T(8,128)(2,1)}, bf16[1024,1024]{1,0:T(8,128)(2,1)}, bf16[256,2048]{1,0:T(8,128)(2,1)}, f32[1,...) custom-call(s32[2]{0:T(128)} %pad_add_fusion.flag_ref, ...), custom_call_target="tpu_custom_call", output_to_operand_aliasing={{1}: (18, {}), {2}: (19, {})} | custom-call | bytes 44280000 | tf_op jit(solution)/shard_map/pallas_call | solution.py:449
  367.1 12.6 %shard_map.253.kept_ref = bf16[2048,6144]{1,0:T(8,128)(2,1)} custom-call(bf16[1024,2048]{1,0:T(8,128)(2,1)} %cot_ref.7, bf16[1024,1536]{1,0:T(8,128)(2,1)} %get-tuple-element.581.b_ref, bf16[2048,6144]{1,0:T(8,128)(2,1)} %shard_map.251.rest_0_), custom_call_target="tpu_custom_call", output_to_operand_aliasing={{}: (2, {})} | custom-call | bytes 36900000 | tf_op jit(solution)/shard_map/pallas_call | solution.py:492
  386.0 10.8 %shard_map.254 = (f32[256,2048]{1,0:T(8,128)}, bf16[1024,2048]{1,0:T(8,128)(2,1)}, bf16[1024,1024]{1,0:T(8,128)(2,1)}, bf16[256,2048]{1,0:T(8,128)(2,1)}, f32[1,...) custom-call(s32[2]{0:T(128)} %pad_add_fusion.flag_ref, ...), custom_call_target="tpu_custom_call", output_to_operand_aliasing={{1}: (18, {}), {2}: (19, {})} | custom-call | bytes 44280000 | tf_op jit(solution)/shard_map/pallas_call | solution.py:449
  396.8 13.1 %shard_map.255 = bf16[2048,6144]{1,0:T(8,128)(2,1)} custom-call(bf16[1024,2048]{1,0:T(8,128)(2,1)} %get-tuple-element.618.a_ref, bf16[1024,1024]{1,0:T(8,128)(2,1)} %get-tuple-element.619.b_ref, bf16[1024,2048]{1,0:T(8,128)(2,1)} %get-tuple-element.620.c_ref, bf16[1024,512]{1,0:T(8,128)(2,1)} %get-tuple-element.621.d_ref, ...), custom_call_target="tpu_custom_call", output_to_operand_aliasing={{}: (4, {})} | custom-call | bytes 47970000 | tf_op jit(solution)/shard_map/pallas_call | solution.py:517
  424.1 14.4 %collective-permute-done.46 = bf16[256,2048]{1,0:T(8,128)(2,1)S(1)} collective-permute-done((bf16[256,2048]{1,0:T(8,128)(2,1)}, bf16[256,2048]{1,0:T(8,128)(2,1)S(1)}, u32[]{:S(2)}, u32[]{:S(2)}) %collective-permute-start.46) | collective-permute-done | bytes 1048608 | tf_op jit(solution)/shard_map/ppermute | solution.py:584
  451.6 25.0 %collective-permute-start.48 = (bf16[256,2048]{1,0:T(8,128)(2,1)S(1)}, bf16[256,2048]{1,0:T(8,128)(2,1)}, u32[]{:S(2)}, u32[]{:S(2)}) collective-permute-start(bf16[256,2048]{1,0:T(8,128)(2,1)S(1)} %copy-done.20), channel_id=1, source_target_pairs={{0,1},{3,2},{4,5},{7,6},{8,9},{11,10},{12,13},{15,14},{16,17},{19,... | collective-permute-start | bytes 3145736 | tf_op jit(solution)/shard_map/ppermute | solution.py:584
  492.7 8.4 %collective-permute-start.55 = (bf16[256,2048]{1,0:T(8,128)(2,1)S(1)}, bf16[256,2048]{1,0:T(8,128)(2,1)S(1)}, u32[]{:S(2)}, u32[]{:S(2)}) collective-permute-start(bf16[256,2048]{1,0:T(8,128)(2,1)S(1)} %copy-done.21), channel_id=1, source_target_pairs={{0,1},{3,2},{4,5},{7,6},{8,9},{11,10},{12,13},{15,14},{16,17},{19,... | collective-permute-start | bytes 3145736 | tf_op jit(solution)/shard_map/ppermute | solution.py:584
  507.4 8.9 %collective-permute-start.52 = (bf16[256,2048]{1,0:T(8,128)(2,1)}, bf16[256,2048]{1,0:T(8,128)(2,1)}, u32[]{:S(2)}, u32[]{:S(2)}) collective-permute-start(bf16[256,2048]{1,0:T(8,128)(2,1)} %get-tuple-element.694), channel_id=1, source_target_pairs={{0,1},{3,2},{4,5},{7,6},{8,9},{11,10},{12,13},{15,14},{16,17},{19,... | collective-permute-start | bytes 3145736 | tf_op jit(solution)/shard_map/ppermute | solution.py:584
  570.5 11.8 %collective-permute-done.64.r_ref = bf16[256,2048]{1,0:T(8,128)(2,1)S(1)} collective-permute-done((bf16[256,2048]{1,0:T(8,128)(2,1)S(1)}, bf16[256,2048]{1,0:T(8,128)(2,1)S(1)}, u32[]{:S(2)}, u32[]{:S(2)}) %collective-permute-start.64) | collective-permute-done | bytes 1048608 | tf_op jit(solution)/shard_map/ppermute | solution.py:592
  (344 shorter events, 280.1 us)
Async XLA Ops:
  7.2 152.5 %all-gather.3.cloned.1.call-start = ((), (), s32[]{:S(2)}) async-start(), calls=%async_computation.2 | async-start | bytes 21233664 | tf_op jit(solution)/shard_map/all_gather | solution.py:748
  46.5 541.3 %reduce-scatter.2.cloned.1.call-start = ((), (), s32[]{:S(2)}) async-start(), calls=%async_computation.1 | async-start | bytes 28311552 | tf_op jit(solution)/shard_map/reduce_scatter | solution.py:820
  83.7 40.9 %collective-permute-start.17 = (bf16[256,2048]{1,0:T(8,128)(2,1)}, bf16[256,2048]{1,0:T(8,128)(2,1)S(1)}, u32[]{:S(2)}, u32[]{:S(2)}) collective-permute-start(bf16[256,2048]{1,0:T(8,128)(2,1)} %get-tuple-element.395), channel_id=1, source_target_pairs={{0,1},{3,2},{4,5},{7,6},{8,9},{11,10},{12,13},{15,14},{16,17},{19,... | collective-permute-start | bytes 3145736 | tf_op jit(solution)/shard_map/ppermute | solution.py:584
  109.2 37.8 %collective-permute-start.20 = (bf16[256,2048]{1,0:T(8,128)(2,1)S(1)}, bf16[256,2048]{1,0:T(8,128)(2,1)S(1)}, u32[]{:S(2)}, u32[]{:S(2)}) collective-permute-start(bf16[256,2048]{1,0:T(8,128)(2,1)S(1)} %copy-done.40), channel_id=1, source_target_pairs={{0,1},{3,2},{4,5},{7,6},{8,9},{11,10},{12,13},{15,14},{16,17},{19,... | collective-permute-start | bytes 3145736 | tf_op jit(solution)/shard_map/ppermute | solution.py:584
  127.5 55.0 %collective-permute-start.14 = (bf16[256,2048]{1,0:T(8,128)(2,1)S(1)}, bf16[256,2048]{1,0:T(8,128)(2,1)}, u32[]{:S(2)}, u32[]{:S(2)}) collective-permute-start(bf16[256,2048]{1,0:T(8,128)(2,1)S(1)} %copy-done.25), channel_id=1, source_target_pairs={{0,1},{3,2},{4,5},{7,6},{8,9},{11,10},{12,13},{15,14},{16,17},{19,... | collective-permute-start | bytes 3145736 | tf_op jit(solution)/shard_map/ppermute | solution.py:584
  147.4 37.4 %collective-permute-start.24 = (bf16[256,2048]{1,0:T(8,128)(2,1)S(1)}, bf16[256,2048]{1,0:T(8,128)(2,1)}, u32[]{:S(2)}, u32[]{:S(2)}) collective-permute-start(bf16[256,2048]{1,0:T(8,128)(2,1)S(1)} %add.140), channel_id=1, source_target_pairs={{1,2},{2,1},{5,6},{6,5},{9,10},{10,9},{13,14},{14,13},{17,18},{18,... | collective-permute-start | bytes 3145736 | tf_op jit(solution)/shard_map/ppermute | solution.py:587
  149.5 38.7 %collective-permute-start.23 = (bf16[256,2048]{1,0:T(8,128)(2,1)S(1)}, bf16[256,2048]{1,0:T(8,128)(2,1)}, u32[]{:S(2)}, u32[]{:S(2)}) collective-permute-start(bf16[256,2048]{1,0:T(8,128)(2,1)S(1)} %add.141.t_ref), channel_id=1, source_target_pairs={{1,0},{2,3},{5,4},{6,7},{9,8},{10,11},{13,12},{14,15},{17,16},{18,... | collective-permute-start | bytes 3145736 | tf_op jit(solution)/shard_map/ppermute | solution.py:592
  207.0 35.3 %collective-permute-start.28 = (bf16[256,2048]{1,0:T(8,128)(2,1)}, bf16[256,2048]{1,0:T(8,128)(2,1)S(1)}, u32[]{:S(2)}, u32[]{:S(2)}) collective-permute-start(bf16[256,2048]{1,0:T(8,128)(2,1)} %get-tuple-element.457), channel_id=1, source_target_pairs={{0,1},{3,2},{4,5},{7,6},{8,9},{11,10},{12,13},{15,14},{16,17},{19,... | collective-permute-start | bytes 3145736 | tf_op jit(solution)/shard_map/ppermute | solution.py:584
  236.7 36.3 %collective-permute-start.32 = (bf16[256,2048]{1,0:T(8,128)(2,1)}, bf16[256,2048]{1,0:T(8,128)(2,1)}, u32[]{:S(2)}, u32[]{:S(2)}) collective-permute-start(bf16[256,2048]{1,0:T(8,128)(2,1)} %get-tuple-element.482), channel_id=1, source_target_pairs={{0,1},{3,2},{4,5},{7,6},{8,9},{11,10},{12,13},{15,14},{16,17},{19,... | collective-permute-start | bytes 3145736 | tf_op jit(solution)/shard_map/ppermute | solution.py:584
  267.4 42.6 %collective-permute-start.29 = (bf16[256,2048]{1,0:T(8,128)(2,1)}, bf16[256,2048]{1,0:T(8,128)(2,1)}, u32[]{:S(2)}, u32[]{:S(2)}) collective-permute-start(bf16[256,2048]{1,0:T(8,128)(2,1)} %get-tuple-element.504), channel_id=1, source_target_pairs={{0,1},{3,2},{4,5},{7,6},{8,9},{11,10},{12,13},{15,14},{16,17},{19,... | collective-permute-start | bytes 3145736 | tf_op jit(solution)/shard_map/ppermute | solution.py:584
  274.6 37.7 %collective-permute-start.36 = (bf16[256,2048]{1,0:T(8,128)(2,1)S(1)}, bf16[256,2048]{1,0:T(8,128)(2,1)}, u32[]{:S(2)}, u32[]{:S(2)}) collective-permute-start(bf16[256,2048]{1,0:T(8,128)(2,1)S(1)} %add.148), channel_id=1, source_target_pairs={{1,2},{2,1},{5,6},{6,5},{9,10},{10,9},{13,14},{14,13},{17,18},{18,... | collective-permute-start | bytes 3145736 | tf_op jit(solution)/shard_map/ppermute | solution.py:587
  277.9 37.6 %collective-permute-start.35 = (bf16[256,2048]{1,0:T(8,128)(2,1)S(1)}, bf16[256,2048]{1,0:T(8,128)(2,1)S(1)}, u32[]{:S(2)}, u32[]{:S(2)}) collective-permute-start(bf16[256,2048]{1,0:T(8,128)(2,1)S(1)} %add.149.t_ref), channel_id=1, source_target_pairs={{1,0},{2,3},{5,4},{6,7},{9,8},{10,11},{13,12},{14,15},{17,16},{18,... | collective-permute-start | bytes 3145736 | tf_op jit(solution)/shard_map/ppermute | solution.py:592
  292.1 53.9 %collective-permute-start.34 = (bf16[256,2048]{1,0:T(8,128)(2,1)}, bf16[256,2048]{1,0:T(8,128)(2,1)}, u32[]{:S(2)}, u32[]{:S(2)}) collective-permute-start(bf16[256,2048]{1,0:T(8,128)(2,1)} %get-tuple-element.540), channel_id=1, source_target_pairs={{0,1},{3,2},{4,5},{7,6},{8,9},{11,10},{12,13},{15,14},{16,17},{19,... | collective-permute-start | bytes 3145736 | tf_op jit(solution)/shard_map/ppermute | solution.py:584
  311.6 40.9 %collective-permute-start.33 = (bf16[256,2048]{1,0:T(8,128)(2,1)S(1)}, bf16[256,2048]{1,0:T(8,128)(2,1)S(1)}, u32[]{:S(2)}, u32[]{:S(2)}) collective-permute-start(bf16[256,2048]{1,0:T(8,128)(2,1)S(1)} %add.150), channel_id=1, source_target_pairs={{1,2},{2,1},{5,6},{6,5},{9,10},{10,9},{13,14},{14,13},{17,18},{18,... | collective-permute-start | bytes 3145736 | tf_op jit(solution)/shard_map/ppermute | solution.py:587
  314.0 40.5 %collective-permute-start.38 = (bf16[256,2048]{1,0:T(8,128)(2,1)S(1)}, bf16[256,2048]{1,0:T(8,128)(2,1)S(1)}, u32[]{:S(2)}, u32[]{:S(2)}) collective-permute-start(bf16[256,2048]{1,0:T(8,128)(2,1)S(1)} %add.151.t_ref), channel_id=1, source_target_pairs={{1,0},{2,3},{5,4},{6,7},{9,8},{10,11},{13,12},{14,15},{17,16},{18,... | collective-permute-start | bytes 3145736 | tf_op jit(solution)/shard_map/ppermute | solution.py:592
  328.1 51.6 %collective-permute-start.41 = (bf16[256,2048]{1,0:T(8,128)(2,1)}, bf16[256,2048]{1,0:T(8,128)(2,1)}, u32[]{:S(2)}, u32[]{:S(2)}) collective-permute-start(bf16[256,2048]{1,0:T(8,128)(2,1)} %get-tuple-element.583), channel_id=1, source_target_pairs={{0,1},{3,2},{4,5},{7,6},{8,9},{11,10},{12,13},{15,14},{16,17},{19,... | collective-permute-start | bytes 3145736 | tf_op jit(solution)/shard_map/ppermute | solution.py:584
  417.5 59.2 %collective-permute-start.42 = (bf16[256,2048]{1,0:T(8,128)(2,1)}, bf16[256,2048]{1,0:T(8,128)(2,1)}, u32[]{:S(2)}, u32[]{:S(2)}) collective-permute-start(bf16[256,2048]{1,0:T(8,128)(2,1)} %get-tuple-element.636), channel_id=1, source_target_pairs={{0,1},{3,2},{4,5},{7,6},{8,9},{11,10},{12,13},{15,14},{16,17},{19,... | collective-permute-start | bytes 3145736 | tf_op jit(solution)/shard_map/ppermute | solution.py:584
  440.3 39.8 %collective-permute-start.51 = (bf16[256,2048]{1,0:T(8,128)(2,1)S(1)}, bf16[256,2048]{1,0:T(8,128)(2,1)}, u32[]{:S(2)}, u32[]{:S(2)}) collective-permute-start(bf16[256,2048]{1,0:T(8,128)(2,1)S(1)} %add.157), channel_id=1, source_target_pairs={{1,2},{2,1},{5,6},{6,5},{9,10},{10,9},{13,14},{14,13},{17,18},{18,... | collective-permute-start | bytes 3145736 | tf_op jit(solution)/shard_map/ppermute | solution.py:587
  442.3 40.7 %collective-permute-start.50 = (bf16[256,2048]{1,0:T(8,128)(2,1)S(1)}, bf16[256,2048]{1,0:T(8,128)(2,1)}, u32[]{:S(2)}, u32[]{:S(2)}) collective-permute-start(bf16[256,2048]{1,0:T(8,128)(2,1)S(1)} %add.158.t_ref), channel_id=1, source_target_pairs={{1,0},{2,3},{5,4},{6,7},{9,8},{10,11},{13,12},{14,15},{17,16},{18,... | collective-permute-start | bytes 3145736 | tf_op jit(solution)/shard_map/ppermute | solution.py:592
  444.1 44.8 %collective-permute-start.49 = (bf16[256,2048]{1,0:T(8,128)(2,1)S(1)}, bf16[256,2048]{1,0:T(8,128)(2,1)}, u32[]{:S(2)}, u32[]{:S(2)}) collective-permute-start(bf16[256,2048]{1,0:T(8,128)(2,1)S(1)} %add.159.t_ref), channel_id=1, source_target_pairs={{1,0},{2,3},{5,4},{6,7},{9,8},{10,11},{13,12},{14,15},{17,16},{18,... | collective-permute-start | bytes 3145736 | tf_op jit(solution)/shard_map/ppermute | solution.py:592
  451.6 49.6 %collective-permute-start.48 = (bf16[256,2048]{1,0:T(8,128)(2,1)S(1)}, bf16[256,2048]{1,0:T(8,128)(2,1)}, u32[]{:S(2)}, u32[]{:S(2)}) collective-permute-start(bf16[256,2048]{1,0:T(8,128)(2,1)S(1)} %copy-done.20), channel_id=1, source_target_pairs={{0,1},{3,2},{4,5},{7,6},{8,9},{11,10},{12,13},{15,14},{16,17},{19,... | collective-permute-start | bytes 3145736 | tf_op jit(solution)/shard_map/ppermute | solution.py:584
  481.8 34.6 %collective-permute-start.56 = (bf16[256,2048]{1,0:T(8,128)(2,1)S(1)}, bf16[256,2048]{1,0:T(8,128)(2,1)S(1)}, u32[]{:S(2)}, u32[]{:S(2)}) collective-permute-start(bf16[256,2048]{1,0:T(8,128)(2,1)S(1)} %add.161.t_ref), channel_id=1, source_target_pairs={{1,0},{2,3},{5,4},{6,7},{9,8},{10,11},{13,12},{14,15},{17,16},{18,... | collective-permute-start | bytes 3145736 | tf_op jit(solution)/shard_map/ppermute | solution.py:592
  506.1 35.1 %collective-permute-start.58 = (bf16[256,2048]{1,0:T(8,128)(2,1)S(1)}, bf16[256,2048]{1,0:T(8,128)(2,1)}, u32[]{:S(2)}, u32[]{:S(2)}) collective-permute-start(bf16[256,2048]{1,0:T(8,128)(2,1)S(1)} %add.163.t_ref), channel_id=1, source_target_pairs={{1,0},{2,3},{5,4},{6,7},{9,8},{10,11},{13,12},{14,15},{17,16},{18,... | collective-permute-start | bytes 3145736 | tf_op jit(solution)/shard_map/ppermute | solution.py:592
  507.4 40.7 %collective-permute-start.52 = (bf16[256,2048]{1,0:T(8,128)(2,1)}, bf16[256,2048]{1,0:T(8,128)(2,1)}, u32[]{:S(2)}, u32[]{:S(2)}) collective-permute-start(bf16[256,2048]{1,0:T(8,128)(2,1)} %get-tuple-element.694), channel_id=1, source_target_pairs={{0,1},{3,2},{4,5},{7,6},{8,9},{11,10},{12,13},{15,14},{16,17},{19,... | collective-permute-start | bytes 3145736 | tf_op jit(solution)/shard_map/ppermute | solution.py:584
  (104 other events, 1669.8 us)
Sparse Core Ops, SparseCore 0:
  46.6 99.0 all-gather.2
  410.1 156.6 reduce-scatter.1

commit v4 on v3

--- a/solution.py
+++ b/solution.py
@@ -259,28 +259,39 @@
     )(ends, rot, w, *([] if first else [att]))
 
 
-def mlp_kernel(tiles, flag_ref, x_ref, t_ref, r_ref, cot_ref, gain_ref, w_hbm, *rest):
-    mid_ref, n2_ref, prod_ref, gg_ref, gu_ref, down_ref, gnt_ref, acc_d, acc_g, w, sems = rest[-11:]
+def mlp_kernel(c, tiles, flag_ref, x_hbm, t_hbm, r_hbm, cot_hbm, gain_ref, w_hbm, *rest):
+    outs, rest = rest[-22:-15], rest[-15:]
+    x_ref, t_ref, r_ref, cot_ref, mid_ref, n2_ref, prod_ref, gg_ref, gu_ref, down_ref, gnt_ref, acc_d, acc_g, w, sems = rest
+    mid_out, n2_out, prod_out, gg_out, gu_out, down_out, gnt_out = outs
     tile = w.shape[4]
+    rows = pl.ds(c * CHUNK, CHUNK)
+    copy = pltpu.make_async_copy
+    first = [copy(t_hbm, t_ref, sems.at[0]), copy(r_hbm, r_ref, sems.at[1]), copy(x_hbm.at[rows], x_ref, sems.at[2])]
+    cot_copy = [copy(cot_hbm.at[rows], cot_ref, sems.at[3])]
     copies = [
-        [[fetch(w_hbm, w.at[j % 2, i], sems.at[j % 2, i], (i * tiles + j) * tile)] for i in range(3)]
+        [[fetch(w_hbm, w.at[j % 2, i], sems.at[4 + 3 * (j % 2) + i], (i * tiles + j) * tile)] for i in range(3)]
         for j in range(tiles)
     ]
-    for j in range(min(tiles, 2)):
+    saves = [copy(mid_ref, mid_out, sems.at[10]), copy(n2_ref, n2_out.at[rows], sems.at[11])]
+    start(first + copies[0][0] + copies[0][1] + cot_copy + copies[0][2])
+    for j in range(1, min(tiles, 2)):
         for i in range(3):
             start(copies[j][i])
+    wait(first)
     branch = jnp.where(flag_ref[0] == 1, r_ref[...], t_ref[...]).astype(F32)
     mid = x_ref[...].astype(F32) + branch
     mid_ref[...] = mid
-    n2 = (mid * rms_r(mid) * gain_ref[...]).astype(BF)
-    n2_ref[...] = n2
+    n2_ref[...] = (mid * rms_r(mid) * gain_ref[...]).astype(BF)
+    start(saves)
     for j in range(tiles):
         wg, wu, wd = (w.at[j % 2, i] for i in range(3))
-        cols = slice(j * tile, (j + 1) * tile)
+        cols = pl.ds(j * tile, tile)
         wait(copies[j][0])
         g = dot(n2_ref[...], joined(wg))
         wait(copies[j][1])
         u = dot(n2_ref[...], joined(wu))
+        if j == 0:
+            wait(cot_copy)
         wait(copies[j][2])
         gp = dot(cot_ref[...], joined(wd))
         s = 1.0 / (1.0 + jnp.exp(-g))
@@ -288,41 +299,55 @@
         prod = (gs * u).astype(BF)
         gg = (gp * u * s * (1.0 + g * (1.0 - s))).astype(BF)
         gu = (gp * gs).astype(BF)
-        prod_ref[:, cols] = prod
-        gg_ref[:, cols] = gg
-        gu_ref[:, cols] = gu
+        prod_ref[:, j * tile : (j + 1) * tile] = prod
+        gg_ref[:, j * tile : (j + 1) * tile] = gg
+        gu_ref[:, j * tile : (j + 1) * tile] = gu
+        now = [
+            copy(ref.at[:, cols], out.at[rows, cols], sems.at[12 + 3 * j + i])
+            for i, (ref, out) in enumerate(((prod_ref, prod_out), (gg_ref, gg_out), (gu_ref, gu_out)))
+        ]
+        start(now)
+        saves += now
         gnt = dot(gg, joined(wg), NT) + dot(gu, joined(wu), NT)
+        if j:
+            gnt = gnt + acc_g[...]
+        if j < tiles - 1:
+            acc_g[...] = gnt
+        else:
+            gnt_ref[...] = gnt.astype(BF)
+            now = [copy(gnt_ref, gnt_out, sems.at[12 + 3 * tiles])]
+            start(now)
+            saves += now
         down = dot(prod, joined(wd), NT)
         if j:
-            gnt = gnt + acc_g[...]
             down = down + acc_d[...]
         if j < tiles - 1:
-            acc_g[...] = gnt
             acc_d[...] = down
         else:
-            gnt_ref[...] = gnt.astype(BF)
             down_ref[...] = down.astype(BF)
+            now = [copy(down_ref, down_out, sems.at[13 + 3 * tiles])]
+            start(now)
+            saves += now
         if j + 2 < tiles:
             for i in range(3):
                 start(copies[j + 2][i])
+    wait(saves)
+
+
+MLP_TILES = 3
 
 
 def mlp_call(c, flag, x, t, r, cot, gain, w, kept):
     tok, d = x.shape
     n_dp, depth, ff = w.shape[0], w.shape[1], w.shape[2] // 3
-    tiles = 2
-    tile = ff // tiles
+    tiles = MLP_TILES
     first = kept is None
-    blk = chunk_block(c, d)
-    own = pl.BlockSpec((CHUNK, d), lambda j: (0, 0))
-    ffblk = chunk_block(c, ff)
-    full = lambda a: pl.BlockSpec(a.shape, lambda j: (0,) * a.ndim)
     n_alias = 0 if first else 4
+    chunk = lambda n, kind: pltpu.VMEM((CHUNK, n), kind)
     out = pl.pallas_call(
-        functools.partial(mlp_kernel, tiles),
-        grid=(1,),
-        in_specs=[smem(), blk, own, own, blk, full(gain)] + [hbm()] * (1 + n_alias),
-        out_specs=[own, blk, ffblk, ffblk, ffblk, own, own],
+        functools.partial(mlp_kernel, c, tiles),
+        in_specs=[smem(), hbm(), hbm(), hbm(), hbm(), whole(), hbm()] + [hbm()] * n_alias,
+        out_specs=[hbm()] * 7,
         out_shape=[
             jax.ShapeDtypeStruct((CHUNK, d), F32),
             jax.ShapeDtypeStruct((tok, d), BF),
@@ -332,12 +357,12 @@
             jax.ShapeDtypeStruct((CHUNK, d), BF),
             jax.ShapeDtypeStruct((CHUNK, d), BF),
         ],
-        scratch_shapes=[
-            pltpu.VMEM((CHUNK, d), F32),
-            pltpu.VMEM((CHUNK, d), F32),
-            pltpu.VMEM((2, 3, n_dp, depth, tile), BF),
-            pltpu.SemaphoreType.DMA((2, 3)),
-        ],
+        scratch_shapes=[chunk(d, BF)] * 4
+        + [chunk(d, F32), chunk(d, BF)]
+        + [chunk(ff, BF)] * 3
+        + [chunk(d, BF)] * 2
+        + [chunk(d, F32)] * 2
+        + [pltpu.VMEM((2, 3, n_dp, depth, ff // tiles), BF), pltpu.SemaphoreType.DMA((14 + 3 * tiles,))],
         input_output_aliases={} if first else {7: 1, 8: 2, 9: 3, 10: 4},
         compiler_params=params(),
         cost_estimate=cost(19),
@@ -346,16 +371,26 @@
 
 
 def back_kernel(
-    c, nq, nk, first, flag_ref, ends_ref, mid_ref, t_ref, r_ref, cot_ref, gain_ref, rot_ref,
-    lse_ref, lin_ref, cos_ref, sin_ref, gq_ref, gk_ref, w_hbm, *rest,
+    c, nq, nk, first, flag_ref, ends_ref, mid_ref, t_ref, r_ref, cot_ref, gain_ref, rot_hbm,
+    lse_ref, lin_hbm, cos_ref, sin_ref, gq_ref, gk_ref, w_hbm, *rest,
 ):
-    gm_ref, gb_ref, gqkv_ref, part_ref, gain_out, head_out, carry_out, wo, w, sems = rest[-10:]
+    gm_out, gb_out, gqkv_ref, part_ref, gain_out, head_out, carry_out = rest[-16:-9]
+    gm_ref, gb_ref, rot_ref, lin_ref, wo, w, sems, late_sems, save_sems = rest[-9:]
+    lo, width = band(c)
+    rows = pl.ds(c * CHUNK, CHUNK)
+    late = [
+        pltpu.make_async_copy(rot_hbm.at[pl.ds(lo, width)], rot_ref, late_sems.at[0]),
+        pltpu.make_async_copy(lin_hbm.at[rows], lin_ref, late_sems.at[1]),
+    ]
+    saves = [
+        pltpu.make_async_copy(gm_ref, gm_out, save_sems.at[0]),
+        pltpu.make_async_copy(gb_ref, gb_out.at[rows], save_sems.at[1]),
+    ]
     if not first:
         carry_ref, gain_in, head_in = rest[:3]
     out_copies = [fetch(w_hbm, wo, sems.at[0], (nq + 2 * nk) * HD)]
     in_copies = [fetch(w_hbm, w, sems.at[1], 0)]
-    start(out_copies)
-    start(in_copies)
+    start(out_copies + late + in_copies)
     gnt = jnp.where(flag_ref[0] == 1, r_ref[...], t_ref[...]).astype(F32)
     mid = mid_ref[...]
     r2 = rms_r(mid)
@@ -370,9 +405,10 @@
     gm_ref[...] = gm
     gb = gm.astype(BF)
     gb_ref[...] = gb
+    start(saves)
     wait(out_copies)
     ga = dot(gb, joined(wo)).astype(BF)
-    lo, width = band(c)
+    wait(late)
     mask = allowed(c, ends_ref)
     group = nq // nk
     cosine = cos_ref[...]
@@ -389,13 +425,13 @@
     sum_k = jnp.zeros((1, HD), F32) if first else head_in[1:2, :]
     outs = [None] * (nq + 2 * nk)
     for j in range(nk):
-        k = rot_ref[lo : lo + width, (nq + j) * HD : (nq + j + 1) * HD]
-        v = rot_ref[lo : lo + width, (nq + nk + j) * HD : (nq + nk + j + 1) * HD]
+        k = rot_ref[:, (nq + j) * HD : (nq + j + 1) * HD]
+        v = rot_ref[:, (nq + nk + j) * HD : (nq + nk + j + 1) * HD]
         dk = jnp.zeros((width, HD), F32)
         dv = jnp.zeros((width, HD), F32)
         for g in range(group):
             i = j * group + g
-            q = rot_ref[c * CHUNK : (c + 1) * CHUNK, i * HD : (i + 1) * HD]
+            q = rot_ref[width - CHUNK :, i * HD : (i + 1) * HD]
             gah = ga[:, i * HD : (i + 1) * HD]
             s = jnp.where(mask, dot(q, k, NT) * SCALE, -1e30)
             p = jnp.exp(s - lse_ref[:, i : i + 1])
@@ -423,6 +459,7 @@
     head_out[1:2, :] = sum_k
     wait(in_copies)
     part_ref[...] = dot(gqkv, joined(w), NT).astype(BF)
+    wait(saves)
 
 
 def back_call(
@@ -434,7 +471,8 @@
     args = [flag, ends, mid, t, r, cot, gain, rot, lse, lin, cosine, sine, gq, gk]
     specs = [smem(), smem()] + [full(a) for a in args[2:]]
     specs[5] = chunk_block(c, d)
-    specs[9] = chunk_block(c, lin.shape[1])
+    specs[7] = hbm()
+    specs[9] = hbm()
     specs[10] = chunk_block(c, HD)
     specs[11] = chunk_block(c, HD)
     args.append(w)
@@ -451,8 +489,8 @@
         grid=(1,),
         in_specs=specs,
         out_specs=[
-            own(d),
-            chunk_block(c, d),
+            hbm(),
+            hbm(),
             chunk_block(c, cols),
             own(d),
             pl.BlockSpec((1, d), lambda i: (0, 0)),
@@ -469,8 +507,14 @@
             jax.ShapeDtypeStruct((CHUNK, 2 * nk * HD), F32),
         ],
         scratch_shapes=[
+            pltpu.VMEM((CHUNK, d), F32),
+            pltpu.VMEM((CHUNK, d), BF),
+            pltpu.VMEM((band(c)[1], cols), BF),
+            pltpu.VMEM((CHUNK, lin.shape[1]), F32),
             pltpu.VMEM((n_dp, depth, nq * HD), BF),
             pltpu.VMEM((n_dp, depth, cols), BF),
+            pltpu.SemaphoreType.DMA((2,)),
+            pltpu.SemaphoreType.DMA((2,)),
             pltpu.SemaphoreType.DMA((2,)),
         ],
         input_output_aliases={} if first else {18: 1, 19: 2},
@@ -613,6 +657,39 @@
         while self.result is None:
             self.step()
         return self.result
+
+
+class Stream:
+    def __init__(self, line):
+        self.line = line
+        self.four = lax.axis_size("mp") == 4
+        me = lax.axis_index("mp")
+        self.end = (me == 0) | (me == 3)
+        self.parts, self.sent, self.got, self.sums = [], [], [], {}
+
+    def push(self, part=None):
+        i = len(self.parts)
+        self.parts.append(part)
+        if not self.four:
+            if part is not None:
+                self.sums[i] = Sum(self.line, part).total()
+            return i
+        pairs = [(1, 0), (2, 3)] + ([] if part is None else [(0, 1), (3, 2)])
+        if part is None:
+            part = self.line(jnp.add, *self.sums[i - 2])
+        elif i > 1:
+            part = self.line(lambda end, p, a, b: jnp.where(end, p, a + b), self.end, part, *self.sums[i - 2])
+        self.sent.append(part)
+        self.got.append(lax.ppermute(part, "mp", pairs))
+        return i
+
+    def middle(self, i):
+        if self.four:
+            both = self.line(jnp.add, self.parts[i], self.got[i])
+            self.sums[i] = both, lax.ppermute(both, "mp", [(1, 2), (2, 1)])
+
+    def total(self, i):
+        return (self.sent[i + 2], self.got[i + 2]) if self.four else self.sums[i]
 
 
 class Line:
@@ -762,10 +839,6 @@
 
     line = Line()
 
-    def steps(*sums):
-        for s in sums:
-            s.step()
-
     normed, lin, rot, gain_attn, gain_mlp, gain_query, gain_key, w_attn = line(
         functools.partial(qkv_call, nq=nq, nk=nk), flag, hidden_in, cosine, sine, [h.blocks() for h in halves]
     )
@@ -773,9 +846,10 @@
     order = list(reversed(range(tok // CHUNK)))
     att = None
     lse, branch, mid, down, gnt, gn = {}, {}, {}, {}, {}, {}
-    for c in order:
+    stream = Stream(line)
+    for k, c in enumerate(order):
         att, lse[c], part = line(functools.partial(attn_call, c, nq=nq, nk=nk), ends, rot, w_attn, att)
-        branch[c] = Sum(line, part)
+        branch[c] = stream.push(part) if k < 2 else part
 
     c0, c1, c2, c3 = order
     state = {"mlp": None, "back": None, "carry": None, "input": None, "output": None}
@@ -783,35 +857,34 @@
     ff = w_gate.shape[1]
 
     def run_mlp(c):
-        t, r = branch[c].total()
+        t, r = stream.total(branch[c])
         mid[c], state["mlp"], down[c], gnt_part = line(
             functools.partial(mlp_call, c), flag, hidden_in, t, r, cotangent, gain_mlp,
             w_mlp, state["mlp"],
         )
-        gnt[c] = Sum(line, gnt_part)
+        gnt[c] = gnt_part
 
     def run_back(c):
-        t, r = gnt[c].total()
+        t, r = stream.total(gnt[c])
         gm[c], state["back"], part, state["carry"] = line(
             functools.partial(back_call, c, nq=nq, nk=nk), flag, ends, mid[c], t, r, cotangent,
             gain_mlp, rot, lse[c], lin, cosine, sine, gain_query, gain_key, w_attn,
             state["back"], state["carry"],
         )
-        gn[c] = Sum(line, part)
+        gn[c] = part
 
     def run_input(c):
-        t, r = gn[c].total()
+        t, r = stream.total(gn[c])
         state["input"] = line(
             functools.partial(input_call, c), flag, hidden_in, t, r, gm[c], gain_attn, state["input"]
         )
 
     def run_output(c):
-        t, r = down[c].total()
+        t, r = stream.total(down[c])
         state["output"] = line(functools.partial(output_call, c, tok=tok), flag, mid[c], t, r, state["output"])
 
-    def start_down(*cs):
-        for c in cs:
-            down[c] = Sum(line, line.after(down[c])[0])
+    def push(of, c):
+        of[c] = stream.push(line.after(of[c])[0])
 
     def grad(total, at, a, b, kept=None):
         return line(functools.partial(grad_call, n_dp, total, at), a, b, kept)
@@ -827,42 +900,56 @@
         outs[2], outs[6] = outs[2].T, outs[6].T
         return outs
 
-    steps(branch[c0], branch[c1], branch[c0], branch[c2], branch[c1])
+    stream.middle(branch[c0])
+    stream.middle(branch[c1])
+    push(branch, c2)
+    push(branch, c3)
+    stream.middle(branch[c2])
     run_mlp(c0)
-    steps(branch[c3], branch[c2])
+    stream.middle(branch[c3])
+    push(gnt, c0)
     run_mlp(c1)
-    steps(gnt[c0], branch[c3])
+    push(gnt, c1)
+    stream.middle(gnt[c0])
     run_mlp(c2)
-    steps(gnt[c1], gnt[c0])
+    stream.middle(gnt[c1])
+    push(gnt, c2)
     run_mlp(c3)
     n2, prod, gg, gu = state["mlp"]
-    steps(gnt[c2], gnt[c1])
+    push(gnt, c3)
+    stream.middle(gnt[c2])
     run_back(c0)
     g_mlp = grad(3 * ff + wide, 0, n2, gg)
-    steps(gnt[c3], gnt[c2])
+    stream.middle(gnt[c3])
+    push(gn, c0)
     run_back(c1)
-    start_down(c0)
     g_mlp = grad(3 * ff + wide, ff, n2, gu, g_mlp)
-    steps(gn[c0], gnt[c3])
+    push(down, c0)
+    stream.middle(gn[c0])
     run_back(c2)
     g_mlp = grad(3 * ff + wide, 2 * ff, cotangent, prod, g_mlp)
-    steps(gn[c1], gn[c0], down[c0])
+    push(gn, c1)
+    stream.middle(down[c0])
     run_back(c3)
     gb, gqkv = state["back"]
     grads = scatter(line(functools.partial(grad_pair_call, n_dp, 3 * ff), normed, gqkv, gb, att, g_mlp))
-    steps(gn[c2], gn[c1], down[c0])
+    push(gn, c2)
+    stream.middle(gn[c1])
     run_input(c0)
-    start_down(c1)
-    steps(gn[c3], gn[c2])
+    push(gn, c3)
+    stream.middle(gn[c2])
+    run_output(c0)
+    push(down, c1)
+    stream.middle(gn[c3])
     run_input(c1)
-    run_output(c0)
-    start_down(c2)
-    steps(down[c1], gn[c3])
-    start_down(c3)
     _, sum_mlp, sum_head = state["carry"]
     heads = Sum(line, sum_head, "mp", kind=swap_sum)
+    push(down, c2)
+    stream.middle(down[c1])
     run_input(c2)
-    steps(down[c2], down[c1], heads)
+    heads.step()
+    push(down, c3)
+    stream.middle(down[c2])
     run_input(c3)
     grad_input, sum_attn = state["input"]
     heads = heads.total()
@@ -872,9 +959,12 @@
         axis=1,
     )
     sums = Sum(line, sums, dp, kind=own_sum)
-    steps(down[c3], down[c2], sums)
+    stream.push()
+    stream.middle(down[c3])
+    sums.step()
     run_output(c1)
-    steps(down[c3], sums)
+    sums.step()
+    stream.push()
     run_output(c2)
     sums = sums.total()
     outs = line(split, grads)

time: 625 us -> 573 us (0.917)
  starting transfers between devices: 185 us -> 113 us
  waiting for transfers between devices: 89.9 us -> 139 us
  other arithmetic: 57.1 us -> 44.5 us
  local copies, waits for them, and re-layouts: 19.2 us -> 10.5 us
    ppermute x48 -> x34, starting transfers between devices: 166 us -> 96.1 us  [the longest x18 75.3 us: push(): self.got.append(lax.ppermute(part, 'mp', pairs))]
    ppermute x48 -> x34, waiting for transfers between devices: 59 us -> 98.7 us  [the longest x18 98.7 us: push(): self.got.append(lax.ppermute(part, 'mp', pairs))]
    add x37 -> x23, other arithmetic: 42.5 us -> 14 us  [__call__(): out = f(*self.after(*args), **kw)]
    select_n x0 -> x14, other arithmetic: none -> 15.9 us  [push(): jnp.where(end, p, a + b)]
    ppermute x2, waiting for transfers between devices: 6.34 us -> 16.9 us  [swap_sum(): got = lax.ppermute(x, axis, [(i, i ^ step) for i in range(n)])]
    unnamed x120 -> x132, local copies, waits for them, and re-layouts: 12.8 us -> 4.14 us
  transfers between devices with their start and end apart: 69 -> 55, of which waited for: 19 -> 21; matrix products, arithmetic and copies ran while one was open for 10% -> 8% of each run, Pallas kernels for 35% -> 38%
where the time goes in v4:
time: 573 us; the launch traced here: 567 us
  Pallas kernels  245 us (43%)
  waiting for transfers between devices  139 us (24%)
  starting transfers between devices  113 us (20%)
  other arithmetic  44.5 us (8%)
  between operations  15.6 us (3%)
  local copies, waits for them, and re-layouts  10.5 us (2%)
    ppermute x18, waiting for transfers between devices, push(): self.got.append(lax.ppermute(part, 'mp', pairs))  98.7 us
    ppermute x18, starting transfers between devices, push(): self.got.append(lax.ppermute(part, 'mp', pairs))  75.3 us
    pallas_call x4, Pallas kernels, mlp_call(): pl.pallas_call(functools.partial(mlp_kernel, c, tiles), in_specs=[smem(),...  71.3 us
    pallas_call x4, Pallas kernels, back_call(): pl.pallas_call(functools.partial(back_kernel, c, nq, nk, first), grid=(1,...  46 us
    pallas_call x3, Pallas kernels, grad_call(): pl.pallas_call(grad_kernel, grid=(n_dp,), in_specs=[pl.BlockSpec((tok, de...  37 us
    pallas_call x4, Pallas kernels, input_call(): pl.pallas_call(functools.partial(input_kernel, first), grid=(1,), in_spec...  22.2 us
    pallas_call x4, Pallas kernels, attn_call(): pl.pallas_call(functools.partial(attn_kernel, c, nq, nk), grid=(1,), in_s...  21.4 us
    ppermute x16, starting transfers between devices, middle(): self.sums[i] = (both, lax.ppermute(both, 'mp', [(1, 2), (2, 1)]))  20.8 us
  transfers between devices with their start and end apart: 55, of which 21 were waited for; matrix products, arithmetic and copies ran while one was open for 8% of the time, Pallas kernels for 38%

profile of v4, /device:TPU:0, one launch (start us, length us, event | category | flops | bytes accessed | tf_op | source)
XLA Modules:
  0.0 567.1 jit_solution(1844711230118459945)
XLA Ops:
  19.5 8.4 %collective-permute-done.1.rest_2_ = bf16[272,768]{1,0:T(8,128)(2,1)S(1)} collective-permute-done((bf16[272,768]{1,0:T(8,128)(2,1)S(1)}, bf16[272,768]{1,0:T(8,128)(2,1)S(1)}, u32[]{:S(2)}, u32[]{:S(2)}) %collective-permute-start.1) | collective-permute-done | bytes 417824 | tf_op jit(solution)/shard_map/ppermute | solution.py:733
  38.9 7.5 %collective-permute-done.5.rest_6_ = bf16[272,768]{1,0:T(8,128)(2,1)S(1)} collective-permute-done((bf16[272,768]{1,0:T(8,128)(2,1)S(1)}, bf16[272,768]{1,0:T(8,128)(2,1)S(1)}, u32[]{:S(2)}, u32[]{:S(2)}) %collective-permute-start.5) | collective-permute-done | bytes 417824 | tf_op jit(solution)/shard_map/ppermute | solution.py:733
  54.9 14.7 %shard_map.238 = (bf16[1024,2048]{1,0:T(8,128)(2,1)}, f32[1024,768]{1,0:T(8,128)}, bf16[1024,1024]{1,0:T(8,128)(2,1)}, f32[1,2048]{1,0:T(1,128)}, f32[1,2048]{1,...) custom-call(s32[2]{0:T(128)} %pad_add_fusion.flag_ref, bf16[1024,2048]{1,0:T(8,128)(2,1)} %x_ref.5, ...), custom_call_target="tpu_custom_call" | custom-call | bytes 51660000 | tf_op jit(solution)/shard_map/pallas_call | solution.py:159
  93.2 8.0 %collective-permute-done.15 = bf16[256,2048]{1,0:T(8,128)(2,1)S(1)} collective-permute-done((bf16[256,2048]{1,0:T(8,128)(2,1)}, bf16[256,2048]{1,0:T(8,128)(2,1)S(1)}, u32[]{:S(2)}, u32[]{:S(2)}) %collective-permute-start.15) | collective-permute-done | bytes 1048608 | tf_op jit(solution)/shard_map/ppermute | solution.py:683
  102.4 20.6 %collective-permute-done.14 = bf16[256,2048]{1,0:T(8,128)(2,1)S(1)} collective-permute-done((bf16[256,2048]{1,0:T(8,128)(2,1)}, bf16[256,2048]{1,0:T(8,128)(2,1)S(1)}, u32[]{:S(2)}, u32[]{:S(2)}) %collective-permute-start.14) | collective-permute-done | bytes 1048608 | tf_op jit(solution)/shard_map/ppermute | solution.py:683
  129.8 22.2 %collective-permute-start.18 = (bf16[256,2048]{1,0:T(8,128)(2,1)S(1)}, bf16[256,2048]{1,0:T(8,128)(2,1)S(1)}, u32[]{:S(2)}, u32[]{:S(2)}) collective-permute-start(bf16[256,2048]{1,0:T(8,128)(2,1)S(1)} %add_select_fusion.12.t_hbm), channel_id=1, source_target_pairs={{1,0},{2,3},{0,1},{3,2},{5,4},{6,7},{4,5},{7,6},{9,8},{10,11},{8,9... | collective-permute-start | bytes 3145736 | tf_op jit(solution)/shard_map/ppermute | solution.py:683
  155.3 17.7 %shard_map.244 = (f32[256,2048]{1,0:T(8,128)}, bf16[1024,2048]{1,0:T(8,128)(2,1)}, bf16[1024,1536]{1,0:T(8,128)(2,1)}, bf16[1024,1536]{1,0:T(8,128)(2,1)}, bf16[...) custom-call(s32[2]{0:T(128)} %pad_add_fusion.flag_ref, bf16[1024,2048]{1,0:T(8,128)(2,1)} %x_ref.5, ...), custom_call_target="tpu_custom_call" | custom-call | bytes 70110000 | tf_op jit(solution)/shard_map/pallas_call | solution.py:347
  182.3 17.8 %shard_map.245 = (f32[256,2048]{1,0:T(8,128)}, bf16[1024,2048]{1,0:T(8,128)(2,1)}, bf16[1024,1536]{1,0:T(8,128)(2,1)}, bf16[1024,1536]{1,0:T(8,128)(2,1)}, bf16[...) custom-call(s32[2]{0:T(128)} %pad_add_fusion.flag_ref, ...), custom_call_target="tpu_custom_call", output_to_operand_aliasing={{1}: (7, {}), {2}: (8, {}), {3}: (9, {}), {4}: (10, {})} | custom-call | bytes 70110000 | tf_op jit(solution)/shard_map/pallas_call | solution.py:347
  207.0 17.9 %shard_map.246 = (f32[256,2048]{1,0:T(8,128)}, bf16[1024,2048]{1,0:T(8,128)(2,1)}, bf16[1024,1536]{1,0:T(8,128)(2,1)}, bf16[1024,1536]{1,0:T(8,128)(2,1)}, bf16[...) custom-call(s32[2]{0:T(128)} %pad_add_fusion.flag_ref, ...), custom_call_target="tpu_custom_call", output_to_operand_aliasing={{1}: (7, {}), {2}: (8, {}), {3}: (9, {}), {4}: (10, {})} | custom-call | bytes 70110000 | tf_op jit(solution)/shard_map/pallas_call | solution.py:347
  233.7 17.9 %shard_map.247 = (f32[256,2048]{1,0:T(8,128)}, bf16[1024,2048]{1,0:T(8,128)(2,1)}, bf16[1024,1536]{1,0:T(8,128)(2,1)}, bf16[1024,1536]{1,0:T(8,128)(2,1)}, bf16[...) custom-call(s32[2]{0:T(128)} %pad_add_fusion.flag_ref, ...), custom_call_target="tpu_custom_call", output_to_operand_aliasing={{1}: (7, {}), {2}: (8, {}), {3}: (9, {}), {4}: (10, {})} | custom-call | bytes 70110000 | tf_op jit(solution)/shard_map/pallas_call | solution.py:347
  257.2 11.1 %shard_map.248 = (f32[256,2048]{1,0:T(8,128)}, bf16[1024,2048]{1,0:T(8,128)(2,1)}, bf16[1024,1024]{1,0:T(8,128)(2,1)}, bf16[256,2048]{1,0:T(8,128)(2,1)}, f32[1,...) custom-call(s32[2]{0:T(128)} %pad_add_fusion.flag_ref, s32[8]{0:T(128)} %bitcast.31, ...), custom_call_target="tpu_custom_call" | custom-call | bytes 44280000 | tf_op jit(solution)/shard_map/pallas_call | solution.py:487
  268.3 12.3 %shard_map.249.rest_0_ = bf16[2048,6144]{1,0:T(8,128)(2,1)} custom-call(bf16[1024,2048]{1,0:T(8,128)(2,1)} %get-tuple-element.597.a_ref, bf16[1024,1536]{1,0:T(8,128)(2,1)} %get-tuple-element.561.b_ref), custom_call_target="tpu_custom_call" | custom-call | bytes 36900000 | tf_op jit(solution)/shard_map/pallas_call | solution.py:536
  290.0 11.3 %shard_map.250 = (f32[256,2048]{1,0:T(8,128)}, bf16[1024,2048]{1,0:T(8,128)(2,1)}, bf16[1024,1024]{1,0:T(8,128)(2,1)}, bf16[256,2048]{1,0:T(8,128)(2,1)}, f32[1,...) custom-call(s32[2]{0:T(128)} %pad_add_fusion.flag_ref, ...), custom_call_target="tpu_custom_call", output_to_operand_aliasing={{1}: (18, {}), {2}: (19, {})} | custom-call | bytes 44280000 | tf_op jit(solution)/shard_map/pallas_call | solution.py:487
  301.3 12.2 %shard_map.251.rest_0_ = bf16[2048,6144]{1,0:T(8,128)(2,1)} custom-call(bf16[1024,2048]{1,0:T(8,128)(2,1)} %get-tuple-element.597.a_ref, bf16[1024,1536]{1,0:T(8,128)(2,1)} %get-tuple-element.598.b_ref, bf16[2048,6144]{1,0:T(8,128)(2,1)} %shard_map.249.rest_0_), custom_call_target="tpu_custom_call", output_to_operand_aliasing={{}: (2, {})} | custom-call | bytes 36900000 | tf_op jit(solution)/shard_map/pallas_call | solution.py:536
  318.6 11.3 %shard_map.252 = (f32[256,2048]{1,0:T(8,128)}, bf16[1024,2048]{1,0:T(8,128)(2,1)}, bf16[1024,1024]{1,0:T(8,128)(2,1)}, bf16[256,2048]{1,0:T(8,128)(2,1)}, f32[1,...) custom-call(s32[2]{0:T(128)} %pad_add_fusion.flag_ref, ...), custom_call_target="tpu_custom_call", output_to_operand_aliasing={{1}: (18, {}), {2}: (19, {})} | custom-call | bytes 44280000 | tf_op jit(solution)/shard_map/pallas_call | solution.py:487
  329.9 12.5 %shard_map.253.kept_ref = bf16[2048,6144]{1,0:T(8,128)(2,1)} custom-call(bf16[1024,2048]{1,0:T(8,128)(2,1)} %cot_ref.3, bf16[1024,1536]{1,0:T(8,128)(2,1)} %get-tuple-element.642.b_ref, bf16[2048,6144]{1,0:T(8,128)(2,1)} %shard_map.251.rest_0_), custom_call_target="tpu_custom_call", output_to_operand_aliasing={{}: (2, {})} | custom-call | bytes 36900000 | tf_op jit(solution)/shard_map/pallas_call | solution.py:536
  345.5 12.3 %shard_map.254 = (f32[256,2048]{1,0:T(8,128)}, bf16[1024,2048]{1,0:T(8,128)(2,1)}, bf16[1024,1024]{1,0:T(8,128)(2,1)}, bf16[256,2048]{1,0:T(8,128)(2,1)}, f32[1,...) custom-call(s32[2]{0:T(128)} %pad_add_fusion.flag_ref, ...), custom_call_target="tpu_custom_call", output_to_operand_aliasing={{1}: (18, {}), {2}: (19, {})} | custom-call | bytes 44280000 | tf_op jit(solution)/shard_map/pallas_call | solution.py:487
  357.9 13.1 %shard_map.255 = bf16[2048,6144]{1,0:T(8,128)(2,1)} custom-call(bf16[1024,2048]{1,0:T(8,128)(2,1)} %get-tuple-element.678.a_ref, bf16[1024,1024]{1,0:T(8,128)(2,1)} %get-tuple-element.679.b_ref, bf16[1024,2048]{1,0:T(8,128)(2,1)} %get-tuple-element.680.c_ref, bf16[1024,512]{1,0:T(8,128)(2,1)} %get-tuple-element.681.d_ref, ...), custom_call_target="tpu_custom_call", output_to_operand_aliasing={{}: (4, {})} | custom-call | bytes 47970000 | tf_op jit(solution)/shard_map/pallas_call | solution.py:561
  376.3 15.4 %collective-permute-done.36.r_ref = bf16[256,2048]{1,0:T(8,128)(2,1)S(1)} collective-permute-done((bf16[256,2048]{1,0:T(8,128)(2,1)S(1)}, bf16[256,2048]{1,0:T(8,128)(2,1)S(1)}, u32[]{:S(2)}, u32[]{:S(2)}) %collective-permute-start.36) | collective-permute-done | bytes 1048608 | tf_op jit(solution)/shard_map/ppermute | solution.py:683
  404.5 11.3 %collective-permute-done.35.r_ref = bf16[256,2048]{1,0:T(8,128)(2,1)S(1)} collective-permute-done((bf16[256,2048]{1,0:T(8,128)(2,1)S(1)}, bf16[256,2048]{1,0:T(8,128)(2,1)S(1)}, u32[]{:S(2)}, u32[]{:S(2)}) %collective-permute-start.35) | collective-permute-done | bytes 1048608 | tf_op jit(solution)/shard_map/ppermute | solution.py:683
  426.4 12.0 %collective-permute-done.40.r_ref = bf16[256,2048]{1,0:T(8,128)(2,1)S(1)} collective-permute-done((bf16[256,2048]{1,0:T(8,128)(2,1)S(1)}, bf16[256,2048]{1,0:T(8,128)(2,1)S(1)}, u32[]{:S(2)}, u32[]{:S(2)}) %collective-permute-start.40) | collective-permute-done | bytes 1048608 | tf_op jit(solution)/shard_map/ppermute | solution.py:683
  451.6 9.9 %collective-permute-done.39.r_ref = bf16[256,2048]{1,0:T(8,128)(2,1)S(1)} collective-permute-done((bf16[256,2048]{1,0:T(8,128)(2,1)S(1)}, bf16[256,2048]{1,0:T(8,128)(2,1)S(1)}, u32[]{:S(2)}, u32[]{:S(2)}) %collective-permute-start.39) | collective-permute-done | bytes 1048608 | tf_op jit(solution)/shard_map/ppermute | solution.py:683
  473.1 10.6 %collective-permute-done.33 = f32[2,128]{1,0:T(2,128)S(1)} collective-permute-done((f32[2,128]{1,0:T(2,128)S(1)}, f32[2,128]{1,0:T(2,128)S(1)}, u32[]{:S(2)}, u32[]{:S(2)}) %collective-permute-start.33) | collective-permute-done | bytes 1056 | tf_op jit(solution)/shard_map/ppermute | solution.py:764
  540.2 14.8 %collective-permute-done.50.r_ref = bf16[256,2048]{1,0:T(8,128)(2,1)S(1)} collective-permute-done((bf16[256,2048]{1,0:T(8,128)(2,1)}, bf16[256,2048]{1,0:T(8,128)(2,1)S(1)}, u32[]{:S(2)}, u32[]{:S(2)}) %collective-permute-start.50) | collective-permute-done | bytes 1048608 | tf_op jit(solution)/shard_map/ppermute | solution.py:683
  (328 shorter events, 229.0 us)
Async XLA Ops:
  7.2 148.1 %all-gather.3.cloned.1.call-start = ((), (), s32[]{:S(2)}) async-start(), calls=%async_computation.2 | async-start | bytes 21233664 | tf_op jit(solution)/shard_map/all_gather | solution.py:825
  46.5 485.1 %reduce-scatter.2.cloned.1.call-start = ((), (), s32[]{:S(2)}) async-start(), calls=%async_computation.1 | async-start | bytes 28311552 | tf_op jit(solution)/shard_map/reduce_scatter | solution.py:893
  74.9 26.3 %collective-permute-start.15 = (bf16[256,2048]{1,0:T(8,128)(2,1)}, bf16[256,2048]{1,0:T(8,128)(2,1)S(1)}, u32[]{:S(2)}, u32[]{:S(2)}) collective-permute-start(bf16[256,2048]{1,0:T(8,128)(2,1)} %get-tuple-element.431), channel_id=1, source_target_pairs={{1,0},{2,3},{0,1},{3,2},{5,4},{6,7},{4,5},{7,6},{9,8},{10,11},{8,9... | collective-permute-start | bytes 3145736 | tf_op jit(solution)/shard_map/ppermute | solution.py:683
  81.9 41.1 %collective-permute-start.14 = (bf16[256,2048]{1,0:T(8,128)(2,1)}, bf16[256,2048]{1,0:T(8,128)(2,1)S(1)}, u32[]{:S(2)}, u32[]{:S(2)}) collective-permute-start(bf16[256,2048]{1,0:T(8,128)(2,1)} %get-tuple-element.433), channel_id=1, source_target_pairs={{1,0},{2,3},{0,1},{3,2},{5,4},{6,7},{4,5},{7,6},{9,8},{10,11},{8,9... | collective-permute-start | bytes 3145736 | tf_op jit(solution)/shard_map/ppermute | solution.py:683
  101.5 22.6 %collective-permute-start.16 = (bf16[256,2048]{1,0:T(8,128)(2,1)S(1)}, bf16[256,2048]{1,0:T(8,128)(2,1)S(1)}, u32[]{:S(2)}, u32[]{:S(2)}) collective-permute-start(bf16[256,2048]{1,0:T(8,128)(2,1)S(1)} %add.137), channel_id=1, source_target_pairs={{1,2},{2,1},{5,6},{6,5},{9,10},{10,9},{13,14},{14,13},{17,18},{18,... | collective-permute-start | bytes 3145736 | tf_op jit(solution)/shard_map/ppermute | solution.py:689
  124.4 27.6 %collective-permute-start.19 = (bf16[256,2048]{1,0:T(8,128)(2,1)S(1)}, bf16[256,2048]{1,0:T(8,128)(2,1)S(1)}, u32[]{:S(2)}, u32[]{:S(2)}) collective-permute-start(bf16[256,2048]{1,0:T(8,128)(2,1)S(1)} %add_select_fusion.13.t_hbm), channel_id=1, source_target_pairs={{1,0},{2,3},{0,1},{3,2},{5,4},{6,7},{4,5},{7,6},{9,8},{10,11},{8,9... | collective-permute-start | bytes 3145736 | tf_op jit(solution)/shard_map/ppermute | solution.py:683
  129.8 44.3 %collective-permute-start.18 = (bf16[256,2048]{1,0:T(8,128)(2,1)S(1)}, bf16[256,2048]{1,0:T(8,128)(2,1)S(1)}, u32[]{:S(2)}, u32[]{:S(2)}) collective-permute-start(bf16[256,2048]{1,0:T(8,128)(2,1)S(1)} %add_select_fusion.12.t_hbm), channel_id=1, source_target_pairs={{1,0},{2,3},{0,1},{3,2},{5,4},{6,7},{4,5},{7,6},{9,8},{10,11},{8,9... | collective-permute-start | bytes 3145736 | tf_op jit(solution)/shard_map/ppermute | solution.py:683
  153.4 22.3 %collective-permute-start.20 = (bf16[256,2048]{1,0:T(8,128)(2,1)}, bf16[256,2048]{1,0:T(8,128)(2,1)}, u32[]{:S(2)}, u32[]{:S(2)}) collective-permute-start(bf16[256,2048]{1,0:T(8,128)(2,1)} %add.141), channel_id=1, source_target_pairs={{1,2},{2,1},{5,6},{6,5},{9,10},{10,9},{13,14},{14,13},{17,18},{18,... | collective-permute-start | bytes 3145736 | tf_op jit(solution)/shard_map/ppermute | solution.py:689
  174.6 25.6 %collective-permute-start.21 = (bf16[256,2048]{1,0:T(8,128)(2,1)S(1)}, bf16[256,2048]{1,0:T(8,128)(2,1)S(1)}, u32[]{:S(2)}, u32[]{:S(2)}) collective-permute-start(bf16[256,2048]{1,0:T(8,128)(2,1)S(1)} %add.142), channel_id=1, source_target_pairs={{1,2},{2,1},{5,6},{6,5},{9,10},{10,9},{13,14},{14,13},{17,18},{18,... | collective-permute-start | bytes 3145736 | tf_op jit(solution)/shard_map/ppermute | solution.py:689
  177.6 27.2 %collective-permute-start.23 = (bf16[256,2048]{1,0:T(8,128)(2,1)S(1)}, bf16[256,2048]{1,0:T(8,128)(2,1)S(1)}, u32[]{:S(2)}, u32[]{:S(2)}) collective-permute-start(bf16[256,2048]{1,0:T(8,128)(2,1)S(1)} %add_select_fusion.11.t_hbm), channel_id=1, source_target_pairs={{1,0},{2,3},{0,1},{3,2},{5,4},{6,7},{4,5},{7,6},{9,8},{10,11},{8,9... | collective-permute-start | bytes 3145736 | tf_op jit(solution)/shard_map/ppermute | solution.py:683
  201.6 24.1 %collective-permute-start.22 = (bf16[256,2048]{1,0:T(8,128)(2,1)S(1)}, bf16[256,2048]{1,0:T(8,128)(2,1)S(1)}, u32[]{:S(2)}, u32[]{:S(2)}) collective-permute-start(bf16[256,2048]{1,0:T(8,128)(2,1)S(1)} %add_select_fusion.10.t_hbm), channel_id=1, source_target_pairs={{1,0},{2,3},{0,1},{3,2},{5,4},{6,7},{4,5},{7,6},{9,8},{10,11},{8,9... | collective-permute-start | bytes 3145736 | tf_op jit(solution)/shard_map/ppermute | solution.py:683
  205.2 21.8 %collective-permute-start.24 = (bf16[256,2048]{1,0:T(8,128)(2,1)S(1)}, bf16[256,2048]{1,0:T(8,128)(2,1)}, u32[]{:S(2)}, u32[]{:S(2)}) collective-permute-start(bf16[256,2048]{1,0:T(8,128)(2,1)S(1)} %add.145), channel_id=1, source_target_pairs={{1,2},{2,1},{5,6},{6,5},{9,10},{10,9},{13,14},{14,13},{17,18},{18,... | collective-permute-start | bytes 3145736 | tf_op jit(solution)/shard_map/ppermute | solution.py:689
  226.1 25.5 %collective-permute-start.26 = (bf16[256,2048]{1,0:T(8,128)(2,1)S(1)}, bf16[256,2048]{1,0:T(8,128)(2,1)S(1)}, u32[]{:S(2)}, u32[]{:S(2)}) collective-permute-start(bf16[256,2048]{1,0:T(8,128)(2,1)S(1)} %add.146), channel_id=1, source_target_pairs={{1,2},{2,1},{5,6},{6,5},{9,10},{10,9},{13,14},{14,13},{17,18},{18,... | collective-permute-start | bytes 3145736 | tf_op jit(solution)/shard_map/ppermute | solution.py:689
  228.5 26.4 %collective-permute-start.25 = (bf16[256,2048]{1,0:T(8,128)(2,1)S(1)}, bf16[256,2048]{1,0:T(8,128)(2,1)S(1)}, u32[]{:S(2)}, u32[]{:S(2)}) collective-permute-start(bf16[256,2048]{1,0:T(8,128)(2,1)S(1)} %add_select_fusion.9.t_ref), channel_id=1, source_target_pairs={{1,0},{2,3},{0,1},{3,2},{5,4},{6,7},{4,5},{7,6},{9,8},{10,11},{8,9... | collective-permute-start | bytes 3145736 | tf_op jit(solution)/shard_map/ppermute | solution.py:683
  253.0 27.6 %collective-permute-start.27 = (bf16[256,2048]{1,0:T(8,128)(2,1)S(1)}, bf16[256,2048]{1,0:T(8,128)(2,1)S(1)}, u32[]{:S(2)}, u32[]{:S(2)}) collective-permute-start(bf16[256,2048]{1,0:T(8,128)(2,1)S(1)} %add_select_fusion.8.t_ref), channel_id=1, source_target_pairs={{1,0},{2,3},{0,1},{3,2},{5,4},{6,7},{4,5},{7,6},{9,8},{10,11},{8,9... | collective-permute-start | bytes 3145736 | tf_op jit(solution)/shard_map/ppermute | solution.py:683
  255.3 27.0 %collective-permute-start.28 = (bf16[256,2048]{1,0:T(8,128)(2,1)S(1)}, bf16[256,2048]{1,0:T(8,128)(2,1)}, u32[]{:S(2)}, u32[]{:S(2)}) collective-permute-start(bf16[256,2048]{1,0:T(8,128)(2,1)S(1)} %add.149), channel_id=1, source_target_pairs={{1,2},{2,1},{5,6},{6,5},{9,10},{10,9},{13,14},{14,13},{17,18},{18,... | collective-permute-start | bytes 3145736 | tf_op jit(solution)/shard_map/ppermute | solution.py:689
  281.0 32.5 %collective-permute-start.29 = (bf16[256,2048]{1,0:T(8,128)(2,1)S(1)}, bf16[256,2048]{1,0:T(8,128)(2,1)S(1)}, u32[]{:S(2)}, u32[]{:S(2)}) collective-permute-start(bf16[256,2048]{1,0:T(8,128)(2,1)S(1)} %add.150), channel_id=1, source_target_pairs={{1,2},{2,1},{5,6},{6,5},{9,10},{10,9},{13,14},{14,13},{17,18},{18,... | collective-permute-start | bytes 3145736 | tf_op jit(solution)/shard_map/ppermute | solution.py:689
  283.8 29.9 %collective-permute-start.31 = (bf16[256,2048]{1,0:T(8,128)(2,1)S(1)}, bf16[256,2048]{1,0:T(8,128)(2,1)S(1)}, u32[]{:S(2)}, u32[]{:S(2)}) collective-permute-start(bf16[256,2048]{1,0:T(8,128)(2,1)S(1)} %add_select_fusion.7.t_ref), channel_id=1, source_target_pairs={{1,0},{2,3},{0,1},{3,2},{5,4},{6,7},{4,5},{7,6},{9,8},{10,11},{8,9... | collective-permute-start | bytes 3145736 | tf_op jit(solution)/shard_map/ppermute | solution.py:683
  314.1 28.3 %collective-permute-start.32 = (bf16[256,2048]{1,0:T(8,128)(2,1)S(1)}, bf16[256,2048]{1,0:T(8,128)(2,1)}, u32[]{:S(2)}, u32[]{:S(2)}) collective-permute-start(bf16[256,2048]{1,0:T(8,128)(2,1)S(1)} %add.153), channel_id=1, source_target_pairs={{1,2},{2,1},{5,6},{6,5},{9,10},{10,9},{13,14},{14,13},{17,18},{18,... | collective-permute-start | bytes 3145736 | tf_op jit(solution)/shard_map/ppermute | solution.py:689
  316.0 27.9 %collective-permute-start.30 = (bf16[256,2048]{1,0:T(8,128)(2,1)S(1)}, bf16[256,2048]{1,0:T(8,128)(2,1)S(1)}, u32[]{:S(2)}, u32[]{:S(2)}) collective-permute-start(bf16[256,2048]{1,0:T(8,128)(2,1)S(1)} %add_select_fusion.6.t_ref), channel_id=1, source_target_pairs={{1,0},{2,3},{0,1},{3,2},{5,4},{6,7},{4,5},{7,6},{9,8},{10,11},{8,9... | collective-permute-start | bytes 3145736 | tf_op jit(solution)/shard_map/ppermute | solution.py:683
  392.8 23.0 %collective-permute-start.35 = (bf16[256,2048]{1,0:T(8,128)(2,1)S(1)}, bf16[256,2048]{1,0:T(8,128)(2,1)S(1)}, u32[]{:S(2)}, u32[]{:S(2)}) collective-permute-start(bf16[256,2048]{1,0:T(8,128)(2,1)S(1)} %add_select_fusion.4.t_ref), channel_id=1, source_target_pairs={{1,0},{2,3},{0,1},{3,2},{5,4},{6,7},{4,5},{7,6},{9,8},{10,11},{8,9... | collective-permute-start | bytes 3145736 | tf_op jit(solution)/shard_map/ppermute | solution.py:683
  461.9 21.8 %collective-permute-start.42 = (bf16[256,2048]{1,0:T(8,128)(2,1)S(1)}, bf16[256,2048]{1,0:T(8,128)(2,1)}, u32[]{:S(2)}, u32[]{:S(2)}) collective-permute-start(bf16[256,2048]{1,0:T(8,128)(2,1)S(1)} %add.163), channel_id=1, source_target_pairs={{1,2},{2,1},{5,6},{6,5},{9,10},{10,9},{13,14},{14,13},{17,18},{18,... | collective-permute-start | bytes 3145736 | tf_op jit(solution)/shard_map/ppermute | solution.py:689
  488.5 22.8 %collective-permute-start.43 = (bf16[256,2048]{1,0:T(8,128)(2,1)S(1)}, bf16[256,2048]{1,0:T(8,128)(2,1)S(1)}, u32[]{:S(2)}, u32[]{:S(2)}) collective-permute-start(bf16[256,2048]{1,0:T(8,128)(2,1)S(1)} %add_select_fusion.t_ref), channel_id=1, source_target_pairs={{1,0},{2,3},{0,1},{3,2},{5,4},{6,7},{4,5},{7,6},{9,8},{10,11},{8,9... | collective-permute-start | bytes 3145736 | tf_op jit(solution)/shard_map/ppermute | solution.py:683
  524.9 30.1 %collective-permute-start.50 = (bf16[256,2048]{1,0:T(8,128)(2,1)}, bf16[256,2048]{1,0:T(8,128)(2,1)S(1)}, u32[]{:S(2)}, u32[]{:S(2)}) collective-permute-start(bf16[256,2048]{1,0:T(8,128)(2,1)} %add.172.t_ref), channel_id=1, source_target_pairs={{1,0},{2,3},{5,4},{6,7},{9,8},{10,11},{13,12},{14,15},{17,16},{18,... | collective-permute-start | bytes 3145736 | tf_op jit(solution)/shard_map/ppermute | solution.py:683
  (96 other events, 1192.5 us)
Sparse Core Ops, SparseCore 0:
  46.6 99.0 all-gather.2
  371.1 155.7 reduce-scatter.1

commit v5 on v4

--- a/solution.py
+++ b/solution.py
@@ -570,6 +570,32 @@
     )(a, b, c, d, kept)
 
 
+def split_kernel(turned, g_ref, *outs):
+    at = 0
+    for i, out in enumerate(outs):
+        if i in turned:
+            cols = out.shape[0]
+            out[...] = g_ref[:, at : at + cols].astype(F32).T
+        else:
+            cols = out.shape[1]
+            out[...] = g_ref[:, at : at + cols].astype(F32)
+        at += cols
+
+
+def split_call(widths, turned, g):
+    rows = g.shape[0]
+    return pl.pallas_call(
+        functools.partial(split_kernel, turned),
+        in_specs=[whole()],
+        out_specs=[whole()] * len(widths),
+        out_shape=[
+            jax.ShapeDtypeStruct((w, rows) if i in turned else (rows, w), F32) for i, w in enumerate(widths)
+        ],
+        compiler_params=params(),
+        cost_estimate=cost(5),
+    )(g)
+
+
 def input_kernel(first, flag_ref, x_ref, t_ref, r_ref, gm_ref, gain_ref, *rest):
     out_ref, gain_out = rest[-2:]
     gn = jnp.where(flag_ref[0] == 1, r_ref[...], t_ref[...]).astype(F32)
@@ -891,14 +917,6 @@
 
     def scatter(g):
         return lax.psum_scatter(line.after(g)[0], DP, scatter_dimension=0, tiled=True)
-
-    def split(grads):
-        outs, at = [], 0
-        for cols in (ff, ff, ff, nq * HD, nk * HD, nk * HD, nq * HD):
-            outs.append(grads[:, at : at + cols].astype(F32))
-            at += cols
-        outs[2], outs[6] = outs[2].T, outs[6].T
-        return outs
 
     stream.middle(branch[c0])
     stream.middle(branch[c1])
@@ -932,9 +950,10 @@
     stream.middle(down[c0])
     run_back(c3)
     gb, gqkv = state["back"]
-    grads = scatter(line(functools.partial(grad_pair_call, n_dp, 3 * ff), normed, gqkv, gb, att, g_mlp))
+    grads = line(functools.partial(grad_pair_call, n_dp, 3 * ff), normed, gqkv, gb, att, g_mlp)
     push(gn, c2)
     stream.middle(gn[c1])
+    grads = scatter(grads)
     run_input(c0)
     push(gn, c3)
     stream.middle(gn[c2])
@@ -967,7 +986,8 @@
     stream.push()
     run_output(c2)
     sums = sums.total()
-    outs = line(split, grads)
+    widths = (ff, ff, ff, nq * HD, nk * HD, nk * HD, nq * HD)
+    outs = line(functools.partial(split_call, widths, (2, 6)), grads)
     run_output(c3)
 
     return (

time: 573 us -> 558 us (0.974)
  waiting for transfers between devices: 139 us -> 125 us
  Pallas kernels: 245 us -> 251 us
    ppermute x18, waiting for transfers between devices: 98.7 us -> 80.2 us  [push(): self.got.append(lax.ppermute(part, 'mp', pairs))]
    reduce_scatter x1, waiting for transfers between devices: 0.01 us -> 6.22 us  [scatter(): lax.psum_scatter(line.after(g)[0], DP, scatter_dimension=0, tiled=True)]
  transfers between devices with their start and end apart: 55 -> 55, of which waited for: 21 -> 20; matrix products, arithmetic and copies ran while one was open for 8% -> 7% of each run, Pallas kernels for 38% -> 44%
where the time goes in v5:
time: 558 us; the launch traced here: 551 us
  Pallas kernels  251 us (45%)
  waiting for transfers between devices  125 us (22%)
  starting transfers between devices  109 us (20%)
  other arithmetic  40.5 us (7%)
  between operations  15.5 us (3%)
  local copies, waits for them, and re-layouts  10.2 us (2%)
    ppermute x18, waiting for transfers between devices, push(): self.got.append(lax.ppermute(part, 'mp', pairs))  80.2 us
    ppermute x18, starting transfers between devices, push(): self.got.append(lax.ppermute(part, 'mp', pairs))  71.6 us
    pallas_call x4, Pallas kernels, mlp_call(): pl.pallas_call(functools.partial(mlp_kernel, c, tiles), in_specs=[smem(),...  71.3 us
    pallas_call x4, Pallas kernels, back_call(): pl.pallas_call(functools.partial(back_kernel, c, nq, nk, first), grid=(1,...  46 us
    pallas_call x3, Pallas kernels, grad_call(): pl.pallas_call(grad_kernel, grid=(n_dp,), in_specs=[pl.BlockSpec((tok, de...  36.8 us
    ppermute x16, starting transfers between devices, middle(): self.sums[i] = (both, lax.ppermute(both, 'mp', [(1, 2), (2, 1)]))  22.9 us
    pallas_call x4, Pallas kernels, input_call(): pl.pallas_call(functools.partial(input_kernel, first), grid=(1,), in_spec...  22 us
    pallas_call x4, Pallas kernels, attn_call(): pl.pallas_call(functools.partial(attn_kernel, c, nq, nk), grid=(1,), in_s...  21.5 us
  transfers between devices with their start and end apart: 55, of which 20 were waited for; matrix products, arithmetic and copies ran while one was open for 7% of the time, Pallas kernels for 44%

profile of v5, /device:TPU:0, one launch (start us, length us, event | category | flops | bytes accessed | tf_op | source)
XLA Modules:
  0.0 551.3 jit_solution(11909262583519928714)
XLA Ops:
  19.5 8.4 %collective-permute-done.1.rest_2_ = bf16[272,768]{1,0:T(8,128)(2,1)S(1)} collective-permute-done((bf16[272,768]{1,0:T(8,128)(2,1)S(1)}, bf16[272,768]{1,0:T(8,128)(2,1)S(1)}, u32[]{:S(2)}, u32[]{:S(2)}) %collective-permute-start.1) | collective-permute-done | bytes 417824 | tf_op jit(solution)/shard_map/ppermute | solution.py:759
  38.9 7.5 %collective-permute-done.5.rest_6_ = bf16[272,768]{1,0:T(8,128)(2,1)S(1)} collective-permute-done((bf16[272,768]{1,0:T(8,128)(2,1)S(1)}, bf16[272,768]{1,0:T(8,128)(2,1)S(1)}, u32[]{:S(2)}, u32[]{:S(2)}) %collective-permute-start.5) | collective-permute-done | bytes 417824 | tf_op jit(solution)/shard_map/ppermute | solution.py:759
  54.9 14.7 %shard_map.238 = (bf16[1024,2048]{1,0:T(8,128)(2,1)}, f32[1024,768]{1,0:T(8,128)}, bf16[1024,1024]{1,0:T(8,128)(2,1)}, f32[1,2048]{1,0:T(1,128)}, f32[1,2048]{1,...) custom-call(s32[2]{0:T(128)} %pad_add_fusion.flag_ref, bf16[1024,2048]{1,0:T(8,128)(2,1)} %x_ref.5, ...), custom_call_target="tpu_custom_call" | custom-call | bytes 51660000 | tf_op jit(solution)/shard_map/pallas_call | solution.py:159
  93.3 7.9 %collective-permute-done.15 = bf16[256,2048]{1,0:T(8,128)(2,1)S(1)} collective-permute-done((bf16[256,2048]{1,0:T(8,128)(2,1)}, bf16[256,2048]{1,0:T(8,128)(2,1)S(1)}, u32[]{:S(2)}, u32[]{:S(2)}) %collective-permute-start.15) | collective-permute-done | bytes 1048608 | tf_op jit(solution)/shard_map/ppermute | solution.py:709
  102.5 20.6 %collective-permute-done.14 = bf16[256,2048]{1,0:T(8,128)(2,1)S(1)} collective-permute-done((bf16[256,2048]{1,0:T(8,128)(2,1)}, bf16[256,2048]{1,0:T(8,128)(2,1)S(1)}, u32[]{:S(2)}, u32[]{:S(2)}) %collective-permute-start.14) | collective-permute-done | bytes 1048608 | tf_op jit(solution)/shard_map/ppermute | solution.py:709
  129.9 22.2 %collective-permute-start.18 = (bf16[256,2048]{1,0:T(8,128)(2,1)S(1)}, bf16[256,2048]{1,0:T(8,128)(2,1)S(1)}, u32[]{:S(2)}, u32[]{:S(2)}) collective-permute-start(bf16[256,2048]{1,0:T(8,128)(2,1)S(1)} %add_select_fusion.12.t_hbm), channel_id=1, source_target_pairs={{1,0},{2,3},{0,1},{3,2},{5,4},{6,7},{4,5},{7,6},{9,8},{10,11},{8,9... | collective-permute-start | bytes 3145736 | tf_op jit(solution)/shard_map/ppermute | solution.py:709
  155.3 17.7 %shard_map.244 = (f32[256,2048]{1,0:T(8,128)}, bf16[1024,2048]{1,0:T(8,128)(2,1)}, bf16[1024,1536]{1,0:T(8,128)(2,1)}, bf16[1024,1536]{1,0:T(8,128)(2,1)}, bf16[...) custom-call(s32[2]{0:T(128)} %pad_add_fusion.flag_ref, bf16[1024,2048]{1,0:T(8,128)(2,1)} %x_ref.5, ...), custom_call_target="tpu_custom_call" | custom-call | bytes 70110000 | tf_op jit(solution)/shard_map/pallas_call | solution.py:347
  182.4 17.8 %shard_map.245 = (f32[256,2048]{1,0:T(8,128)}, bf16[1024,2048]{1,0:T(8,128)(2,1)}, bf16[1024,1536]{1,0:T(8,128)(2,1)}, bf16[1024,1536]{1,0:T(8,128)(2,1)}, bf16[...) custom-call(s32[2]{0:T(128)} %pad_add_fusion.flag_ref, ...), custom_call_target="tpu_custom_call", output_to_operand_aliasing={{1}: (7, {}), {2}: (8, {}), {3}: (9, {}), {4}: (10, {})} | custom-call | bytes 70110000 | tf_op jit(solution)/shard_map/pallas_call | solution.py:347
  207.1 17.9 %shard_map.246 = (f32[256,2048]{1,0:T(8,128)}, bf16[1024,2048]{1,0:T(8,128)(2,1)}, bf16[1024,1536]{1,0:T(8,128)(2,1)}, bf16[1024,1536]{1,0:T(8,128)(2,1)}, bf16[...) custom-call(s32[2]{0:T(128)} %pad_add_fusion.flag_ref, ...), custom_call_target="tpu_custom_call", output_to_operand_aliasing={{1}: (7, {}), {2}: (8, {}), {3}: (9, {}), {4}: (10, {})} | custom-call | bytes 70110000 | tf_op jit(solution)/shard_map/pallas_call | solution.py:347
  233.8 17.9 %shard_map.247 = (f32[256,2048]{1,0:T(8,128)}, bf16[1024,2048]{1,0:T(8,128)(2,1)}, bf16[1024,1536]{1,0:T(8,128)(2,1)}, bf16[1024,1536]{1,0:T(8,128)(2,1)}, bf16[...) custom-call(s32[2]{0:T(128)} %pad_add_fusion.flag_ref, ...), custom_call_target="tpu_custom_call", output_to_operand_aliasing={{1}: (7, {}), {2}: (8, {}), {3}: (9, {}), {4}: (10, {})} | custom-call | bytes 70110000 | tf_op jit(solution)/shard_map/pallas_call | solution.py:347
  256.3 11.1 %shard_map.248 = (f32[256,2048]{1,0:T(8,128)}, bf16[1024,2048]{1,0:T(8,128)(2,1)}, bf16[1024,1024]{1,0:T(8,128)(2,1)}, bf16[256,2048]{1,0:T(8,128)(2,1)}, f32[1,...) custom-call(s32[2]{0:T(128)} %pad_add_fusion.flag_ref, s32[8]{0:T(128)} %bitcast.27, ...), custom_call_target="tpu_custom_call" | custom-call | bytes 44280000 | tf_op jit(solution)/shard_map/pallas_call | solution.py:487
  267.5 12.2 %shard_map.249.rest_0_ = bf16[2048,6144]{1,0:T(8,128)(2,1)} custom-call(bf16[1024,2048]{1,0:T(8,128)(2,1)} %get-tuple-element.604.a_ref, bf16[1024,1536]{1,0:T(8,128)(2,1)} %get-tuple-element.568.b_ref), custom_call_target="tpu_custom_call" | custom-call | bytes 36900000 | tf_op jit(solution)/shard_map/pallas_call | solution.py:536
  288.7 11.3 %shard_map.250 = (f32[256,2048]{1,0:T(8,128)}, bf16[1024,2048]{1,0:T(8,128)(2,1)}, bf16[1024,1024]{1,0:T(8,128)(2,1)}, bf16[256,2048]{1,0:T(8,128)(2,1)}, f32[1,...) custom-call(s32[2]{0:T(128)} %pad_add_fusion.flag_ref, ...), custom_call_target="tpu_custom_call", output_to_operand_aliasing={{1}: (18, {}), {2}: (19, {})} | custom-call | bytes 44280000 | tf_op jit(solution)/shard_map/pallas_call | solution.py:487
  300.0 12.3 %shard_map.251.rest_0_ = bf16[2048,6144]{1,0:T(8,128)(2,1)} custom-call(bf16[1024,2048]{1,0:T(8,128)(2,1)} %get-tuple-element.604.a_ref, bf16[1024,1536]{1,0:T(8,128)(2,1)} %get-tuple-element.605.b_ref, bf16[2048,6144]{1,0:T(8,128)(2,1)} %shard_map.249.rest_0_), custom_call_target="tpu_custom_call", output_to_operand_aliasing={{}: (2, {})} | custom-call | bytes 36900000 | tf_op jit(solution)/shard_map/pallas_call | solution.py:536
  318.7 11.3 %shard_map.252 = (f32[256,2048]{1,0:T(8,128)}, bf16[1024,2048]{1,0:T(8,128)(2,1)}, bf16[1024,1024]{1,0:T(8,128)(2,1)}, bf16[256,2048]{1,0:T(8,128)(2,1)}, f32[1,...) custom-call(s32[2]{0:T(128)} %pad_add_fusion.flag_ref, ...), custom_call_target="tpu_custom_call", output_to_operand_aliasing={{1}: (18, {}), {2}: (19, {})} | custom-call | bytes 44280000 | tf_op jit(solution)/shard_map/pallas_call | solution.py:487
  330.0 12.2 %shard_map.253.kept_ref = bf16[2048,6144]{1,0:T(8,128)(2,1)} custom-call(bf16[1024,2048]{1,0:T(8,128)(2,1)} %cot_ref.3, bf16[1024,1536]{1,0:T(8,128)(2,1)} %get-tuple-element.649.b_ref, bf16[2048,6144]{1,0:T(8,128)(2,1)} %shard_map.251.rest_0_), custom_call_target="tpu_custom_call", output_to_operand_aliasing={{}: (2, {})} | custom-call | bytes 36900000 | tf_op jit(solution)/shard_map/pallas_call | solution.py:536
  349.0 12.3 %shard_map.254 = (f32[256,2048]{1,0:T(8,128)}, bf16[1024,2048]{1,0:T(8,128)(2,1)}, bf16[1024,1024]{1,0:T(8,128)(2,1)}, bf16[256,2048]{1,0:T(8,128)(2,1)}, f32[1,...) custom-call(s32[2]{0:T(128)} %pad_add_fusion.flag_ref, ...), custom_call_target="tpu_custom_call", output_to_operand_aliasing={{1}: (18, {}), {2}: (19, {})} | custom-call | bytes 44280000 | tf_op jit(solution)/shard_map/pallas_call | solution.py:487
  361.4 13.1 %shard_map.255 = bf16[2048,6144]{1,0:T(8,128)(2,1)} custom-call(bf16[1024,2048]{1,0:T(8,128)(2,1)} %get-tuple-element.685.a_ref, bf16[1024,1024]{1,0:T(8,128)(2,1)} %get-tuple-element.686.b_ref, bf16[1024,2048]{1,0:T(8,128)(2,1)} %get-tuple-element.687.c_ref, bf16[1024,512]{1,0:T(8,128)(2,1)} %get-tuple-element.688.d_ref, ...), custom_call_target="tpu_custom_call", output_to_operand_aliasing={{}: (4, {})} | custom-call | bytes 47970000 | tf_op jit(solution)/shard_map/pallas_call | solution.py:561
  388.1 11.7 %collective-permute-done.35.r_ref = bf16[256,2048]{1,0:T(8,128)(2,1)S(1)} collective-permute-done((bf16[256,2048]{1,0:T(8,128)(2,1)S(1)}, bf16[256,2048]{1,0:T(8,128)(2,1)S(1)}, u32[]{:S(2)}, u32[]{:S(2)}) %collective-permute-start.35) | collective-permute-done | bytes 1048608 | tf_op jit(solution)/shard_map/ppermute | solution.py:709
  412.0 10.5 %collective-permute-done.40.r_ref = bf16[256,2048]{1,0:T(8,128)(2,1)S(1)} collective-permute-done((bf16[256,2048]{1,0:T(8,128)(2,1)S(1)}, bf16[256,2048]{1,0:T(8,128)(2,1)S(1)}, u32[]{:S(2)}, u32[]{:S(2)}) %collective-permute-start.40) | collective-permute-done | bytes 1048608 | tf_op jit(solution)/shard_map/ppermute | solution.py:709
  435.6 10.4 %collective-permute-done.39.r_ref = bf16[256,2048]{1,0:T(8,128)(2,1)S(1)} collective-permute-done((bf16[256,2048]{1,0:T(8,128)(2,1)S(1)}, bf16[256,2048]{1,0:T(8,128)(2,1)S(1)}, u32[]{:S(2)}, u32[]{:S(2)}) %collective-permute-start.39) | collective-permute-done | bytes 1048608 | tf_op jit(solution)/shard_map/ppermute | solution.py:709
  457.7 9.2 %collective-permute-done.33 = f32[2,128]{1,0:T(2,128)S(1)} collective-permute-done((f32[2,128]{1,0:T(2,128)S(1)}, f32[2,128]{1,0:T(2,128)S(1)}, u32[]{:S(2)}, u32[]{:S(2)}) %collective-permute-start.33) | collective-permute-done | bytes 1056 | tf_op jit(solution)/shard_map/ppermute | solution.py:790
  510.1 13.0 %collective-permute-done.51.r_ref = bf16[256,2048]{1,0:T(8,128)(2,1)S(1)} collective-permute-done((bf16[256,2048]{1,0:T(8,128)(2,1)S(1)}, bf16[256,2048]{1,0:T(8,128)(2,1)S(1)}, u32[]{:S(2)}, u32[]{:S(2)}) %collective-permute-start.51) | collective-permute-done | bytes 1048608 | tf_op jit(solution)/shard_map/ppermute | solution.py:709
  528.7 6.2 %reduce-scatter.2.cloned.1.call-done.g_ref = bf16[256,6144]{1,0:T(8,128)(2,1)} async-done(((bf16[2048,6144]{1,0:T(8,128)(2,1)}), bf16[256,6144]{1,0:T(8,128)(2,1)}) %reduce-scatter.2.cloned.1.call-update) | async-done | bytes 3145744 | tf_op jit(solution)/shard_map/reduce_scatter | solution.py:919
  (326 shorter events, 226.3 us)
Async XLA Ops:
  7.2 148.1 %all-gather.3.cloned.1.call-start = ((), (), s32[]{:S(2)}) async-start(), calls=%async_computation.2 | async-start | bytes 21233664 | tf_op jit(solution)/shard_map/all_gather | solution.py:851
  46.5 488.4 %reduce-scatter.2.cloned.1.call-start = ((), (), s32[]{:S(2)}) async-start(), calls=%async_computation.1 | async-start | bytes 28311552 | tf_op jit(solution)/shard_map/reduce_scatter | solution.py:919
  74.9 26.3 %collective-permute-start.15 = (bf16[256,2048]{1,0:T(8,128)(2,1)}, bf16[256,2048]{1,0:T(8,128)(2,1)S(1)}, u32[]{:S(2)}, u32[]{:S(2)}) collective-permute-start(bf16[256,2048]{1,0:T(8,128)(2,1)} %get-tuple-element.438), channel_id=1, source_target_pairs={{1,0},{2,3},{0,1},{3,2},{5,4},{6,7},{4,5},{7,6},{9,8},{10,11},{8,9... | collective-permute-start | bytes 3145736 | tf_op jit(solution)/shard_map/ppermute | solution.py:709
  81.9 41.1 %collective-permute-start.14 = (bf16[256,2048]{1,0:T(8,128)(2,1)}, bf16[256,2048]{1,0:T(8,128)(2,1)S(1)}, u32[]{:S(2)}, u32[]{:S(2)}) collective-permute-start(bf16[256,2048]{1,0:T(8,128)(2,1)} %get-tuple-element.440), channel_id=1, source_target_pairs={{1,0},{2,3},{0,1},{3,2},{5,4},{6,7},{4,5},{7,6},{9,8},{10,11},{8,9... | collective-permute-start | bytes 3145736 | tf_op jit(solution)/shard_map/ppermute | solution.py:709
  101.6 22.6 %collective-permute-start.16 = (bf16[256,2048]{1,0:T(8,128)(2,1)S(1)}, bf16[256,2048]{1,0:T(8,128)(2,1)S(1)}, u32[]{:S(2)}, u32[]{:S(2)}) collective-permute-start(bf16[256,2048]{1,0:T(8,128)(2,1)S(1)} %add.137), channel_id=1, source_target_pairs={{1,2},{2,1},{5,6},{6,5},{9,10},{10,9},{13,14},{14,13},{17,18},{18,... | collective-permute-start | bytes 3145736 | tf_op jit(solution)/shard_map/ppermute | solution.py:715
  124.5 27.6 %collective-permute-start.19 = (bf16[256,2048]{1,0:T(8,128)(2,1)S(1)}, bf16[256,2048]{1,0:T(8,128)(2,1)S(1)}, u32[]{:S(2)}, u32[]{:S(2)}) collective-permute-start(bf16[256,2048]{1,0:T(8,128)(2,1)S(1)} %add_select_fusion.13.t_hbm), channel_id=1, source_target_pairs={{1,0},{2,3},{0,1},{3,2},{5,4},{6,7},{4,5},{7,6},{9,8},{10,11},{8,9... | collective-permute-start | bytes 3145736 | tf_op jit(solution)/shard_map/ppermute | solution.py:709
  129.9 44.3 %collective-permute-start.18 = (bf16[256,2048]{1,0:T(8,128)(2,1)S(1)}, bf16[256,2048]{1,0:T(8,128)(2,1)S(1)}, u32[]{:S(2)}, u32[]{:S(2)}) collective-permute-start(bf16[256,2048]{1,0:T(8,128)(2,1)S(1)} %add_select_fusion.12.t_hbm), channel_id=1, source_target_pairs={{1,0},{2,3},{0,1},{3,2},{5,4},{6,7},{4,5},{7,6},{9,8},{10,11},{8,9... | collective-permute-start | bytes 3145736 | tf_op jit(solution)/shard_map/ppermute | solution.py:709
  153.4 22.3 %collective-permute-start.20 = (bf16[256,2048]{1,0:T(8,128)(2,1)}, bf16[256,2048]{1,0:T(8,128)(2,1)}, u32[]{:S(2)}, u32[]{:S(2)}) collective-permute-start(bf16[256,2048]{1,0:T(8,128)(2,1)} %add.141), channel_id=1, source_target_pairs={{1,2},{2,1},{5,6},{6,5},{9,10},{10,9},{13,14},{14,13},{17,18},{18,... | collective-permute-start | bytes 3145736 | tf_op jit(solution)/shard_map/ppermute | solution.py:715
  174.6 25.6 %collective-permute-start.21 = (bf16[256,2048]{1,0:T(8,128)(2,1)S(1)}, bf16[256,2048]{1,0:T(8,128)(2,1)S(1)}, u32[]{:S(2)}, u32[]{:S(2)}) collective-permute-start(bf16[256,2048]{1,0:T(8,128)(2,1)S(1)} %add.142), channel_id=1, source_target_pairs={{1,2},{2,1},{5,6},{6,5},{9,10},{10,9},{13,14},{14,13},{17,18},{18,... | collective-permute-start | bytes 3145736 | tf_op jit(solution)/shard_map/ppermute | solution.py:715
  177.6 27.2 %collective-permute-start.23 = (bf16[256,2048]{1,0:T(8,128)(2,1)S(1)}, bf16[256,2048]{1,0:T(8,128)(2,1)S(1)}, u32[]{:S(2)}, u32[]{:S(2)}) collective-permute-start(bf16[256,2048]{1,0:T(8,128)(2,1)S(1)} %add_select_fusion.11.t_hbm), channel_id=1, source_target_pairs={{1,0},{2,3},{0,1},{3,2},{5,4},{6,7},{4,5},{7,6},{9,8},{10,11},{8,9... | collective-permute-start | bytes 3145736 | tf_op jit(solution)/shard_map/ppermute | solution.py:709
  201.7 24.1 %collective-permute-start.22 = (bf16[256,2048]{1,0:T(8,128)(2,1)S(1)}, bf16[256,2048]{1,0:T(8,128)(2,1)S(1)}, u32[]{:S(2)}, u32[]{:S(2)}) collective-permute-start(bf16[256,2048]{1,0:T(8,128)(2,1)S(1)} %add_select_fusion.10.t_hbm), channel_id=1, source_target_pairs={{1,0},{2,3},{0,1},{3,2},{5,4},{6,7},{4,5},{7,6},{9,8},{10,11},{8,9... | collective-permute-start | bytes 3145736 | tf_op jit(solution)/shard_map/ppermute | solution.py:709
  205.3 21.9 %collective-permute-start.24 = (bf16[256,2048]{1,0:T(8,128)(2,1)S(1)}, bf16[256,2048]{1,0:T(8,128)(2,1)}, u32[]{:S(2)}, u32[]{:S(2)}) collective-permute-start(bf16[256,2048]{1,0:T(8,128)(2,1)S(1)} %add.145), channel_id=1, source_target_pairs={{1,2},{2,1},{5,6},{6,5},{9,10},{10,9},{13,14},{14,13},{17,18},{18,... | collective-permute-start | bytes 3145736 | tf_op jit(solution)/shard_map/ppermute | solution.py:715
  226.2 25.5 %collective-permute-start.26 = (bf16[256,2048]{1,0:T(8,128)(2,1)S(1)}, bf16[256,2048]{1,0:T(8,128)(2,1)S(1)}, u32[]{:S(2)}, u32[]{:S(2)}) collective-permute-start(bf16[256,2048]{1,0:T(8,128)(2,1)S(1)} %add.146), channel_id=1, source_target_pairs={{1,2},{2,1},{5,6},{6,5},{9,10},{10,9},{13,14},{14,13},{17,18},{18,... | collective-permute-start | bytes 3145736 | tf_op jit(solution)/shard_map/ppermute | solution.py:715
  228.6 26.4 %collective-permute-start.25 = (bf16[256,2048]{1,0:T(8,128)(2,1)S(1)}, bf16[256,2048]{1,0:T(8,128)(2,1)S(1)}, u32[]{:S(2)}, u32[]{:S(2)}) collective-permute-start(bf16[256,2048]{1,0:T(8,128)(2,1)S(1)} %add_select_fusion.9.t_ref), channel_id=1, source_target_pairs={{1,0},{2,3},{0,1},{3,2},{5,4},{6,7},{4,5},{7,6},{9,8},{10,11},{8,9... | collective-permute-start | bytes 3145736 | tf_op jit(solution)/shard_map/ppermute | solution.py:709
  253.1 26.6 %collective-permute-start.27 = (bf16[256,2048]{1,0:T(8,128)(2,1)S(1)}, bf16[256,2048]{1,0:T(8,128)(2,1)S(1)}, u32[]{:S(2)}, u32[]{:S(2)}) collective-permute-start(bf16[256,2048]{1,0:T(8,128)(2,1)S(1)} %add_select_fusion.8.t_ref), channel_id=1, source_target_pairs={{1,0},{2,3},{0,1},{3,2},{5,4},{6,7},{4,5},{7,6},{9,8},{10,11},{8,9... | collective-permute-start | bytes 3145736 | tf_op jit(solution)/shard_map/ppermute | solution.py:709
  255.3 27.0 %collective-permute-start.28 = (bf16[256,2048]{1,0:T(8,128)(2,1)S(1)}, bf16[256,2048]{1,0:T(8,128)(2,1)S(1)}, u32[]{:S(2)}, u32[]{:S(2)}) collective-permute-start(bf16[256,2048]{1,0:T(8,128)(2,1)S(1)} %add.149), channel_id=1, source_target_pairs={{1,2},{2,1},{5,6},{6,5},{9,10},{10,9},{13,14},{14,13},{17,18},{18,... | collective-permute-start | bytes 3145736 | tf_op jit(solution)/shard_map/ppermute | solution.py:715
  280.1 32.2 %collective-permute-start.29 = (bf16[256,2048]{1,0:T(8,128)(2,1)S(1)}, bf16[256,2048]{1,0:T(8,128)(2,1)}, u32[]{:S(2)}, u32[]{:S(2)}) collective-permute-start(bf16[256,2048]{1,0:T(8,128)(2,1)S(1)} %add.150), channel_id=1, source_target_pairs={{1,2},{2,1},{5,6},{6,5},{9,10},{10,9},{13,14},{14,13},{17,18},{18,... | collective-permute-start | bytes 3145736 | tf_op jit(solution)/shard_map/ppermute | solution.py:715
  282.6 31.2 %collective-permute-start.31 = (bf16[256,2048]{1,0:T(8,128)(2,1)S(1)}, bf16[256,2048]{1,0:T(8,128)(2,1)S(1)}, u32[]{:S(2)}, u32[]{:S(2)}) collective-permute-start(bf16[256,2048]{1,0:T(8,128)(2,1)S(1)} %add_select_fusion.7.t_ref), channel_id=1, source_target_pairs={{1,0},{2,3},{0,1},{3,2},{5,4},{6,7},{4,5},{7,6},{9,8},{10,11},{8,9... | collective-permute-start | bytes 3145736 | tf_op jit(solution)/shard_map/ppermute | solution.py:709
  314.2 28.1 %collective-permute-start.32 = (bf16[256,2048]{1,0:T(8,128)(2,1)S(1)}, bf16[256,2048]{1,0:T(8,128)(2,1)}, u32[]{:S(2)}, u32[]{:S(2)}) collective-permute-start(bf16[256,2048]{1,0:T(8,128)(2,1)S(1)} %add.153), channel_id=1, source_target_pairs={{1,2},{2,1},{5,6},{6,5},{9,10},{10,9},{13,14},{14,13},{17,18},{18,... | collective-permute-start | bytes 3145736 | tf_op jit(solution)/shard_map/ppermute | solution.py:715
  316.0 27.8 %collective-permute-start.30 = (bf16[256,2048]{1,0:T(8,128)(2,1)S(1)}, bf16[256,2048]{1,0:T(8,128)(2,1)S(1)}, u32[]{:S(2)}, u32[]{:S(2)}) collective-permute-start(bf16[256,2048]{1,0:T(8,128)(2,1)S(1)} %add_select_fusion.6.t_ref), channel_id=1, source_target_pairs={{1,0},{2,3},{0,1},{3,2},{5,4},{6,7},{4,5},{7,6},{9,8},{10,11},{8,9... | collective-permute-start | bytes 3145736 | tf_op jit(solution)/shard_map/ppermute | solution.py:709
  345.4 29.1 %collective-permute-start.34 = (bf16[256,2048]{1,0:T(8,128)(2,1)}, bf16[256,2048]{1,0:T(8,128)(2,1)}, u32[]{:S(2)}, u32[]{:S(2)}) collective-permute-start(bf16[256,2048]{1,0:T(8,128)(2,1)} %add.155), channel_id=1, source_target_pairs={{1,2},{2,1},{5,6},{6,5},{9,10},{10,9},{13,14},{14,13},{17,18},{18,... | collective-permute-start | bytes 3145736 | tf_op jit(solution)/shard_map/ppermute | solution.py:715
  347.3 30.0 %collective-permute-start.36 = (bf16[256,2048]{1,0:T(8,128)(2,1)S(1)}, bf16[256,2048]{1,0:T(8,128)(2,1)}, u32[]{:S(2)}, u32[]{:S(2)}) collective-permute-start(bf16[256,2048]{1,0:T(8,128)(2,1)S(1)} %add_select_fusion.5.t_ref), channel_id=1, source_target_pairs={{1,0},{2,3},{0,1},{3,2},{5,4},{6,7},{4,5},{7,6},{9,8},{10,11},{8,9... | collective-permute-start | bytes 3145736 | tf_op jit(solution)/shard_map/ppermute | solution.py:709
  495.4 27.8 %collective-permute-start.51 = (bf16[256,2048]{1,0:T(8,128)(2,1)S(1)}, bf16[256,2048]{1,0:T(8,128)(2,1)S(1)}, u32[]{:S(2)}, u32[]{:S(2)}) collective-permute-start(bf16[256,2048]{1,0:T(8,128)(2,1)S(1)} %copy-done.11), channel_id=1, source_target_pairs={{1,0},{2,3},{5,4},{6,7},{9,8},{10,11},{13,12},{14,15},{17,16},{18,... | collective-permute-start | bytes 3145736 | tf_op jit(solution)/shard_map/ppermute | solution.py:709
  508.7 31.1 %collective-permute-start.50 = (bf16[256,2048]{1,0:T(8,128)(2,1)S(1)}, bf16[256,2048]{1,0:T(8,128)(2,1)S(1)}, u32[]{:S(2)}, u32[]{:S(2)}) collective-permute-start(bf16[256,2048]{1,0:T(8,128)(2,1)S(1)} %add.172.t_ref), channel_id=1, source_target_pairs={{1,0},{2,3},{5,4},{6,7},{9,8},{10,11},{13,12},{14,15},{17,16},{18,... | collective-permute-start | bytes 3145736 | tf_op jit(solution)/shard_map/ppermute | solution.py:709
  (97 other events, 1204.1 us)
Sparse Core Ops, SparseCore 0:
  46.6 99.0 all-gather.2
  379.0 155.8 reduce-scatter.1

commit v6 on v5

--- a/solution.py
+++ b/solution.py
@@ -530,12 +530,12 @@
 
 def grad_call(n_dp, total, at, a, b, kept):
     tok, d = a.shape
-    depth = d // n_dp
+    depth = 2 * d // n_dp
     cols = b.shape[1]
     first = kept is None
     return pl.pallas_call(
         grad_kernel,
-        grid=(n_dp,),
+        grid=(n_dp // 2,),
         in_specs=[pl.BlockSpec((tok, depth), lambda i: (0, i)), pl.BlockSpec(b.shape, lambda i: (0, 0))]
         + ([] if first else [hbm()]),
         out_specs=pl.BlockSpec((depth, cols), lambda i: (i, at // cols)),
@@ -554,13 +554,13 @@
 
 def grad_pair_call(n_dp, at, a, b, c, d, kept):
     tok, rows = a.shape
-    depth = rows // n_dp
+    depth = 2 * rows // n_dp
     cols = b.shape[1] + d.shape[1]
     block = pl.BlockSpec((tok, depth), lambda i: (0, i))
     full = lambda x: pl.BlockSpec(x.shape, lambda i: (0, 0))
     return pl.pallas_call(
         grad_pair_kernel,
-        grid=(n_dp,),
+        grid=(n_dp // 2,),
         in_specs=[block, full(b), block, full(d), hbm()],
         out_specs=pl.BlockSpec((depth, cols), lambda i: (i, at // cols)),
         out_shape=jax.ShapeDtypeStruct(kept.shape, BF),

time: 558 us -> 551 us (0.987)
  Pallas kernels: 251 us -> 245 us
    pallas_call x4, Pallas kernels: 49.9 us -> 44.1 us  [the longest x3 32.6 us: grad_call(): pl.pallas_call(grad_kernel, grid=(n_dp // 2,), in_specs=[pl.BlockSpec((to...]
where the time goes in v6:
time: 551 us; the launch traced here: 546 us
  Pallas kernels  245 us (44%)
  waiting for transfers between devices  125 us (23%)
  starting transfers between devices  109 us (20%)
  other arithmetic  40.4 us (7%)
  between operations  15.6 us (3%)
  local copies, waits for them, and re-layouts  10.2 us (2%)
    ppermute x18, waiting for transfers between devices, push(): self.got.append(lax.ppermute(part, 'mp', pairs))  80.9 us
    ppermute x18, starting transfers between devices, push(): self.got.append(lax.ppermute(part, 'mp', pairs))  71.7 us
    pallas_call x4, Pallas kernels, mlp_call(): pl.pallas_call(functools.partial(mlp_kernel, c, tiles), in_specs=[smem(),...  71.3 us
    pallas_call x4, Pallas kernels, back_call(): pl.pallas_call(functools.partial(back_kernel, c, nq, nk, first), grid=(1,...  46 us
    pallas_call x3, Pallas kernels, grad_call(): pl.pallas_call(grad_kernel, grid=(n_dp // 2,), in_specs=[pl.BlockSpec((to...  32.6 us
    ppermute x16, starting transfers between devices, middle(): self.sums[i] = (both, lax.ppermute(both, 'mp', [(1, 2), (2, 1)]))  22.9 us
    pallas_call x4, Pallas kernels, input_call(): pl.pallas_call(functools.partial(input_kernel, first), grid=(1,), in_spec...  22.1 us
    pallas_call x4, Pallas kernels, attn_call(): pl.pallas_call(functools.partial(attn_kernel, c, nq, nk), grid=(1,), in_s...  21.5 us
  transfers between devices with their start and end apart: 55, of which 20 were waited for; matrix products, arithmetic and copies ran while one was open for 7% of the time, Pallas kernels for 44%

profile of v6, /device:TPU:0, one launch (start us, length us, event | category | flops | bytes accessed | tf_op | source)
XLA Modules:
  0.0 545.6 jit_solution(16329477902032138687)
XLA Ops:
  19.5 8.4 %collective-permute-done.1.rest_2_ = bf16[272,768]{1,0:T(8,128)(2,1)S(1)} collective-permute-done((bf16[272,768]{1,0:T(8,128)(2,1)S(1)}, bf16[272,768]{1,0:T(8,128)(2,1)S(1)}, u32[]{:S(2)}, u32[]{:S(2)}) %collective-permute-start.1) | collective-permute-done | bytes 417824 | tf_op jit(solution)/shard_map/ppermute | solution.py:759
  38.9 7.5 %collective-permute-done.5.rest_6_ = bf16[272,768]{1,0:T(8,128)(2,1)S(1)} collective-permute-done((bf16[272,768]{1,0:T(8,128)(2,1)S(1)}, bf16[272,768]{1,0:T(8,128)(2,1)S(1)}, u32[]{:S(2)}, u32[]{:S(2)}) %collective-permute-start.5) | collective-permute-done | bytes 417824 | tf_op jit(solution)/shard_map/ppermute | solution.py:759
  54.9 14.7 %shard_map.238 = (bf16[1024,2048]{1,0:T(8,128)(2,1)}, f32[1024,768]{1,0:T(8,128)}, bf16[1024,1024]{1,0:T(8,128)(2,1)}, f32[1,2048]{1,0:T(1,128)}, f32[1,2048]{1,...) custom-call(s32[2]{0:T(128)} %pad_add_fusion.flag_ref, bf16[1024,2048]{1,0:T(8,128)(2,1)} %x_ref.5, ...), custom_call_target="tpu_custom_call" | custom-call | bytes 51660000 | tf_op jit(solution)/shard_map/pallas_call | solution.py:159
  93.3 7.9 %collective-permute-done.15 = bf16[256,2048]{1,0:T(8,128)(2,1)S(1)} collective-permute-done((bf16[256,2048]{1,0:T(8,128)(2,1)}, bf16[256,2048]{1,0:T(8,128)(2,1)S(1)}, u32[]{:S(2)}, u32[]{:S(2)}) %collective-permute-start.15) | collective-permute-done | bytes 1048608 | tf_op jit(solution)/shard_map/ppermute | solution.py:709
  102.5 20.6 %collective-permute-done.14 = bf16[256,2048]{1,0:T(8,128)(2,1)S(1)} collective-permute-done((bf16[256,2048]{1,0:T(8,128)(2,1)}, bf16[256,2048]{1,0:T(8,128)(2,1)S(1)}, u32[]{:S(2)}, u32[]{:S(2)}) %collective-permute-start.14) | collective-permute-done | bytes 1048608 | tf_op jit(solution)/shard_map/ppermute | solution.py:709
  129.9 22.2 %collective-permute-start.18 = (bf16[256,2048]{1,0:T(8,128)(2,1)S(1)}, bf16[256,2048]{1,0:T(8,128)(2,1)S(1)}, u32[]{:S(2)}, u32[]{:S(2)}) collective-permute-start(bf16[256,2048]{1,0:T(8,128)(2,1)S(1)} %add_select_fusion.12.t_hbm), channel_id=1, source_target_pairs={{1,0},{2,3},{0,1},{3,2},{5,4},{6,7},{4,5},{7,6},{9,8},{10,11},{8,9... | collective-permute-start | bytes 3145736 | tf_op jit(solution)/shard_map/ppermute | solution.py:709
  155.3 17.7 %shard_map.244 = (f32[256,2048]{1,0:T(8,128)}, bf16[1024,2048]{1,0:T(8,128)(2,1)}, bf16[1024,1536]{1,0:T(8,128)(2,1)}, bf16[1024,1536]{1,0:T(8,128)(2,1)}, bf16[...) custom-call(s32[2]{0:T(128)} %pad_add_fusion.flag_ref, bf16[1024,2048]{1,0:T(8,128)(2,1)} %x_ref.5, ...), custom_call_target="tpu_custom_call" | custom-call | bytes 70110000 | tf_op jit(solution)/shard_map/pallas_call | solution.py:347
  182.4 17.8 %shard_map.245 = (f32[256,2048]{1,0:T(8,128)}, bf16[1024,2048]{1,0:T(8,128)(2,1)}, bf16[1024,1536]{1,0:T(8,128)(2,1)}, bf16[1024,1536]{1,0:T(8,128)(2,1)}, bf16[...) custom-call(s32[2]{0:T(128)} %pad_add_fusion.flag_ref, ...), custom_call_target="tpu_custom_call", output_to_operand_aliasing={{1}: (7, {}), {2}: (8, {}), {3}: (9, {}), {4}: (10, {})} | custom-call | bytes 70110000 | tf_op jit(solution)/shard_map/pallas_call | solution.py:347
  207.1 17.9 %shard_map.246 = (f32[256,2048]{1,0:T(8,128)}, bf16[1024,2048]{1,0:T(8,128)(2,1)}, bf16[1024,1536]{1,0:T(8,128)(2,1)}, bf16[1024,1536]{1,0:T(8,128)(2,1)}, bf16[...) custom-call(s32[2]{0:T(128)} %pad_add_fusion.flag_ref, ...), custom_call_target="tpu_custom_call", output_to_operand_aliasing={{1}: (7, {}), {2}: (8, {}), {3}: (9, {}), {4}: (10, {})} | custom-call | bytes 70110000 | tf_op jit(solution)/shard_map/pallas_call | solution.py:347
  233.8 17.9 %shard_map.247 = (f32[256,2048]{1,0:T(8,128)}, bf16[1024,2048]{1,0:T(8,128)(2,1)}, bf16[1024,1536]{1,0:T(8,128)(2,1)}, bf16[1024,1536]{1,0:T(8,128)(2,1)}, bf16[...) custom-call(s32[2]{0:T(128)} %pad_add_fusion.flag_ref, ...), custom_call_target="tpu_custom_call", output_to_operand_aliasing={{1}: (7, {}), {2}: (8, {}), {3}: (9, {}), {4}: (10, {})} | custom-call | bytes 70110000 | tf_op jit(solution)/shard_map/pallas_call | solution.py:347
  256.3 11.1 %shard_map.248 = (f32[256,2048]{1,0:T(8,128)}, bf16[1024,2048]{1,0:T(8,128)(2,1)}, bf16[1024,1024]{1,0:T(8,128)(2,1)}, bf16[256,2048]{1,0:T(8,128)(2,1)}, f32[1,...) custom-call(s32[2]{0:T(128)} %pad_add_fusion.flag_ref, s32[8]{0:T(128)} %bitcast.27, ...), custom_call_target="tpu_custom_call" | custom-call | bytes 44280000 | tf_op jit(solution)/shard_map/pallas_call | solution.py:487
  267.5 10.9 %shard_map.249.rest_0_ = bf16[2048,6144]{1,0:T(8,128)(2,1)} custom-call(bf16[1024,2048]{1,0:T(8,128)(2,1)} %get-tuple-element.604.a_ref, bf16[1024,1536]{1,0:T(8,128)(2,1)} %get-tuple-element.568.b_ref), custom_call_target="tpu_custom_call" | custom-call | bytes 36900000 | tf_op jit(solution)/shard_map/pallas_call | solution.py:536
  287.3 11.3 %shard_map.250 = (f32[256,2048]{1,0:T(8,128)}, bf16[1024,2048]{1,0:T(8,128)(2,1)}, bf16[1024,1024]{1,0:T(8,128)(2,1)}, bf16[256,2048]{1,0:T(8,128)(2,1)}, f32[1,...) custom-call(s32[2]{0:T(128)} %pad_add_fusion.flag_ref, ...), custom_call_target="tpu_custom_call", output_to_operand_aliasing={{1}: (18, {}), {2}: (19, {})} | custom-call | bytes 44280000 | tf_op jit(solution)/shard_map/pallas_call | solution.py:487
  298.6 10.9 %shard_map.251.rest_0_ = bf16[2048,6144]{1,0:T(8,128)(2,1)} custom-call(bf16[1024,2048]{1,0:T(8,128)(2,1)} %get-tuple-element.604.a_ref, bf16[1024,1536]{1,0:T(8,128)(2,1)} %get-tuple-element.605.b_ref, bf16[2048,6144]{1,0:T(8,128)(2,1)} %shard_map.249.rest_0_), custom_call_target="tpu_custom_call", output_to_operand_aliasing={{}: (2, {})} | custom-call | bytes 36900000 | tf_op jit(solution)/shard_map/pallas_call | solution.py:536
  315.9 11.3 %shard_map.252 = (f32[256,2048]{1,0:T(8,128)}, bf16[1024,2048]{1,0:T(8,128)(2,1)}, bf16[1024,1024]{1,0:T(8,128)(2,1)}, bf16[256,2048]{1,0:T(8,128)(2,1)}, f32[1,...) custom-call(s32[2]{0:T(128)} %pad_add_fusion.flag_ref, ...), custom_call_target="tpu_custom_call", output_to_operand_aliasing={{1}: (18, {}), {2}: (19, {})} | custom-call | bytes 44280000 | tf_op jit(solution)/shard_map/pallas_call | solution.py:487
  327.3 10.9 %shard_map.253.kept_ref = bf16[2048,6144]{1,0:T(8,128)(2,1)} custom-call(bf16[1024,2048]{1,0:T(8,128)(2,1)} %cot_ref.3, bf16[1024,1536]{1,0:T(8,128)(2,1)} %get-tuple-element.649.b_ref, bf16[2048,6144]{1,0:T(8,128)(2,1)} %shard_map.251.rest_0_), custom_call_target="tpu_custom_call", output_to_operand_aliasing={{}: (2, {})} | custom-call | bytes 36900000 | tf_op jit(solution)/shard_map/pallas_call | solution.py:536
  344.9 12.3 %shard_map.254 = (f32[256,2048]{1,0:T(8,128)}, bf16[1024,2048]{1,0:T(8,128)(2,1)}, bf16[1024,1024]{1,0:T(8,128)(2,1)}, bf16[256,2048]{1,0:T(8,128)(2,1)}, f32[1,...) custom-call(s32[2]{0:T(128)} %pad_add_fusion.flag_ref, ...), custom_call_target="tpu_custom_call", output_to_operand_aliasing={{1}: (18, {}), {2}: (19, {})} | custom-call | bytes 44280000 | tf_op jit(solution)/shard_map/pallas_call | solution.py:487
  357.2 11.5 %shard_map.255 = bf16[2048,6144]{1,0:T(8,128)(2,1)} custom-call(bf16[1024,2048]{1,0:T(8,128)(2,1)} %get-tuple-element.685.a_ref, bf16[1024,1024]{1,0:T(8,128)(2,1)} %get-tuple-element.686.b_ref, bf16[1024,2048]{1,0:T(8,128)(2,1)} %get-tuple-element.687.c_ref, bf16[1024,512]{1,0:T(8,128)(2,1)} %get-tuple-element.688.d_ref, ...), custom_call_target="tpu_custom_call", output_to_operand_aliasing={{}: (4, {})} | custom-call | bytes 47970000 | tf_op jit(solution)/shard_map/pallas_call | solution.py:561
  376.0 6.2 %shard_map.256 = (f32[1024,2048]{1,0:T(8,128)}, f32[1,2048]{1,0:T(1,128)}) custom-call(s32[2]{0:T(128)} %pad_add_fusion.flag_ref, bf16[1024,2048]{1,0:T(8,128)(2,1)} %x_ref.5, bf16[256,2048]{1,0:T(8,128)(2,1)} %copy-done.13, bf16[256,2048]{1,0:T(8,128)(2,1)} %collective-permute-done.36.r_ref, f32[256,2048]{1,0:T(8,128)} %get-tuple-element.704.gm_ref, ...), custom_call_target="tpu_custom_call" | custom-call | bytes 18450000 | tf_op jit(solution)/shard_map/pallas_call | solution.py:615
  382.3 11.8 %collective-permute-done.35.r_ref = bf16[256,2048]{1,0:T(8,128)(2,1)S(1)} collective-permute-done((bf16[256,2048]{1,0:T(8,128)(2,1)S(1)}, bf16[256,2048]{1,0:T(8,128)(2,1)S(1)}, u32[]{:S(2)}, u32[]{:S(2)}) %collective-permute-start.35) | collective-permute-done | bytes 1048608 | tf_op jit(solution)/shard_map/ppermute | solution.py:709
  406.3 10.4 %collective-permute-done.40.r_ref = bf16[256,2048]{1,0:T(8,128)(2,1)S(1)} collective-permute-done((bf16[256,2048]{1,0:T(8,128)(2,1)S(1)}, bf16[256,2048]{1,0:T(8,128)(2,1)S(1)}, u32[]{:S(2)}, u32[]{:S(2)}) %collective-permute-start.40) | collective-permute-done | bytes 1048608 | tf_op jit(solution)/shard_map/ppermute | solution.py:709
  429.8 10.4 %collective-permute-done.39.r_ref = bf16[256,2048]{1,0:T(8,128)(2,1)S(1)} collective-permute-done((bf16[256,2048]{1,0:T(8,128)(2,1)S(1)}, bf16[256,2048]{1,0:T(8,128)(2,1)S(1)}, u32[]{:S(2)}, u32[]{:S(2)}) %collective-permute-start.39) | collective-permute-done | bytes 1048608 | tf_op jit(solution)/shard_map/ppermute | solution.py:709
  451.9 9.2 %collective-permute-done.33 = f32[2,128]{1,0:T(2,128)S(1)} collective-permute-done((f32[2,128]{1,0:T(2,128)S(1)}, f32[2,128]{1,0:T(2,128)S(1)}, u32[]{:S(2)}, u32[]{:S(2)}) %collective-permute-start.33) | collective-permute-done | bytes 1056 | tf_op jit(solution)/shard_map/ppermute | solution.py:790
  504.0 13.7 %collective-permute-done.51.r_ref = bf16[256,2048]{1,0:T(8,128)(2,1)S(1)} collective-permute-done((bf16[256,2048]{1,0:T(8,128)(2,1)S(1)}, bf16[256,2048]{1,0:T(8,128)(2,1)S(1)}, u32[]{:S(2)}, u32[]{:S(2)}) %collective-permute-start.51) | collective-permute-done | bytes 1048608 | tf_op jit(solution)/shard_map/ppermute | solution.py:709
  (326 shorter events, 225.7 us)
Async XLA Ops:
  7.2 148.1 %all-gather.3.cloned.1.call-start = ((), (), s32[]{:S(2)}) async-start(), calls=%async_computation.2 | async-start | bytes 21233664 | tf_op jit(solution)/shard_map/all_gather | solution.py:851
  46.5 482.7 %reduce-scatter.2.cloned.1.call-start = ((), (), s32[]{:S(2)}) async-start(), calls=%async_computation.1 | async-start | bytes 28311552 | tf_op jit(solution)/shard_map/reduce_scatter | solution.py:919
  74.9 26.3 %collective-permute-start.15 = (bf16[256,2048]{1,0:T(8,128)(2,1)}, bf16[256,2048]{1,0:T(8,128)(2,1)S(1)}, u32[]{:S(2)}, u32[]{:S(2)}) collective-permute-start(bf16[256,2048]{1,0:T(8,128)(2,1)} %get-tuple-element.438), channel_id=1, source_target_pairs={{1,0},{2,3},{0,1},{3,2},{5,4},{6,7},{4,5},{7,6},{9,8},{10,11},{8,9... | collective-permute-start | bytes 3145736 | tf_op jit(solution)/shard_map/ppermute | solution.py:709
  81.9 41.1 %collective-permute-start.14 = (bf16[256,2048]{1,0:T(8,128)(2,1)}, bf16[256,2048]{1,0:T(8,128)(2,1)S(1)}, u32[]{:S(2)}, u32[]{:S(2)}) collective-permute-start(bf16[256,2048]{1,0:T(8,128)(2,1)} %get-tuple-element.440), channel_id=1, source_target_pairs={{1,0},{2,3},{0,1},{3,2},{5,4},{6,7},{4,5},{7,6},{9,8},{10,11},{8,9... | collective-permute-start | bytes 3145736 | tf_op jit(solution)/shard_map/ppermute | solution.py:709
  101.6 22.6 %collective-permute-start.16 = (bf16[256,2048]{1,0:T(8,128)(2,1)S(1)}, bf16[256,2048]{1,0:T(8,128)(2,1)S(1)}, u32[]{:S(2)}, u32[]{:S(2)}) collective-permute-start(bf16[256,2048]{1,0:T(8,128)(2,1)S(1)} %add.137), channel_id=1, source_target_pairs={{1,2},{2,1},{5,6},{6,5},{9,10},{10,9},{13,14},{14,13},{17,18},{18,... | collective-permute-start | bytes 3145736 | tf_op jit(solution)/shard_map/ppermute | solution.py:715
  124.5 27.6 %collective-permute-start.19 = (bf16[256,2048]{1,0:T(8,128)(2,1)S(1)}, bf16[256,2048]{1,0:T(8,128)(2,1)S(1)}, u32[]{:S(2)}, u32[]{:S(2)}) collective-permute-start(bf16[256,2048]{1,0:T(8,128)(2,1)S(1)} %add_select_fusion.13.t_hbm), channel_id=1, source_target_pairs={{1,0},{2,3},{0,1},{3,2},{5,4},{6,7},{4,5},{7,6},{9,8},{10,11},{8,9... | collective-permute-start | bytes 3145736 | tf_op jit(solution)/shard_map/ppermute | solution.py:709
  129.9 44.3 %collective-permute-start.18 = (bf16[256,2048]{1,0:T(8,128)(2,1)S(1)}, bf16[256,2048]{1,0:T(8,128)(2,1)S(1)}, u32[]{:S(2)}, u32[]{:S(2)}) collective-permute-start(bf16[256,2048]{1,0:T(8,128)(2,1)S(1)} %add_select_fusion.12.t_hbm), channel_id=1, source_target_pairs={{1,0},{2,3},{0,1},{3,2},{5,4},{6,7},{4,5},{7,6},{9,8},{10,11},{8,9... | collective-permute-start | bytes 3145736 | tf_op jit(solution)/shard_map/ppermute | solution.py:709
  153.4 22.3 %collective-permute-start.20 = (bf16[256,2048]{1,0:T(8,128)(2,1)}, bf16[256,2048]{1,0:T(8,128)(2,1)}, u32[]{:S(2)}, u32[]{:S(2)}) collective-permute-start(bf16[256,2048]{1,0:T(8,128)(2,1)} %add.141), channel_id=1, source_target_pairs={{1,2},{2,1},{5,6},{6,5},{9,10},{10,9},{13,14},{14,13},{17,18},{18,... | collective-permute-start | bytes 3145736 | tf_op jit(solution)/shard_map/ppermute | solution.py:715
  174.6 25.6 %collective-permute-start.21 = (bf16[256,2048]{1,0:T(8,128)(2,1)S(1)}, bf16[256,2048]{1,0:T(8,128)(2,1)S(1)}, u32[]{:S(2)}, u32[]{:S(2)}) collective-permute-start(bf16[256,2048]{1,0:T(8,128)(2,1)S(1)} %add.142), channel_id=1, source_target_pairs={{1,2},{2,1},{5,6},{6,5},{9,10},{10,9},{13,14},{14,13},{17,18},{18,... | collective-permute-start | bytes 3145736 | tf_op jit(solution)/shard_map/ppermute | solution.py:715
  177.6 27.2 %collective-permute-start.23 = (bf16[256,2048]{1,0:T(8,128)(2,1)S(1)}, bf16[256,2048]{1,0:T(8,128)(2,1)S(1)}, u32[]{:S(2)}, u32[]{:S(2)}) collective-permute-start(bf16[256,2048]{1,0:T(8,128)(2,1)S(1)} %add_select_fusion.11.t_hbm), channel_id=1, source_target_pairs={{1,0},{2,3},{0,1},{3,2},{5,4},{6,7},{4,5},{7,6},{9,8},{10,11},{8,9... | collective-permute-start | bytes 3145736 | tf_op jit(solution)/shard_map/ppermute | solution.py:709
  201.7 24.1 %collective-permute-start.22 = (bf16[256,2048]{1,0:T(8,128)(2,1)S(1)}, bf16[256,2048]{1,0:T(8,128)(2,1)S(1)}, u32[]{:S(2)}, u32[]{:S(2)}) collective-permute-start(bf16[256,2048]{1,0:T(8,128)(2,1)S(1)} %add_select_fusion.10.t_hbm), channel_id=1, source_target_pairs={{1,0},{2,3},{0,1},{3,2},{5,4},{6,7},{4,5},{7,6},{9,8},{10,11},{8,9... | collective-permute-start | bytes 3145736 | tf_op jit(solution)/shard_map/ppermute | solution.py:709
  205.3 21.9 %collective-permute-start.24 = (bf16[256,2048]{1,0:T(8,128)(2,1)S(1)}, bf16[256,2048]{1,0:T(8,128)(2,1)}, u32[]{:S(2)}, u32[]{:S(2)}) collective-permute-start(bf16[256,2048]{1,0:T(8,128)(2,1)S(1)} %add.145), channel_id=1, source_target_pairs={{1,2},{2,1},{5,6},{6,5},{9,10},{10,9},{13,14},{14,13},{17,18},{18,... | collective-permute-start | bytes 3145736 | tf_op jit(solution)/shard_map/ppermute | solution.py:715
  226.2 25.5 %collective-permute-start.26 = (bf16[256,2048]{1,0:T(8,128)(2,1)S(1)}, bf16[256,2048]{1,0:T(8,128)(2,1)S(1)}, u32[]{:S(2)}, u32[]{:S(2)}) collective-permute-start(bf16[256,2048]{1,0:T(8,128)(2,1)S(1)} %add.146), channel_id=1, source_target_pairs={{1,2},{2,1},{5,6},{6,5},{9,10},{10,9},{13,14},{14,13},{17,18},{18,... | collective-permute-start | bytes 3145736 | tf_op jit(solution)/shard_map/ppermute | solution.py:715
  228.6 26.4 %collective-permute-start.25 = (bf16[256,2048]{1,0:T(8,128)(2,1)S(1)}, bf16[256,2048]{1,0:T(8,128)(2,1)S(1)}, u32[]{:S(2)}, u32[]{:S(2)}) collective-permute-start(bf16[256,2048]{1,0:T(8,128)(2,1)S(1)} %add_select_fusion.9.t_ref), channel_id=1, source_target_pairs={{1,0},{2,3},{0,1},{3,2},{5,4},{6,7},{4,5},{7,6},{9,8},{10,11},{8,9... | collective-permute-start | bytes 3145736 | tf_op jit(solution)/shard_map/ppermute | solution.py:709
  253.1 25.2 %collective-permute-start.27 = (bf16[256,2048]{1,0:T(8,128)(2,1)S(1)}, bf16[256,2048]{1,0:T(8,128)(2,1)S(1)}, u32[]{:S(2)}, u32[]{:S(2)}) collective-permute-start(bf16[256,2048]{1,0:T(8,128)(2,1)S(1)} %add_select_fusion.8.t_ref), channel_id=1, source_target_pairs={{1,0},{2,3},{0,1},{3,2},{5,4},{6,7},{4,5},{7,6},{9,8},{10,11},{8,9... | collective-permute-start | bytes 3145736 | tf_op jit(solution)/shard_map/ppermute | solution.py:709
  255.3 25.6 %collective-permute-start.28 = (bf16[256,2048]{1,0:T(8,128)(2,1)S(1)}, bf16[256,2048]{1,0:T(8,128)(2,1)S(1)}, u32[]{:S(2)}, u32[]{:S(2)}) collective-permute-start(bf16[256,2048]{1,0:T(8,128)(2,1)S(1)} %add.149), channel_id=1, source_target_pairs={{1,2},{2,1},{5,6},{6,5},{9,10},{10,9},{13,14},{14,13},{17,18},{18,... | collective-permute-start | bytes 3145736 | tf_op jit(solution)/shard_map/ppermute | solution.py:715
  278.7 30.8 %collective-permute-start.29 = (bf16[256,2048]{1,0:T(8,128)(2,1)S(1)}, bf16[256,2048]{1,0:T(8,128)(2,1)}, u32[]{:S(2)}, u32[]{:S(2)}) collective-permute-start(bf16[256,2048]{1,0:T(8,128)(2,1)S(1)} %add.150), channel_id=1, source_target_pairs={{1,2},{2,1},{5,6},{6,5},{9,10},{10,9},{13,14},{14,13},{17,18},{18,... | collective-permute-start | bytes 3145736 | tf_op jit(solution)/shard_map/ppermute | solution.py:715
  281.2 29.8 %collective-permute-start.31 = (bf16[256,2048]{1,0:T(8,128)(2,1)S(1)}, bf16[256,2048]{1,0:T(8,128)(2,1)S(1)}, u32[]{:S(2)}, u32[]{:S(2)}) collective-permute-start(bf16[256,2048]{1,0:T(8,128)(2,1)S(1)} %add_select_fusion.7.t_ref), channel_id=1, source_target_pairs={{1,0},{2,3},{0,1},{3,2},{5,4},{6,7},{4,5},{7,6},{9,8},{10,11},{8,9... | collective-permute-start | bytes 3145736 | tf_op jit(solution)/shard_map/ppermute | solution.py:709
  311.4 26.7 %collective-permute-start.32 = (bf16[256,2048]{1,0:T(8,128)(2,1)S(1)}, bf16[256,2048]{1,0:T(8,128)(2,1)}, u32[]{:S(2)}, u32[]{:S(2)}) collective-permute-start(bf16[256,2048]{1,0:T(8,128)(2,1)S(1)} %add.153), channel_id=1, source_target_pairs={{1,2},{2,1},{5,6},{6,5},{9,10},{10,9},{13,14},{14,13},{17,18},{18,... | collective-permute-start | bytes 3145736 | tf_op jit(solution)/shard_map/ppermute | solution.py:715
  313.2 26.4 %collective-permute-start.30 = (bf16[256,2048]{1,0:T(8,128)(2,1)S(1)}, bf16[256,2048]{1,0:T(8,128)(2,1)S(1)}, u32[]{:S(2)}, u32[]{:S(2)}) collective-permute-start(bf16[256,2048]{1,0:T(8,128)(2,1)S(1)} %add_select_fusion.6.t_ref), channel_id=1, source_target_pairs={{1,0},{2,3},{0,1},{3,2},{5,4},{6,7},{4,5},{7,6},{9,8},{10,11},{8,9... | collective-permute-start | bytes 3145736 | tf_op jit(solution)/shard_map/ppermute | solution.py:709
  341.2 27.5 %collective-permute-start.34 = (bf16[256,2048]{1,0:T(8,128)(2,1)}, bf16[256,2048]{1,0:T(8,128)(2,1)}, u32[]{:S(2)}, u32[]{:S(2)}) collective-permute-start(bf16[256,2048]{1,0:T(8,128)(2,1)} %add.155), channel_id=1, source_target_pairs={{1,2},{2,1},{5,6},{6,5},{9,10},{10,9},{13,14},{14,13},{17,18},{18,... | collective-permute-start | bytes 3145736 | tf_op jit(solution)/shard_map/ppermute | solution.py:715
  343.1 28.4 %collective-permute-start.36 = (bf16[256,2048]{1,0:T(8,128)(2,1)S(1)}, bf16[256,2048]{1,0:T(8,128)(2,1)}, u32[]{:S(2)}, u32[]{:S(2)}) collective-permute-start(bf16[256,2048]{1,0:T(8,128)(2,1)S(1)} %add_select_fusion.5.t_ref), channel_id=1, source_target_pairs={{1,0},{2,3},{0,1},{3,2},{5,4},{6,7},{4,5},{7,6},{9,8},{10,11},{8,9... | collective-permute-start | bytes 3145736 | tf_op jit(solution)/shard_map/ppermute | solution.py:709
  489.6 28.1 %collective-permute-start.51 = (bf16[256,2048]{1,0:T(8,128)(2,1)S(1)}, bf16[256,2048]{1,0:T(8,128)(2,1)S(1)}, u32[]{:S(2)}, u32[]{:S(2)}) collective-permute-start(bf16[256,2048]{1,0:T(8,128)(2,1)S(1)} %copy-done.11), channel_id=1, source_target_pairs={{1,0},{2,3},{5,4},{6,7},{9,8},{10,11},{13,12},{14,15},{17,16},{18,... | collective-permute-start | bytes 3145736 | tf_op jit(solution)/shard_map/ppermute | solution.py:709
  502.6 31.5 %collective-permute-start.50 = (bf16[256,2048]{1,0:T(8,128)(2,1)S(1)}, bf16[256,2048]{1,0:T(8,128)(2,1)S(1)}, u32[]{:S(2)}, u32[]{:S(2)}) collective-permute-start(bf16[256,2048]{1,0:T(8,128)(2,1)S(1)} %add.172.t_ref), channel_id=1, source_target_pairs={{1,0},{2,3},{5,4},{6,7},{9,8},{10,11},{13,12},{14,15},{17,16},{18,... | collective-permute-start | bytes 3145736 | tf_op jit(solution)/shard_map/ppermute | solution.py:709
  (97 other events, 1198.7 us)
Sparse Core Ops, SparseCore 0:
  46.6 99.0 all-gather.2
  373.3 155.8 reduce-scatter.1
